TPU v7x, 32 devices: a whole 2x2x4 slice. The times are simulated.
32 devices in a mesh: dp: 8 (over z, x), fsdp: 4 (over y, core).
Axes of the slice: x: 2, y: 2, z: 4, core: 2. Of those that a mesh axis runs over, the one named last changes fastest.
Arguments:
- tokens: bfloat16 [64, 320, 1024], P(('dp', 'fsdp')), may hold values from -6 to 6
- condition: float32 [3, 1024], replicated, may hold values from -6 to 6
- clip_frames: int32 [3], replicated, may hold values from 2 to 9, as said below
- ada_weight: bfloat16 [1024, 6144], P('fsdp', 'dp'), may hold values from -0.1875 to 0.1875
- ada_bias: bfloat16 [6144], P('dp'), may hold values from -1.796875 to 1.796875
- qkv_weight: bfloat16 [1024, 3072], P('fsdp', 'dp'), may hold values from -0.1875 to 0.1875
- out_weight: bfloat16 [1024, 1024], P('fsdp', 'dp'), may hold values from -0.75 to 0.75
- up_weight: bfloat16 [1024, 4096], P('fsdp', 'dp'), may hold values from -0.1875 to 0.1875
- down_weight: bfloat16 [4096, 1024], P('fsdp', 'dp'), may hold values from -0.09375 to 0.09375
- rel_table: bfloat16 [16, 2025], P('dp'), may hold values from -3 to 3
- cotangent: bfloat16 [64, 320, 1024], P(('dp', 'fsdp')), may hold values from -6 to 6
Outputs:
- output: bfloat16 [64, 320, 1024], P(('dp', 'fsdp'))
- grad_tokens: float32 [64, 320, 1024], P(('dp', 'fsdp'))
- grad_condition: float32 [3, 1024], replicated
- grad_ada_weight: float32 [1024, 6144], P('fsdp', 'dp')
- grad_ada_bias: float32 [6144], P('dp')
- grad_qkv: float32 [1024, 3072], P('fsdp', 'dp')
- grad_out: float32 [1024, 1024], P('fsdp', 'dp')
- grad_up: float32 [1024, 4096], P('fsdp', 'dp')
- grad_down: float32 [4096, 1024], P('fsdp', 'dp')
- grad_table: float32 [16, 2025], P('dp')
Inputs may be any that keep to these rules, and one draw needn't show every extreme that they name: `clip_frames`: A third of the 3 clips, at places drawn from the seed, have 5 + 1 to 9 frames and span two slabs; the others have 2 to 5 frames. Some clip has 2 frames and some 2*5 - 1.
All inputs are finite; a program needn't handle non-finite values.
Results may differ from a plain program's by a relative error of at most 0.018.
The roundings to bfloat16 on the way count: a program that leaves them out, or rounds other values in their place, can miss the bound.
Values may be sent and summed in bfloat16 or wider, within the bound.
A program may use at most 320 MiB of HBM per device.

v0:
```python
import jax
import jax.numpy as jnp
from jax import lax
from jax.sharding import PartitionSpec as P

D = 1024
H = 16
HD = 64
WT = 5
WSIDE = 8
WIN = 320
SPW = 16
REL = 2025


EPSILON = 1e-06
NEGATIVE = -1000000000.0
HIGHEST = lax.Precision.HIGHEST


def normalize(values):
    center = values - jnp.mean(values, axis=-1, keepdims=True)
    spread = jnp.mean(center * center, axis=-1, keepdims=True)
    return center * lax.rsqrt(spread + EPSILON)


def modulate(values, shift_part, scale_part):
    return normalize(values) * (1.0 + scale_part) + shift_part


def gelu_tanh(values):
    return (
        0.5
        * values
        * (1.0 + jnp.tanh(0.7978845608028654 * (values + 0.044715 * values * values * values)))
    )


def relative_index():
    places = jnp.arange(WIN, dtype=jnp.int32)
    frame_pos = places // (WSIDE * WSIDE)
    row_pos = places // WSIDE % WSIDE
    col_pos = places % WSIDE
    side_span = 2 * WSIDE - 1
    frame_diff = frame_pos[:, None] - frame_pos[None, :] + (WT - 1)
    row_diff = row_pos[:, None] - row_pos[None, :] + (WSIDE - 1)
    col_diff = col_pos[:, None] - col_pos[None, :] + (WSIDE - 1)
    return (frame_diff * side_span + row_diff) * side_span + col_diff


def window_layout(clip_frames, first_window, window_count):
    slab_count = 1 + (clip_frames > WT).astype(jnp.int32)
    starts = jnp.cumsum(slab_count, dtype=jnp.int32) - slab_count
    global_window = first_window + jnp.arange(window_count, dtype=jnp.int32)
    slab_of = global_window // SPW
    owners = jnp.sum((starts[None, :] <= slab_of[:, None]).astype(jnp.int32), axis=1) - 1
    clip_ids = jnp.arange(clip_frames.shape[0], dtype=jnp.int32)
    member = (owners[:, None] == clip_ids[None, :]).astype(jnp.int32)
    clip_start = jnp.sum(member * starts[None, :], axis=1)
    own_frames = jnp.sum(member * clip_frames[None, :], axis=1)
    inner_slab = slab_of - clip_start
    return (jnp.minimum(own_frames - WT * inner_slab, WT), member)


def fold_rows(left, columns):
    return jnp.dot(
        left,
        lax.all_gather(columns, "fsdp", axis=0, tiled=True),
        preferred_element_type=jnp.float32,
    )


def spread_back(gradient, columns):
    return lax.dot_general(
        gradient,
        lax.all_gather(columns, "fsdp", axis=0, tiled=True),
        (((1,), (1,)), ((), ())),
        preferred_element_type=jnp.float32,
    )


def reduce_rows(left, gradient):
    return lax.psum_scatter(
        lax.dot_general(
            left, gradient, (((0,), (0,)), ((), ())), preferred_element_type=jnp.float32
        ).astype(jnp.bfloat16),
        "fsdp",
        scatter_dimension=0,
        tiled=True,
    ).astype(jnp.float32)


def weight_gradient(left, gradient):
    return reduce_rows(left, gradient)


def score_block(query, keys, key_live, rel_bias):
    scores = (
        jnp.einsum("wqhe,wkhe->whqk", query, keys, preferred_element_type=jnp.float32)
        * HD ** (-0.5)
        + rel_bias[None]
    )
    return jnp.where(key_live[:, None, None, :], scores, NEGATIVE)


def per_device(
    tokens,
    condition,
    clip_frames,
    ada_weight,
    ada_bias,
    qkv_weight,
    out_weight,
    up_weight,
    down_weight,
    rel_table,
    cotangent,
):
    window_count = tokens.shape[0]
    clip_count = condition.shape[0]
    rows_ada = ada_weight.shape[0]
    cols_ada = ada_weight.shape[1]
    row_block = lax.axis_index("fsdp")
    col_block = lax.axis_index("dp")
    first_window = lax.axis_index(("dp", "fsdp")) * window_count
    live_frames, member_int = window_layout(clip_frames, first_window, window_count)
    frame_pos = jnp.arange(WIN, dtype=jnp.int32) // (WSIDE * WSIDE)
    live_mask = frame_pos[None, :] < live_frames[:, None]
    member = member_int.astype(jnp.float32)
    activity = jax.nn.silu(condition)
    activity_low = activity.astype(jnp.bfloat16)
    act_rows = lax.dynamic_slice_in_dim(activity_low, row_block * rows_ada, rows_ada, 1)
    qkv_cols, out_cols, up_cols, down_cols, ada_cols, bias_cols, table_all = (
        lax.all_gather(qkv_weight, "dp", axis=1, tiled=True),
        lax.all_gather(out_weight, "dp", axis=1, tiled=True),
        lax.all_gather(up_weight, "dp", axis=1, tiled=True),
        lax.all_gather(down_weight, "dp", axis=1, tiled=True),
        lax.all_gather(ada_weight, "dp", axis=1, tiled=True),
        lax.all_gather(ada_bias, "dp", axis=0, tiled=True),
        lax.all_gather(rel_table, "dp", axis=0, tiled=True),
    )
    window_act = jnp.dot(
        member, activity, precision=HIGHEST, preferred_element_type=jnp.float32
    ).astype(jnp.bfloat16)
    window_mod = (
        jnp.dot(
            window_act,
            lax.all_gather(ada_cols, "fsdp", axis=0, tiled=True),
            preferred_element_type=jnp.float32,
        )
        + bias_cols.astype(jnp.float32)[None, :]
    )
    shift_one, scale_one, gate_one, shift_two, scale_two, gate_two = jnp.split(
        window_mod[:, None, :], 6, axis=-1
    )
    inputs = tokens.astype(jnp.float32)
    token_rows = window_count * WIN
    block_count = window_count // 2
    index_table = relative_index()
    rel_bias = table_all.astype(jnp.float32)[:, index_table]

    def forward_block(pieces):
        block_qkv, block_live = pieces
        scores = score_block(block_qkv[:, :, 0], block_qkv[:, :, 1], block_live, rel_bias)
        peak = jnp.max(scores, axis=-1, keepdims=True)
        shifted = jnp.exp(scores - peak)
        totals = jnp.sum(shifted, axis=-1, keepdims=True)
        weights_low = (shifted / totals).astype(jnp.bfloat16)
        mixed_part = jnp.einsum(
            "whqk,wkhe->wqhe", weights_low, block_qkv[:, :, 2], preferred_element_type=jnp.float32
        )
        return (mixed_part.astype(jnp.bfloat16), (peak + jnp.log(totals))[..., 0])

    def backward_block(carry, pieces):
        block_qkv, block_live, block_lse, block_grad = pieces
        query = block_qkv[:, :, 0]
        keys = block_qkv[:, :, 1]
        scores = score_block(query, keys, block_live, rel_bias)
        probs_full = jnp.exp(scores - block_lse[..., None])
        weights_low = probs_full.astype(jnp.bfloat16)
        grad_values = jnp.einsum(
            "whqk,wqhe->wkhe", weights_low, block_grad, preferred_element_type=jnp.float32
        )
        grad_probs = jnp.einsum(
            "wqhe,wkhe->whqk", block_grad, block_qkv[:, :, 2], preferred_element_type=jnp.float32
        )
        grad_scores = (
            probs_full * (grad_probs - jnp.sum(probs_full * grad_probs, axis=-1, keepdims=True))
        ).astype(jnp.bfloat16)
        grad_query = jnp.einsum(
            "whqk,wkhe->wqhe", grad_scores, keys, preferred_element_type=jnp.float32
        ) * HD ** (-0.5)
        grad_keys = jnp.einsum(
            "whqk,wqhe->wkhe", grad_scores, query, preferred_element_type=jnp.float32
        ) * HD ** (-0.5)
        packed_grad = jnp.stack([grad_query, grad_keys, grad_values], axis=2).astype(jnp.bfloat16)
        return (carry + jnp.sum(grad_scores.astype(jnp.float32), axis=0), packed_grad)

    normed_full, back_one = jax.vjp(modulate, inputs, shift_one, scale_one)
    normed_one = normed_full.astype(jnp.bfloat16).reshape(token_rows, D)
    packed = fold_rows(normed_one, qkv_cols).astype(jnp.bfloat16)
    packed_blocks = packed.reshape(block_count, 2, WIN, 3, H, HD)
    live_blocks = live_mask.reshape(block_count, 2, WIN)
    mixed_blocks, lse_blocks = lax.map(forward_block, (packed_blocks, live_blocks))
    mixed_heads = mixed_blocks.reshape(token_rows, D)
    attended = fold_rows(mixed_heads, out_cols).reshape(window_count, WIN, D)
    middle = inputs + gate_one * attended
    normed_full_two, back_two = jax.vjp(modulate, middle, shift_two, scale_two)
    normed_two = normed_full_two.astype(jnp.bfloat16).reshape(token_rows, D)
    hidden = fold_rows(normed_two, up_cols)
    activated_full, gelu_back = jax.vjp(gelu_tanh, hidden)
    activated = activated_full.astype(jnp.bfloat16)
    mlp_out = fold_rows(activated, down_cols).reshape(window_count, WIN, D)
    result = middle + gate_two * mlp_out
    output = jnp.where(live_mask[:, :, None], result, 0.0).astype(jnp.bfloat16)
    grad_result = jnp.where(live_mask[:, :, None], cotangent.astype(jnp.float32), 0.0)
    grad_mlp = (gate_two * grad_result).astype(jnp.bfloat16).reshape(token_rows, D)
    grad_gate_two = jnp.sum(grad_result * mlp_out, axis=1, keepdims=True)
    grad_activated = spread_back(grad_mlp, down_cols)
    grad_hidden = gelu_back(grad_activated)[0].astype(jnp.bfloat16)
    grad_down_part = weight_gradient(activated, grad_mlp)
    grad_normed_two = spread_back(grad_hidden, up_cols).reshape(window_count, WIN, D)
    grad_up_part = weight_gradient(normed_two, grad_hidden)
    grad_middle_norm, grad_shift_two, grad_scale_two = back_two(grad_normed_two)
    grad_middle = grad_result + grad_middle_norm
    grad_attended = (gate_one * grad_middle).astype(jnp.bfloat16).reshape(token_rows, D)
    grad_gate_one = jnp.sum(grad_middle * attended, axis=1, keepdims=True)
    grad_mixed = spread_back(grad_attended, out_cols).astype(jnp.bfloat16)
    grad_out_part = weight_gradient(mixed_heads, grad_attended)
    bias_grad, packed_grads = lax.scan(
        backward_block,
        jnp.zeros((H, WIN, WIN), jnp.float32),
        (packed_blocks, live_blocks, lse_blocks, grad_mixed.reshape(block_count, 2, WIN, H, HD)),
    )
    grad_packed = packed_grads.reshape(token_rows, 3 * D)
    grad_normed_one = spread_back(grad_packed, qkv_cols).reshape(window_count, WIN, D)
    grad_qkv_part = weight_gradient(normed_one, grad_packed)
    grad_inputs_norm, grad_shift_one, grad_scale_one = back_one(grad_normed_one)
    grad_tokens = grad_middle + grad_inputs_norm
    grad_window_mod = jnp.concatenate(
        [
            grad_shift_one,
            grad_scale_one,
            grad_gate_one,
            grad_shift_two,
            grad_scale_two,
            grad_gate_two,
        ],
        axis=-1,
    )[:, 0, :]
    clip_part = lax.dot_general(
        member,
        grad_window_mod,
        (((0,), (0,)), ((), ())),
        precision=HIGHEST,
        preferred_element_type=jnp.float32,
    )
    table_part = (
        jnp.zeros((H, REL), jnp.float32)
        .at[:, index_table.reshape(-1)]
        .add(bias_grad.reshape(H, WIN * WIN))
    )
    grad_clip_mod, grad_table_all = lax.psum((clip_part, table_part), ("dp", "fsdp"))
    clip_low = grad_clip_mod.astype(jnp.bfloat16)
    clip_cols = lax.dynamic_slice_in_dim(clip_low, col_block * cols_ada, cols_ada, 1)
    grad_ada_weight = lax.dot_general(
        act_rows, clip_cols, (((0,), (0,)), ((), ())), preferred_element_type=jnp.float32
    )
    grad_ada_bias = jnp.sum(clip_cols.astype(jnp.float32), axis=0)
    cond_part = lax.dot_general(
        clip_cols, ada_weight, (((1,), (1,)), ((), ())), preferred_element_type=jnp.float32
    )
    cond_placed = lax.dynamic_update_slice_in_dim(
        jnp.zeros((clip_count, D), jnp.float32), cond_part, row_block * rows_ada, 1
    )
    cond_total = lax.psum(cond_placed, ("dp", "fsdp"))
    silu_value, silu_back = jax.vjp(jax.nn.silu, condition)
    grad_condition = silu_back(cond_total)[0]
    heads_own = rel_table.shape[0]
    grad_table = lax.dynamic_slice_in_dim(grad_table_all, col_block * heads_own, heads_own, 0)
    grad_qkv, grad_out, grad_up, grad_down = (
        lax.psum_scatter(
            grad_qkv_part.astype(jnp.bfloat16), "dp", scatter_dimension=1, tiled=True
        ).astype(jnp.float32),
        lax.psum_scatter(
            grad_out_part.astype(jnp.bfloat16), "dp", scatter_dimension=1, tiled=True
        ).astype(jnp.float32),
        lax.psum_scatter(
            grad_up_part.astype(jnp.bfloat16), "dp", scatter_dimension=1, tiled=True
        ).astype(jnp.float32),
        lax.psum_scatter(
            grad_down_part.astype(jnp.bfloat16), "dp", scatter_dimension=1, tiled=True
        ).astype(jnp.float32),
    )
    return (
        output,
        grad_tokens,
        grad_condition,
        grad_ada_weight,
        grad_ada_bias,
        grad_qkv,
        grad_out,
        grad_up,
        grad_down,
        grad_table,
    )


def solution(mesh):
    in_specs = (
        P(("dp", "fsdp"), None, None),
        P(),
        P(),
        P("fsdp", "dp"),
        P("dp"),
        P("fsdp", "dp"),
        P("fsdp", "dp"),
        P("fsdp", "dp"),
        P("fsdp", "dp"),
        P("dp", None),
        P(("dp", "fsdp"), None, None),
    )
    out_specs = (
        P(("dp", "fsdp"), None, None),
        P(("dp", "fsdp"), None, None),
        P(),
        P("fsdp", "dp"),
        P("dp"),
        P("fsdp", "dp"),
        P("fsdp", "dp"),
        P("fsdp", "dp"),
        P("fsdp", "dp"),
        P("dp", None),
    )
    return jax.shard_map(
        per_device, mesh=mesh, in_specs=in_specs, out_specs=out_specs, check_vma=False
    )
```

profile of v0, /device:TPU:0, one launch (start us, length us, event | category | flops | bytes accessed | tf_op | source)
XLA Modules:
  0.0 1903.5 jit_solution(1815682943499689542)
XLA Ops:
  10.0 63.4 %all-gather.12.cloned.1.call-done = bf16[256,6144]{1,0:T(8,128)(2,1)} async-done(((bf16[256,768]{1,0:T(8,128)(2,1)}), bf16[256,6144]{1,0:T(8,128)(2,1)}) %all-gather.12.cloned.1.call-update) | async-done | bytes 3145744 | tf_op jit(solution)/shard_map/all_gather | solution.py:138
  73.5 45.8 %all-gather.16.cloned.1.call-done = bf16[256,3072]{1,0:T(8,128)(2,1)} async-done(((bf16[256,384]{1,0:T(8,128)(2,1)}), bf16[256,3072]{1,0:T(8,128)(2,1)}) %all-gather.16.cloned.1.call-update) | async-done | bytes 1572880 | tf_op jit(solution)/shard_map/all_gather | solution.py:134
  119.4 30.5 %all_gather.46 = bf16[256,1024]{1,0:T(8,128)(2,1)} all-gather(bf16[256,128]{1,0:T(8,128)(2,1)S(1)} %copy-done.33), channel_id=1, replica_groups=mesh['dp'=8,'fsdp'=4] {'dp'}, dimensions={1}, use_global_device_ids=true | all-gather | bytes 589824 | tf_op jit(solution)/shard_map/all_gather | solution.py:135
  150.0 23.9 %all-gather.26.cloned.1.call-done = bf16[1024,1024]{1,0:T(8,128)(2,1)} async-done(((bf16[1024,128]{1,0:T(8,128)(2,1)}), bf16[1024,1024]{1,0:T(8,128)(2,1)}) %all-gather.26.cloned.1.call-update) | async-done | bytes 2097168 | tf_op jit(solution)/shard_map/all_gather | solution.py:137
  175.4 49.6 %all-gather.22.cloned.1.call-done = bf16[256,4096]{1,0:T(8,128)(2,1)} async-done(((bf16[256,512]{1,0:T(8,128)(2,1)}), bf16[256,4096]{1,0:T(8,128)(2,1)}) %all-gather.22.cloned.1.call-update) | async-done | bytes 2097168 | tf_op jit(solution)/shard_map/all_gather | solution.py:136
  225.1 30.5 %all-gather.1 = bf16[8,2,2025]{2,1,0:T(2,128)(2,1)S(1)} all-gather(bf16[1,2,2025]{2,1,0:T(2,128)(2,1)S(1)} %bitcast.159), channel_id=1, replica_groups=mesh['dp'=8,'fsdp'=4] {'dp'}, dimensions={0}, use_global_device_ids=true | all-gather | bytes 72900 | tf_op jit(solution)/shard_map/all_gather | solution.py:140
  255.7 30.3 %all-gather = bf16[8,1,768]{2,1,0:T(2,128)(2,1)S(1)} all-gather(bf16[1,1,768]{2,1,0:T(2,128)(2,1)S(1)} %reshape.619), channel_id=1, replica_groups=mesh['dp'=8,'fsdp'=4] {'dp'}, dimensions={0}, use_global_device_ids=true | all-gather | bytes 13824 | tf_op jit(solution)/shard_map/all_gather | solution.py:139
  286.4 338.7 %gather_fusion = f32[102400,16]{1,0:T(8,128)} fusion(f32[16,2025]{0,1:T(8,128)S(1)} %copy.97, s32[102400]{0:T(1024)S(1)} %broadcast_clamp_fusion), kind=kCustom, calls=%fused_computation | custom fusion | bytes 13516800 | tf_op jit(solution)/shard_map/gather | solution.py:160
  625.0 34.4 %copy.98 = f32[320,320,16]{0,1,2:T(8,128)} copy(f32[320,320,16]{2,1,0:T(8,128)} %bitcast.135) | data formatting | bytes 13107200 | tf_op jit(solution)/shard_map/gather | solution.py:160
  661.0 6.3 fusion.12
  668.6 9.0 convolution_convert_fusion.3
  677.5 10.4 reshape.633
  687.9 5.6 fusion.72
  693.5 3.9 copy.132
  697.5 4.5 copy.131
  702.0 5.4 copy.130
  707.4 10.1 fusion.73
  717.5 8.3 fusion
  725.8 9.6 fusion.31
  735.4 5.6 fusion.71
  746.2 12.1 fusion.74
  758.3 19.5 %fusion.5 = (bf16[640,4096]{1,0:T(8,128)(2,1)S(1)}, f32[640,4096]{1,0:T(8,128)}) fusion(f32[640,4096]{1,0:T(8,128)} %fusion.74, bf16[640,1024]{1,0:T(8,128)(2,1)} %bitcast.148, bf16[1024,4096]{1,0:T(8,128)(2,1)} %all-gather.24.cloned.1.call-done), kind=kOutput, calls=%fused_computation.18 | convolution fusion | flops 5431623680 | bytes 35913728 | tf_op jit(solution)/shard_map/dot_general | solution.py:66
  777.9 5.6 fusion.75
  793.0 3.9 copy.102
  802.2 4.8 convolution_convert_fusion.4
  808.4 11.8 multiply_reduce_fusion
  820.2 15.5 convert_reduce_fusion
  839.8 8.0 fusion.28
  850.9 9.3 copy.109
  860.2 10.1 convert_element_type.164
  870.4 9.2 convolution_convert_fusion.2
  880.8 13.7 convolution_convert_fusion.1
  896.0 12.4 convolution_convert_fusion
  908.9 9.0 copy.111
  917.9 7.4 reshape.611
  925.2 26.0 %copy.112 = f32[102400,16]{1,0:T(8,128)} copy(f32[102400,16]{0,1:T(8,128)} %bitcast.136) | data formatting | bytes 13107200 | tf_op jit(solution)/shard_map/reshape | solution.py:261
  951.2 543.6 %scatter_custom_fusion = f32[16,2025]{0,1:T(8,128)} fusion(s32[102400]{0:T(1024)S(1)} %bitcast.154, f32[102400,16]{1,0:T(8,128)} %copy.112, f32[]{:T(128)} %constant.172.clone.1), kind=kCustom, calls=%fused_computation.82 | custom fusion | flops 1638400 | bytes 130112 | tf_op jit(solution)/shard_map/scatter-add | solution.py:261
  1499.8 3.9 copy.124
  1507.2 7.9 fusion.25
  1518.1 11.9 fusion.69
  1530.2 3.7 multiply_reduce_fusion.1
  1534.4 37.8 %psum.21 = bf16[3,6144]{1,0:T(4,128)(2,1)S(1)} all-reduce(f32[3,6144]{1,0:T(4,128)S(1)} %fusion.42), channel_id=1, replica_groups=mesh['dp'=8,'fsdp'=4] {'dp','fsdp'}, use_global_device_ids=true, to_apply=%region_21.22 | all-reduce | flops 18432 | bytes 110592 | tf_op jit(solution)/shard_map/psum | solution.py:263
  1573.0 41.4 %psum.22 = f32[3,1024]{1,0:T(4,128)S(1)} all-reduce(f32[3,1024]{1,0:T(4,128)S(1)} %convolution_dynamic-update-slice_fusion), channel_id=1, replica_groups=mesh['dp'=8,'fsdp'=4] {'dp','fsdp'}, use_global_device_ids=true, to_apply=%region_22.23 | all-reduce | flops 3072 | bytes 24576 | tf_op jit(solution)/shard_map/psum | solution.py:276
  1616.9 3.9 all-reduce.2.cloned.1.call-done
  1623.3 62.6 %reduce-scatter.27.cloned.1.call-done = bf16[128,256]{1,0:T(8,128)(2,1)} async-done(((bf16[1024,256]{1,0:T(8,128)(2,1)}), bf16[128,256]{1,0:T(8,128)(2,1)}) %reduce-scatter.27.cloned.1.call-update) | async-done | bytes 65552
  1687.5 65.5 %reduce-scatter.25.cloned.1.call-done = bf16[384,256]{1,0:T(8,128)(2,1)} async-done(((bf16[3072,256]{1,0:T(8,128)(2,1)}), bf16[384,256]{1,0:T(8,128)(2,1)}) %reduce-scatter.25.cloned.1.call-update) | async-done | bytes 196624
  1754.8 68.5 %reduce-scatter.29.cloned.1.call-done = bf16[128,1024]{1,0:T(8,128)(2,1)} async-done(((bf16[1024,1024]{1,0:T(8,128)(2,1)}), bf16[128,1024]{1,0:T(8,128)(2,1)}) %reduce-scatter.29.cloned.1.call-update) | async-done | bytes 262160
  1825.3 69.1 %reduce-scatter.21.cloned.1.call-done = bf16[256,512]{1,0:T(8,128)(2,1)} async-done(((bf16[256,4096]{1,0:T(8,128)(2,1)}), bf16[256,512]{1,0:T(8,128)(2,1)}) %reduce-scatter.21.cloned.1.call-update) | async-done | bytes 262160 | tf_op jit(solution)/shard_map/reduce_scatter | solution.py:288
  (235 shorter events, 64.0 us)
Async XLA Ops:
  7.2 66.2 %all-gather.12.cloned.1.call-start = ((), (), s32[]{:S(2)}) async-start(), calls=%async_computation.8 | async-start | bytes 3538944 | tf_op jit(solution)/shard_map/all_gather | solution.py:138
  7.9 111.4 %all-gather.16.cloned.1.call-start = ((), (), s32[]{:S(2)}) async-start(), calls=%async_computation.10 | async-start | bytes 1769472 | tf_op jit(solution)/shard_map/all_gather | solution.py:134
  8.7 110.7 %copy-start.33 = (bf16[256,128]{1,0:T(8,128)(2,1)S(1)}, bf16[256,128]{1,0:T(8,128)(2,1)}, u32[]{:S(2)}) copy-start(bf16[256,128]{1,0:T(8,128)(2,1)} %param.17) | copy-start | bytes 196612
  8.7 165.2 %all-gather.26.cloned.1.call-start = ((), (), s32[]{:S(2)}) async-start(), calls=%async_computation.15 | async-start | bytes 2359296 | tf_op jit(solution)/shard_map/all_gather | solution.py:137
  9.4 215.7 %all-gather.22.cloned.1.call-start = ((), (), s32[]{:S(2)}) async-start(), calls=%async_computation.13 | async-start | bytes 2359296 | tf_op jit(solution)/shard_map/all_gather | solution.py:136
  10.0 651.0 %all-gather.14.cloned.1.call-start = ((), (), s32[]{:S(2)}) async-start(), calls=%async_computation.9 | async-start | bytes 15728640 | tf_op jit(solution)/shard_map/all_gather | solution.py:148
  73.5 595.1 %all-gather.18.cloned.1.call-start = ((), (), s32[]{:S(2)}) async-start(), calls=%async_computation.11 | async-start | bytes 7864320 | tf_op jit(solution)/shard_map/all_gather | solution.py:68
  119.3 55.8 %copy-start.55 = (s32[3]{0:T(128)S(1)}, s32[3]{0:T(128)}, u32[]{:S(2)}) copy-start(s32[3]{0:T(128)} %param.13) | copy-start | bytes 40
  119.3 616.0 %all-gather.20.cloned.1.call-start = ((), (), s32[]{:S(2)}) async-start(), calls=%async_computation.12 | async-start | bytes 2621440 | tf_op jit(solution)/shard_map/all_gather | solution.py:68
  150.0 596.2 %all-gather.28.cloned.1.call-start = ((), (), s32[]{:S(2)}) async-start(), calls=%async_computation.16 | async-start | bytes 10485760 | tf_op jit(solution)/shard_map/all_gather | solution.py:68
  173.9 51.2 %copy-start.51 = (bf16[2,2025]{1,0:T(2,128)(2,1)S(1)}, bf16[2,2025]{1,0:T(2,128)(2,1)}, u32[]{:S(2)}) copy-start(bf16[2,2025]{1,0:T(2,128)(2,1)} %param.20) | copy-start | bytes 24304
  173.9 81.7 %copy-start.54 = (bf16[768]{0:T(1024)(128)(2,1)S(1)}, bf16[768]{0:T(1024)(128)(2,1)}, u32[]{:S(2)}) copy-start(bf16[768]{0:T(1024)(128)(2,1)} %param.15) | copy-start | bytes 4612
  173.9 584.4 %all-gather.24.cloned.1.call-start = ((), (), s32[]{:S(2)}) async-start(), calls=%async_computation.14 | async-start | bytes 10485760 | tf_op jit(solution)/shard_map/all_gather | solution.py:68
  174.0 486.6 %copy-start.31 = (s32[320]{0:T(512)}, s32[320]{0:T(512)S(1)}, u32[]{:S(2)}) copy-start(s32[320]{0:T(512)S(1)} %add_select_fusion.4) | copy-start | bytes 3844
  225.1 1269.8 %reduce-scatter.17.cloned.1.call-start = ((), (), s32[]{:S(2)}) async-start(), calls=%async_computation.18 | async-start | bytes 2621440 | tf_op jit(solution)/shard_map/reduce_scatter | solution.py:83
  625.0 34.8 %copy-start.2 = (bf16[2,320,1024]{2,1,0:T(8,128)(2,1)S(1)}, bf16[2,320,1024]{2,1,0:T(8,128)(2,1)}, u32[]{:S(2)}) copy-start(bf16[2,320,1024]{2,1,0:T(8,128)(2,1)} %param.11) | copy-start | bytes 3932164
  659.6 7.7 copy-start.52
  660.1 7.3 copy-start.27
  660.7 125.3 %copy-start.36 = (pred[2,320]{1,0:T(4,128)(4,1)}, pred[2,320]{1,0:T(4,128)(4,1)S(1)}, u32[]{:S(2)}) copy-start(pred[2,320]{1,0:T(4,128)(4,1)S(1)} %broadcast_compare_fusion) | copy-start | bytes 1924
  667.4 74.0 %copy-start.29 = (f32[2,1024]{1,0:T(2,128)}, f32[2,1024]{1,0:T(2,128)S(1)}, u32[]{:S(2)}) copy-start(f32[2,1024]{1,0:T(2,128)S(1)} %get-tuple-element.125) | copy-start | bytes 24580
  668.5 9.0 copy-start.20
  697.5 9.9 copy-start.6
  702.0 15.5 copy-start.8
  717.5 8.3 copy-start.16
  741.0 44.2 %copy-start = (f32[2,320,1024]{2,1,0:T(8,128)}, f32[2,320,1024]{2,1,0:T(8,128)S(1)}, u32[]{:S(2)}) copy-start(f32[2,320,1024]{2,1,0:T(8,128)S(1)} %get-tuple-element.119) | copy-start | bytes 7864324
  758.3 19.5 %copy-start.56 = (bf16[1024,4096]{1,0:T(8,128)(2,1)S(1)}, bf16[1024,4096]{1,0:T(8,128)(2,1)}, u32[]{:S(2)}) copy-start(bf16[1024,4096]{1,0:T(8,128)(2,1)} %all-gather.24.cloned.1.call-done) | copy-start | bytes 25165828
  807.0 690.0 %reduce-scatter.15.cloned.1.call-start = ((), (), s32[]{:S(2)}) async-start(), calls=%async_computation.17 | async-start | bytes 7864320 | tf_op jit(solution)/shard_map/reduce_scatter | solution.py:83
  820.2 15.5 copy-start.9
  860.2 10.2 copy-start.21
  879.5 620.2 %reduce-scatter.23.cloned.1.call-start = ((), (), s32[]{:S(2)}) async-start(), calls=%async_computation.21 | async-start | bytes 10485760 | tf_op jit(solution)/shard_map/reduce_scatter | solution.py:83
  894.6 623.4 %reduce-scatter.19.cloned.1.call-start = ((), (), s32[]{:S(2)}) async-start(), calls=%async_computation.19 | async-start | bytes 10485760 | tf_op jit(solution)/shard_map/reduce_scatter | solution.py:83
  908.4 712.3 %all-reduce.2.cloned.1.call-start = ((), (), s32[]{:S(2)}) async-start(), calls=%async_computation.22 | async-start | bytes 2080768 | tf_op jit(solution)/shard_map/psum | solution.py:263
  1494.8 191.0 %reduce-scatter.27.cloned.1.call-start = ((), (), s32[]{:S(2)}) async-start(), calls=%async_computation.24 | async-start | bytes 589824
  1497.0 256.0 %reduce-scatter.25.cloned.1.call-start = ((), (), s32[]{:S(2)}) async-start(), calls=%async_computation.23 | async-start | bytes 1769472
  1499.7 323.7 %reduce-scatter.29.cloned.1.call-start = ((), (), s32[]{:S(2)}) async-start(), calls=%async_computation.25 | async-start | bytes 2359296
  1503.7 390.7 %reduce-scatter.21.cloned.1.call-start = ((), (), s32[]{:S(2)}) async-start(), calls=%async_computation.20 | async-start | bytes 2359296 | tf_op jit(solution)/shard_map/reduce_scatter | solution.py:288
  1507.1 8.0 copy-start.49
  1507.2 9.4 copy-start.43
  1518.1 12.0 copy-start.1
  1518.1 12.0 copy-start.5
  1518.1 12.0 copy-start.12
  1518.1 12.0 copy-start.14
  1518.1 12.0 copy-start.15
  1518.1 12.0 copy-start.30
  1518.1 12.0 copy-start.37
  1518.1 12.0 copy-start.47
  1530.2 42.6 %copy-start.19 = (bf16[256,768]{1,0:T(8,128)(2,1)S(1)}, bf16[256,768]{1,0:T(8,128)(2,1)}, u32[]{:S(2)}) copy-start(bf16[256,768]{1,0:T(8,128)(2,1)} %param.14) | copy-start | bytes 1179652
  1530.2 84.2 %copy-start.35 = (f32[3,1024]{1,0:T(4,128)S(1)}, f32[3,1024]{1,0:T(4,128)}, u32[]{:S(2)}) copy-start(f32[3,1024]{1,0:T(4,128)} %param.12) | copy-start | bytes 36868
  (28 other events, 70.0 us)
Sparse Core Ops, SparseCore 0:
  10.2 63.1 all-gather.11
  75.5 43.7 all-gather.15
  121.4 52.4 all-gather.25
  175.8 49.2 all-gather.21
  226.5 80.2 all-gather.13
  308.2 46.3 all-gather.17
  356.2 22.5 all-gather.19
  380.4 58.2 all-gather.27
  440.3 58.2 all-gather.23
  807.1 29.4 reduce-scatter.16
  879.7 55.5 reduce-scatter.14
  937.7 71.7 reduce-scatter.22
  1012.2 71.7 reduce-scatter.18
  1495.0 125.7 all-reduce.1
  1624.9 60.9 reduce-scatter.26
  1689.2 63.7 reduce-scatter.24
  1756.8 66.5 reduce-scatter.28
  1827.2 67.2 reduce-scatter.20
where the time goes:
time: 1920 us; the launch traced here: 1900 us
  other arithmetic  590 us (31%)
  local copies, waits for them, and re-layouts  505 us (26%)
  waiting for transfers between devices  455 us (24%)
  blocking collectives  171 us (9%)
  matrix products  166 us (9%)
    scatter-add x1, other arithmetic, per_device(): table_part = jnp.zeros((H, REL), jnp.float32).at[:, index_table.reshape(-...  544 us
    gather x2, local copies, waits for them, and re-layouts, per_device(): rel_bias = table_all.astype(jnp.float32)[:, index_table]  373 us
    unnamed x21, waiting for transfers between devices  199 us
    reduce_scatter x1, waiting for transfers between devices, per_device(): lax.psum_scatter(grad_up_part.astype(jnp.bfloat16), 'dp', scatter_dimensi...  69.1 us
    all_gather x1, waiting for transfers between devices, per_device(): lax.all_gather(ada_weight, 'dp', axis=1, tiled=True)  63.4 us
    all_gather x1, waiting for transfers between devices, per_device(): lax.all_gather(up_weight, 'dp', axis=1, tiled=True)  49.6 us
    dot_general x4, matrix products, fold_rows(): jnp.dot(left, lax.all_gather(columns, 'fsdp', axis=0, tiled=True), prefer...  45.9 us
    all_gather x1, waiting for transfers between devices, per_device(): lax.all_gather(qkv_weight, 'dp', axis=1, tiled=True)  45.8 us
  transfers between devices with their start and end apart: 18, of which 9 were waited for; matrix products, arithmetic and copies ran while one was open for 63% of the time, Pallas kernels for 0%

commit v1 on v0

v1 whole, which is shorter than its diff:
```python
import functools

import jax
import jax.numpy as jnp
from jax import lax
from jax.experimental import pallas as pl
from jax.experimental.pallas import tpu as pltpu
from jax.sharding import PartitionSpec as P

D = 1024
H = 16
HD = 64
WT = 5
WSIDE = 8
WIN = 320
SPW = 16
CELLS = WSIDE * WSIDE
FRAMES = 2 * WT - 1
OFFSETS = (2 * WSIDE - 1) ** 2
REL = FRAMES * OFFSETS
LANES = 128
TILE = 256

EPSILON = 1e-06
NEGATIVE = -1000000000.0
HIGHEST = lax.Precision.HIGHEST
F32 = jnp.float32
BF16 = jnp.bfloat16
MESH = pl.DeviceIdType.MESH
MIB = 2**20

QKV, OUT, UP, DOWN, UNITS = 0, 3, 4, 8, 12
SHARE = 256
HALF = 128


def window_layout(clip_frames, first_window, window_count):
    slab_count = 1 + (clip_frames > WT).astype(jnp.int32)
    starts = jnp.cumsum(slab_count, dtype=jnp.int32) - slab_count
    global_window = first_window + jnp.arange(window_count, dtype=jnp.int32)
    slab_of = global_window // SPW
    owners = jnp.sum((starts[None, :] <= slab_of[:, None]).astype(jnp.int32), axis=1) - 1
    clip_ids = jnp.arange(clip_frames.shape[0], dtype=jnp.int32)
    member = (owners[:, None] == clip_ids[None, :]).astype(jnp.int32)
    clip_start = jnp.sum(member * starts[None, :], axis=1)
    own_frames = jnp.sum(member * clip_frames[None, :], axis=1)
    inner_slab = slab_of - clip_start
    return (jnp.minimum(own_frames - WT * inner_slab, WT), member)


def pair_onehot():
    side_span = 2 * WSIDE - 1
    pair = lax.broadcasted_iota(jnp.int32, (OFFSETS, CELLS * CELLS), 1)
    offset = lax.broadcasted_iota(jnp.int32, (OFFSETS, CELLS * CELLS), 0)
    own, other = pair // CELLS, pair % CELLS
    row_diff = own // WSIDE - other // WSIDE + (WSIDE - 1)
    col_diff = own % WSIDE - other % WSIDE + (WSIDE - 1)
    return (row_diff * side_span + col_diff == offset).astype(BF16)


def bias_strips(table):
    heads = table.shape[0]
    by_frame = table.reshape(heads, FRAMES, OFFSETS)[:, ::-1].reshape(heads * FRAMES, OFFSETS)
    strips = jnp.dot(by_frame, pair_onehot(), preferred_element_type=F32)
    strips = strips.astype(BF16).reshape(heads, FRAMES, CELLS, CELLS)
    return strips.transpose(0, 2, 1, 3).reshape(heads, CELLS, FRAMES * CELLS)


def strips_to_table(strips):
    heads = strips.shape[0]
    by_frame = strips.reshape(heads, CELLS, FRAMES, CELLS).transpose(0, 2, 1, 3)
    by_frame = by_frame.reshape(heads * FRAMES, CELLS * CELLS)
    sums = lax.dot_general(
        by_frame,
        pair_onehot().astype(F32),
        (((1,), (1,)), ((), ())),
        precision=HIGHEST,
        preferred_element_type=F32,
    )
    return sums.reshape(heads, FRAMES, OFFSETS)[:, ::-1].reshape(heads, FRAMES * OFFSETS)


def units_of(qkv, out, up, down):
    return jnp.concatenate(
        [
            qkv.reshape(D, 8, 3, LANES).transpose(2, 1, 0, 3),
            out.reshape(D, 8, 1, LANES).transpose(2, 1, 0, 3),
            up.reshape(D, 8, 4, LANES).transpose(2, 1, 0, 3),
            down.reshape(8, 4, LANES, 8, LANES).transpose(1, 3, 0, 2, 4).reshape(4, 8, D, LANES),
        ]
    )


def weights_of(units):
    def columns(part):
        return part.transpose(2, 1, 0, 3).reshape(D, -1)

    down = units[DOWN:].reshape(4, 8, 8, LANES, LANES).transpose(2, 0, 3, 1, 4)
    return (
        columns(units[QKV:OUT]),
        columns(units[OUT:UP]),
        columns(units[UP:DOWN]),
        down.reshape(4 * D, D),
    )


def own_units(qkv, out, up, down):
    def columns(part):
        return part.reshape(SHARE, -1, LANES).transpose(1, 0, 2)

    down = down.reshape(2, 4, LANES, LANES).transpose(1, 0, 2, 3).reshape(4, SHARE, LANES)
    return jnp.concatenate([columns(qkv), columns(out), columns(up), down])


def own_blocks(shares):
    def columns(part):
        return part.transpose(1, 0, 2).reshape(SHARE, -1)

    down = shares[DOWN:].reshape(4, 2, LANES, LANES).transpose(1, 0, 2, 3).reshape(4 * SHARE, LANES)
    return (columns(shares[QKV:OUT]), columns(shares[OUT:UP]), columns(shares[UP:DOWN]), down)


def dot(left, right):
    return jnp.dot(left, right, preferred_element_type=F32)


def dot_rows(left, right):
    return lax.dot_general(left, right, (((1,), (1,)), ((), ())), preferred_element_type=F32)


def dot_tokens(left, right):
    return lax.dot_general(left, right, (((0,), (0,)), ((), ())), preferred_element_type=F32)


def tile(index):
    return pl.ds(pl.multiple_of(index * TILE, TILE), TILE)


def two_columns(unit, index):
    return jnp.concatenate([unit[2 * index], unit[2 * index + 1]], axis=1)


def some_rows(unit, index):
    return jnp.concatenate([unit[block, tile(index), :] for block in range(8)], axis=1)


def loop(count, body):
    def step(index, carry):
        body(index)
        return carry

    lax.fori_loop(0, count, step, 0)


def centered(values):
    center = values - jnp.mean(values, axis=-1, keepdims=True)
    spread = jnp.mean(center * center, axis=-1, keepdims=True)
    root = lax.rsqrt(spread + EPSILON)
    return center * root, root


def enter_kernel(tokens_ref, mod_ref, held_ref, normed_ref, packed_ref, unit_ref, sems):
    rows = 32

    def fetch(j):
        return pltpu.make_async_copy(held_ref.at[QKV + j], unit_ref.at[j % 2], sems.at[j % 2])

    fetch(0).start()
    for window in range(mod_ref.shape[0]):
        shift, scale = mod_ref[window, 0:1, :], mod_ref[window, 1:2, :]

        def step(index, window=window, shift=shift, scale=scale):
            at = pl.ds(pl.multiple_of(window * WIN + index * rows, rows), rows)
            normal, _ = centered(tokens_ref[at, :].astype(F32))
            normed_ref[at, :] = (normal * (1.0 + scale) + shift).astype(BF16)

        loop(WIN // rows, step)
    for j in range(3):
        fetch(j).wait()
        if j < 2:
            fetch(j + 1).start()

        def project(index, j=j):
            packed_ref[j, :, tile(index)] = dot(
                normed_ref[...], two_columns(unit_ref.at[j % 2], index)
            ).astype(BF16)

        loop(4, project)


def vmem():
    return pl.BlockSpec(memory_space=pltpu.VMEM)


def enter(tokens, mod, held):
    rows = tokens.shape[0]
    return pl.pallas_call(
        enter_kernel,
        in_specs=[vmem(), vmem(), pl.BlockSpec(memory_space=pl.ANY)],
        out_specs=[vmem(), vmem()],
        out_shape=[
            jax.ShapeDtypeStruct((rows, D), BF16),
            jax.ShapeDtypeStruct((3, rows, D), BF16),
        ],
        scratch_shapes=[pltpu.VMEM((2, 8, D, LANES), BF16), pltpu.SemaphoreType.DMA((2,))],
        compiler_params=pltpu.CompilerParams(vmem_limit_bytes=50 * MIB),
        name="enter",
    )(tokens, mod, held)


def attend_kernel(live_ref, query_ref, key_ref, value_ref, strip_ref, mixed_ref, probs_ref):
    live = live_ref[pl.program_id(1)] * CELLS
    key_live = lax.broadcasted_iota(jnp.int32, (1, WIN), 1) < live
    for head in range(2):
        lanes = slice(head * HD, (head + 1) * HD)
        query = query_ref[:, lanes] * BF16(HD ** (-0.5))
        keys = key_ref[:, lanes]
        values = value_ref[:, lanes]
        for frame in range(WT):
            rows = slice(frame * CELLS, (frame + 1) * CELLS)
            first = (WT - 1 - frame) * CELLS
            scores = dot_rows(query[rows], keys)
            scores = scores + strip_ref[head, :, first : first + WIN].astype(F32)
            scores = jnp.where(key_live, scores, NEGATIVE)
            shifted = jnp.exp(scores - jnp.max(scores, axis=-1, keepdims=True))
            totals = jnp.sum(shifted, axis=-1, keepdims=True)
            probs = (shifted * (1.0 / totals)).astype(BF16)
            probs_ref[head, rows] = probs
            mixed_ref[rows, lanes] = dot(probs, values).astype(BF16)


def packed_block(part):
    pairs = H // 2
    return pl.BlockSpec(
        (None, WIN, LANES),
        lambda pair, window, *_: (
            lax.rem(part * pairs + pair, 3),
            window,
            lax.div(part * pairs + pair, 3),
        ),
    )


def attend(packed, strips, live_frames):
    window_count = live_frames.shape[0]
    pairs = H // 2
    return pl.pallas_call(
        attend_kernel,
        grid_spec=pltpu.PrefetchScalarGridSpec(
            num_scalar_prefetch=1,
            grid=(pairs, window_count),
            in_specs=[
                packed_block(0),
                packed_block(1),
                packed_block(2),
                pl.BlockSpec((2, *strips.shape[1:]), lambda p, w, live: (p, 0, 0)),
            ],
            out_specs=[
                pl.BlockSpec((WIN, LANES), lambda p, w, live: (w, p)),
                pl.BlockSpec((None, 2, WIN, WIN), lambda p, w, live: (w, p, 0, 0)),
            ],
        ),
        out_shape=[
            jax.ShapeDtypeStruct((window_count * WIN, D), BF16),
            jax.ShapeDtypeStruct((window_count, H, WIN, WIN), BF16),
        ],
        name="attend",
    )(live_frames, packed, packed, packed, strips)


def attend_back_kernel(
    query_ref, key_ref, value_ref, probs_ref, grad_ref, gq_ref, gk_ref, gv_ref, strip_ref
):
    @pl.when(pl.program_id(1) == 0)
    def _():
        strip_ref[...] = jnp.zeros_like(strip_ref)

    for head in range(2):
        lanes = slice(head * HD, (head + 1) * HD)
        scale = BF16(HD ** (-0.5))
        query = query_ref[:, lanes] * scale
        keys = key_ref[:, lanes] * scale
        values = value_ref[:, lanes]
        grad = grad_ref[:, lanes]
        probs = probs_ref[head]
        gv_ref[:, lanes] = dot_tokens(grad, probs).T.astype(BF16)
        pieces = []
        for frame in range(WT):
            rows = slice(frame * CELLS, (frame + 1) * CELLS)
            first = (WT - 1 - frame) * CELLS
            grad_probs = dot_rows(grad[rows], values)
            weight = probs[rows].astype(F32)
            product = weight * grad_probs
            total = jnp.sum(product, axis=-1, keepdims=True)
            grad_scores = (product - weight * total).astype(BF16)
            strip_ref[head, :, first : first + WIN] += grad_scores.astype(F32)
            gq_ref[rows, lanes] = dot(grad_scores, keys).astype(BF16)
            pieces.append(grad_scores)
        gk_ref[:, lanes] = dot_tokens(query, jnp.concatenate(pieces, axis=0)).T.astype(BF16)


def attend_back(packed, probs, grad_mixed):
    window_count = probs.shape[0]
    rows = window_count * WIN
    pairs = H // 2

    def block():
        return pl.BlockSpec((WIN, LANES), lambda p, w: (w, p))

    return pl.pallas_call(
        attend_back_kernel,
        grid=(pairs, window_count),
        in_specs=[
            packed_block(0),
            packed_block(1),
            packed_block(2),
            pl.BlockSpec((None, 2, WIN, WIN), lambda p, w: (w, p, 0, 0)),
            block(),
        ],
        out_specs=[
            block(),
            block(),
            block(),
            pl.BlockSpec((2, CELLS, FRAMES * CELLS), lambda p, w: (p, 0, 0)),
        ],
        out_shape=[jax.ShapeDtypeStruct((rows, D), BF16)] * 3
        + [jax.ShapeDtypeStruct((H, CELLS, FRAMES * CELLS), F32)],
        name="attend_back",
    )(packed, packed, packed, probs, grad_mixed)


def each_rows(mod_ref, live_ref, body, rows=16):
    for window in range(mod_ref.shape[0]):
        live = live_ref[window] * CELLS

        def step(index, window=window, live=live):
            at = pl.ds(pl.multiple_of(window * WIN + index * rows, rows), rows)
            mods = [mod_ref[window, k : k + 1, :] for k in range(6)]
            slot = index * rows + lax.broadcasted_iota(jnp.int32, (rows, 1), 0)
            body(window, at, mods, slot < live)

        loop(WIN // rows, step)


def add_sums(sums_ref, window, which, values):
    sums_ref[window, which : which + 1, :] += jnp.sum(values, axis=0, keepdims=True)


def norm_back(grad_normed, normal, root, scale):
    grad = grad_normed * (1.0 + scale)
    mean = jnp.mean(grad, axis=-1, keepdims=True)
    along = jnp.mean(grad * normal, axis=-1, keepdims=True)
    return root * (grad - mean - normal * along)


def middle_kernel(
    live_ref,
    tokens_ref,
    cotangent_ref,
    mixed_ref,
    mod_ref,
    held_ref,
    output_ref,
    grad_middle_ref,
    grad_mixed_ref,
    sums_ref,
    part_ref,
    unit_ref,
    attended_ref,
    normed_ref,
    grad_low_ref,
    mlp_ref,
    grad_normed_ref,
    activated_ref,
    grad_hidden_ref,
    made_ref,
    fetch_sem,
    made_sem,
):
    order = [OUT] + [unit for j in range(4) for unit in (UP + j, DOWN + j)] + [OUT]

    def fetch(step):
        return pltpu.make_async_copy(
            held_ref.at[order[step]], unit_ref.at[step % 4], fetch_sem.at[step % 4]
        )

    def put(slot, unit):
        return pltpu.make_async_copy(made_ref.at[slot], part_ref.at[unit], made_sem.at[slot])

    for step in range(3):
        fetch(step).start()
    sums_ref[...] = jnp.zeros_like(sums_ref)
    mlp_ref[...] = jnp.zeros_like(mlp_ref)
    grad_normed_ref[...] = jnp.zeros_like(grad_normed_ref)
    fetch(0).wait()

    def project(index):
        attended_ref[:, tile(index)] = dot(mixed_ref[...], two_columns(unit_ref.at[0], index))

    loop(4, project)

    def modulate(window, at, mods, live):
        middle = tokens_ref[at, :].astype(F32) + mods[2] * attended_ref[at, :]
        normal, _ = centered(middle)
        normed_ref[at, :] = (normal * (1.0 + mods[4]) + mods[3]).astype(BF16)
        grad = jnp.where(live, cotangent_ref[at, :].astype(F32), 0.0)
        grad_low_ref[at, :] = (mods[5] * grad).astype(BF16)

    each_rows(mod_ref, live_ref, modulate)
    for j in range(4):
        step = 1 + 2 * j
        up, down = unit_ref.at[step % 4], unit_ref.at[(step + 1) % 4]
        fetch(step).wait()
        fetch(step + 1).wait()
        fetch(step + 2).start()
        if j < 3:
            fetch(step + 3).start()

        def hide(index, up=up, down=down):
            hidden = dot(normed_ref[...], two_columns(up, index))
            bend = jnp.tanh(0.7978845608028654 * (hidden + 0.044715 * hidden * hidden * hidden))
            activated_ref[:, tile(index)] = (0.5 * hidden * (1.0 + bend)).astype(BF16)
            slope = 0.5 * (1.0 + bend) + 0.5 * hidden * (1.0 - bend * bend) * (
                0.7978845608028654 * (1.0 + 3.0 * 0.044715 * hidden * hidden)
            )
            grad_activated = dot_rows(grad_low_ref[...], some_rows(down, index))
            grad_hidden_ref[:, tile(index)] = (grad_activated * slope).astype(BF16)

        loop(4, hide)
        if j > 0:
            put(0, DOWN + j - 1).wait()

        def down_gradient(index):
            made = dot_tokens(activated_ref[:, tile(index)], grad_low_ref[...]).astype(BF16)
            for block in range(8):
                made_ref[0, block, tile(index), :] = made[:, block * LANES : (block + 1) * LANES]

        loop(4, down_gradient)
        put(0, DOWN + j).start()
        if j > 0:
            put(1, UP + j - 1).wait()

        def up_gradient(index):
            made = dot_tokens(normed_ref[...], grad_hidden_ref[:, tile(index)]).astype(BF16)
            made_ref[1, 2 * index] = made[:, :LANES]
            made_ref[1, 2 * index + 1] = made[:, LANES:]

        loop(4, up_gradient)
        put(1, UP + j).start()

        def out_of_mlp(index, up=up, down=down):
            mlp_ref[:, tile(index)] += dot(activated_ref[...], two_columns(down, index))
            grad_normed_ref[:, tile(index)] += dot_rows(grad_hidden_ref[...], some_rows(up, index))

        loop(4, out_of_mlp)

    def join(window, at, mods, live):
        attended = attended_ref[at, :]
        middle = tokens_ref[at, :].astype(F32) + mods[2] * attended
        normal, root = centered(middle)
        mlp = mlp_ref[at, :]
        output_ref[at, :] = jnp.where(live, middle + mods[5] * mlp, 0.0).astype(BF16)
        grad_result = jnp.where(live, cotangent_ref[at, :].astype(F32), 0.0)
        grad_normed = grad_normed_ref[at, :]
        grad_middle = grad_result + norm_back(grad_normed, normal, root, mods[4])
        grad_middle_ref[at, :] = grad_middle
        grad_low_ref[at, :] = (mods[2] * grad_middle).astype(BF16)
        add_sums(sums_ref, window, 2, grad_middle * attended)
        add_sums(sums_ref, window, 3, grad_normed)
        add_sums(sums_ref, window, 4, grad_normed * normal)
        add_sums(sums_ref, window, 5, grad_result * mlp)

    each_rows(mod_ref, live_ref, join)
    fetch(9).wait()
    put(0, DOWN + 3).wait()

    def back(index):
        made = dot_tokens(mixed_ref[...], grad_low_ref[:, tile(index)]).astype(BF16)
        made_ref[0, 2 * index] = made[:, :LANES]
        made_ref[0, 2 * index + 1] = made[:, LANES:]
        grad_mixed_ref[:, tile(index)] = dot_rows(
            grad_low_ref[...], some_rows(unit_ref.at[1], index)
        ).astype(BF16)

    loop(4, back)
    put(0, OUT).start()
    put(1, UP + 3).wait()
    put(0, OUT).wait()


def middle(live_frames, tokens, cotangent, mixed, mod, held):
    rows = tokens.shape[0]
    unit = (8, D, LANES)
    return pl.pallas_call(
        middle_kernel,
        in_specs=[
            pl.BlockSpec(memory_space=pltpu.SMEM),
            vmem(),
            vmem(),
            vmem(),
            vmem(),
            pl.BlockSpec(memory_space=pl.ANY),
        ],
        out_specs=[vmem(), vmem(), vmem(), vmem(), pl.BlockSpec(memory_space=pl.ANY)],
        out_shape=[
            jax.ShapeDtypeStruct((rows, D), BF16),
            jax.ShapeDtypeStruct((rows, D), F32),
            jax.ShapeDtypeStruct((rows, D), BF16),
            jax.ShapeDtypeStruct((mod.shape[0], 8, D), F32),
            jax.ShapeDtypeStruct((UNITS, *unit), BF16),
        ],
        scratch_shapes=[
            pltpu.VMEM((4, *unit), BF16),
            pltpu.VMEM((rows, D), F32),
            pltpu.VMEM((rows, D), BF16),
            pltpu.VMEM((rows, D), BF16),
            pltpu.VMEM((rows, D), F32),
            pltpu.VMEM((rows, D), F32),
            pltpu.VMEM((rows, D), BF16),
            pltpu.VMEM((rows, D), BF16),
            pltpu.VMEM((2, *unit), BF16),
            pltpu.SemaphoreType.DMA((4,)),
            pltpu.SemaphoreType.DMA((2,)),
        ],
        compiler_params=pltpu.CompilerParams(vmem_limit_bytes=56 * MIB),
        name="middle",
    )(live_frames, tokens, cotangent, mixed, mod, held)


def leave_kernel(
    live_ref,
    tokens_ref,
    mod_ref,
    normed_ref,
    grad_middle_ref,
    gq_ref,
    gk_ref,
    gv_ref,
    held_ref,
    part_in_ref,
    grad_tokens_ref,
    sums_ref,
    part_ref,
    unit_ref,
    packed_ref,
    grad_normed_ref,
    made_ref,
    fetch_sem,
    made_sem,
):
    sources = (gq_ref, gk_ref, gv_ref)

    def fetch(j):
        return pltpu.make_async_copy(held_ref.at[QKV + j], unit_ref.at[j % 2], fetch_sem.at[j % 2])

    def put(j):
        return pltpu.make_async_copy(made_ref.at[j % 2], part_ref.at[QKV + j], made_sem.at[j % 2])

    fetch(0).start()
    sums_ref[...] = jnp.zeros_like(sums_ref)
    grad_normed_ref[...] = jnp.zeros_like(grad_normed_ref)
    for j in range(3):
        for block in range(8):
            part, column = divmod(3 * block + j, 8)
            packed_ref[:, block * LANES : (block + 1) * LANES] = sources[part][
                :, column * LANES : (column + 1) * LANES
            ]
        if j >= 2:
            put(j - 2).wait()

        def weight(index, j=j):
            made = dot_tokens(normed_ref[...], packed_ref[:, tile(index)]).astype(BF16)
            made_ref[j % 2, 2 * index] = made[:, :LANES]
            made_ref[j % 2, 2 * index + 1] = made[:, LANES:]

        loop(4, weight)
        put(j).start()
        fetch(j).wait()
        if j < 2:
            fetch(j + 1).start()

        def back(index, j=j):
            grad_normed_ref[:, tile(index)] += dot_rows(
                packed_ref[...], some_rows(unit_ref.at[j % 2], index)
            )

        loop(4, back)

    def join(window, at, mods, live):
        normal, root = centered(tokens_ref[at, :].astype(F32))
        grad_normed = grad_normed_ref[at, :]
        grad_tokens_ref[at, :] = grad_middle_ref[at, :] + norm_back(
            grad_normed, normal, root, mods[1]
        )
        add_sums(sums_ref, window, 0, grad_normed)
        add_sums(sums_ref, window, 1, grad_normed * normal)

    each_rows(mod_ref, live_ref, join)
    put(1).wait()
    put(2).wait()


def leave(live_frames, tokens, mod, normed, grad_middle, gq, gk, gv, held, part):
    rows = tokens.shape[0]
    unit = (8, D, LANES)
    anywhere = pl.BlockSpec(memory_space=pl.ANY)
    return pl.pallas_call(
        leave_kernel,
        in_specs=[pl.BlockSpec(memory_space=pltpu.SMEM)] + [vmem()] * 7 + [anywhere] * 2,
        out_specs=[vmem(), vmem(), anywhere],
        out_shape=[
            jax.ShapeDtypeStruct((rows, D), F32),
            jax.ShapeDtypeStruct((mod.shape[0], 8, D), F32),
            jax.ShapeDtypeStruct(part.shape, BF16),
        ],
        scratch_shapes=[
            pltpu.VMEM((2, *unit), BF16),
            pltpu.VMEM((rows, D), BF16),
            pltpu.VMEM((rows, D), F32),
            pltpu.VMEM((2, *unit), BF16),
            pltpu.SemaphoreType.DMA((2,)),
            pltpu.SemaphoreType.DMA((2,)),
        ],
        input_output_aliases={9: 2},
        compiler_params=pltpu.CompilerParams(vmem_limit_bytes=56 * MIB),
        name="leave",
    )(live_frames, tokens, mod, normed, grad_middle, gq, gk, gv, held, part)


class Place:
    def __init__(self):
        column, row = lax.axis_index("dp"), lax.axis_index("fsdp")
        self.z, self.x, self.y, self.c = column // 2, column % 2, row // 2, row % 2

    def at(self, z=None, x=None, y=None, c=None):
        z = self.z if z is None else z
        x = self.x if x is None else x
        y = self.y if y is None else y
        c = self.c if c is None else c
        return (z * 2 + x, y * 2 + c)

    def far(self, k):
        return lax.rem(self.z + k, 4)

    def greet(self):
        peers = [self.at(z=self.far(k)) for k in (1, 2, 3)]
        peers += [self.at(x=1 - self.x), self.at(y=1 - self.y), self.at(c=1 - self.c)]
        barrier = pltpu.get_barrier_semaphore()
        for peer in peers:
            pl.semaphore_signal(barrier, inc=1, device_id=peer, device_id_type=MESH)
        pl.semaphore_wait(barrier, len(peers))


class Gather:
    def __init__(self, place, held, send, recv, first):
        self.place, self.held, self.send, self.recv, self.first = place, held, send, recv, first

    def copies(self, unit, stage):
        p, held, index = self.place, self.held, unit - self.first

        def copy(slot, ref, device):
            return pltpu.make_async_remote_copy(
                src_ref=ref,
                dst_ref=ref,
                send_sem=self.send.at[index, slot],
                recv_sem=self.recv.at[index, slot],
                device_id=device,
                device_id_type=MESH,
            )

        if stage == 1:
            own = held.at[unit, p.z, p.x, p.y, p.c]
            return [copy(k - 1, own, p.at(z=p.far(k))) for k in (1, 2, 3)]
        if stage == 2:
            return [
                copy(3, held.at[unit, :, p.x, p.y, p.c, :HALF], p.at(x=1 - p.x)),
                copy(4, held.at[unit, :, p.x, p.y, p.c, HALF:], p.at(y=1 - p.y)),
            ]
        if stage == 3:
            return [
                copy(5, held.at[unit, :, :, p.y, p.c, :HALF], p.at(y=1 - p.y)),
                copy(6, held.at[unit, :, p.x, :, p.c, HALF:], p.at(x=1 - p.x)),
            ]
        return [copy(7, held.at[unit, :, :, :, p.c], p.at(c=1 - p.c))]

    def start(self, unit, stage):
        for copy in self.copies(unit, stage):
            copy.start()

    def arrive(self, unit, stage):
        for copy in self.copies(unit, stage):
            copy.wait_recv()

    def sent(self, unit):
        for stage in (1, 2, 3, 4):
            for copy in self.copies(unit, stage):
                copy.wait_send()


class Reduce:
    def __init__(self, place, part, total, scratch, first):
        self.place, self.part, self.total, self.first = place, part, total, first
        (self.own, self.core, self.side, self.corner, self.distant) = scratch[:5]
        self.send, self.recv, self.load = scratch[5:]

    @staticmethod
    def scratch(count):
        return [
            pltpu.VMEM((2, 4, 2, 2, SHARE, LANES), BF16),
            pltpu.VMEM((count, 4, 2, 2, SHARE, LANES), BF16),
            pltpu.VMEM((count, 2, 4, 2, HALF, LANES), BF16),
            pltpu.VMEM((count, 2, 4, HALF, LANES), BF16),
            pltpu.VMEM((count, 3, 2, HALF, LANES), BF16),
            pltpu.SemaphoreType.DMA((count, 8)),
            pltpu.SemaphoreType.DMA((count, 8)),
            pltpu.SemaphoreType.DMA((2,)),
        ]

    def own_copy(self, unit):
        slot = lax.rem(unit - self.first, 2)
        return pltpu.make_async_copy(
            self.part.at[unit, :, :, :, self.place.c], self.own.at[slot], self.load.at[slot]
        )

    def copies(self, unit, stage):
        p, index = self.place, unit - self.first

        def copy(slot, source, target, device):
            return pltpu.make_async_remote_copy(
                src_ref=source,
                dst_ref=target,
                send_sem=self.send.at[index, slot],
                recv_sem=self.recv.at[index, slot],
                device_id=device,
                device_id_type=MESH,
            )

        core, side, corner = self.core.at[index], self.side.at[index], self.corner.at[index]
        if stage == 1:
            return [copy(0, self.part.at[unit, :, :, :, 1 - p.c], core, p.at(c=1 - p.c))]
        if stage == 2:
            return [
                copy(1, core.at[:, :, 1 - p.y, :HALF], side.at[0], p.at(y=1 - p.y)),
                copy(2, core.at[:, 1 - p.x, :, HALF:], side.at[1], p.at(x=1 - p.x)),
            ]
        if stage == 3:
            return [
                copy(3, side.at[0, :, 1 - p.x], corner.at[0], p.at(x=1 - p.x)),
                copy(4, side.at[1, :, 1 - p.y], corner.at[1], p.at(y=1 - p.y)),
            ]
        return [
            copy(4 + k, corner.at[:, p.far(k)], self.distant.at[index, k - 1], p.at(z=p.far(k)))
            for k in (1, 2, 3)
        ]

    def start(self, unit, stage):
        for copy in self.copies(unit, stage):
            copy.start()
        if stage == 1:
            self.own_copy(unit).start()

    def arrive(self, unit, stage):
        for copy in self.copies(unit, stage):
            copy.wait_recv()
        if stage == 1:
            self.own_copy(unit).wait()

    def sent(self, unit):
        for stage in (1, 2, 3, 4):
            for copy in self.copies(unit, stage):
                copy.wait_send()

    def combine(self, unit, stage):
        p, index = self.place, unit - self.first
        core, side, corner = self.core.at[index], self.side.at[index], self.corner.at[index]

        def plus(left, right):
            return (left.astype(F32) + right.astype(F32)).astype(BF16)

        def from_core(step):
            z, x, y = step // 4, step // 2 % 2, step % 2
            own = self.own[lax.rem(index, 2), z, x, y]
            core[z, x, y] = plus(core[z, x, y], own)

        def from_side(step):
            z, b = step // 2, step % 2
            side[0, z, b] = plus(side[0, z, b], core[z, b, p.y, :HALF])
            side[1, z, b] = plus(side[1, z, b], core[z, p.x, b, HALF:])

        def from_corner(z):
            corner[0, z] = plus(corner[0, z], side[0, z, p.x])
            corner[1, z] = plus(corner[1, z], side[1, z, p.y])

        def from_far(half):
            total = corner[half, p.z].astype(F32)
            for k in range(3):
                total = total + self.distant[index, k, half].astype(F32)
            self.total[index, pl.ds(pl.multiple_of(half * HALF, HALF), HALF), :] = total

        count, body = {1: (16, from_core), 2: (8, from_side), 3: (4, from_corner), 4: (2, from_far)}[
            stage
        ]
        loop(count, body)

    def advance(self, unit, stage):
        self.arrive(unit, stage)
        self.combine(unit, stage)
        if stage < 4:
            self.start(unit, stage + 1)


def gather_kernel(own_ref, held_ref, local, send, recv):
    place = Place()
    place.greet()
    work = Gather(place, held_ref, send, recv, 0)

    def own_copy(unit):
        own = held_ref.at[unit, place.z, place.x, place.y, place.c]
        return pltpu.make_async_copy(own_ref.at[unit], own, local.at[unit])

    loop(UNITS, lambda unit: own_copy(unit).start())
    loop(UNITS, lambda unit: own_copy(unit).wait())
    work.start(0, 1)
    work.start(1, 1)

    def tick(step):
        @pl.when(step + 2 < UNITS)
        def _():
            work.start(step + 2, 1)

        for stage in (1, 2, 3):
            unit = step + 1 - stage

            @pl.when((unit >= 0) & (unit < UNITS))
            def _(unit=unit, stage=stage):
                work.arrive(unit, stage)
                work.start(unit, stage + 1)

    loop(UNITS + 2, tick)

    def finish(unit):
        work.arrive(unit, 4)
        work.sent(unit)

    loop(UNITS, finish)


def gather(own):
    held = pl.pallas_call(
        gather_kernel,
        in_specs=[pl.BlockSpec(memory_space=pl.ANY)],
        out_specs=pl.BlockSpec(memory_space=pl.ANY),
        out_shape=jax.ShapeDtypeStruct((UNITS, 4, 2, 2, 2, SHARE, LANES), BF16),
        scratch_shapes=[
            pltpu.SemaphoreType.DMA((UNITS,)),
            pltpu.SemaphoreType.DMA((UNITS, 8)),
            pltpu.SemaphoreType.DMA((UNITS, 8)),
        ],
        compiler_params=pltpu.CompilerParams(collective_id=0, has_side_effects=True),
        name="gather",
    )(own)
    return held.reshape(UNITS, 8, D, LANES)


def reduce_kernel(part_ref, total_ref, *scratch):
    place = Place()
    place.greet()
    work = Reduce(place, part_ref, total_ref, scratch, 0)
    work.start(0, 1)
    work.start(1, 1)

    def tick(step):
        for stage in (1, 2, 3, 4):
            unit = step + 1 - stage

            @pl.when((unit >= 0) & (unit < UNITS))
            def _(unit=unit, stage=stage):
                work.advance(unit, stage)
                if stage == 1:

                    @pl.when(unit + 2 < UNITS)
                    def _():
                        work.start(unit + 2, 1)

    loop(UNITS + 3, tick)
    loop(UNITS, work.sent)


def reduce(part):
    return pl.pallas_call(
        reduce_kernel,
        in_specs=[pl.BlockSpec(memory_space=pl.ANY)],
        out_specs=vmem(),
        out_shape=jax.ShapeDtypeStruct((UNITS, SHARE, LANES), F32),
        scratch_shapes=Reduce.scratch(UNITS),
        compiler_params=pltpu.CompilerParams(
            collective_id=1, has_side_effects=True, vmem_limit_bytes=48 * MIB
        ),
        name="reduce",
    )(part.reshape(UNITS, 4, 2, 2, 2, SHARE, LANES))


def per_device(
    special,
    tokens,
    condition,
    clip_frames,
    ada_weight,
    ada_bias,
    qkv_weight,
    out_weight,
    up_weight,
    down_weight,
    rel_table,
    cotangent,
):
    window_count = tokens.shape[0]
    clip_count = condition.shape[0]
    rows_ada, cols_ada = ada_weight.shape
    row_block = lax.axis_index("fsdp")
    col_block = lax.axis_index("dp")
    row_count = lax.axis_size("fsdp")
    first_window = lax.axis_index(("dp", "fsdp")) * window_count
    live_frames, member_int = window_layout(clip_frames, first_window, window_count)
    member = member_int.astype(F32)
    activity_low = jax.nn.silu(condition).astype(BF16)
    act_rows = lax.dynamic_slice_in_dim(activity_low, row_block * rows_ada, rows_ada, 1)

    mod_part = jnp.dot(act_rows, ada_weight, preferred_element_type=F32)
    mod_part = mod_part + jnp.where(row_block == 0, ada_bias.astype(F32), 0.0)[None, :]
    mod_size = mod_part.size
    table_size = rel_table.size
    table_part = -(-table_size // row_count)
    table_flat = jnp.pad(
        rel_table.astype(F32).reshape(-1), (0, table_part * row_count - table_size)
    )
    table_own = lax.dynamic_slice_in_dim(table_flat, row_block * table_part, table_part, 0)
    small = lax.all_gather(
        jnp.concatenate([mod_part.reshape(-1), table_own]), ("dp", "fsdp"), axis=0
    )
    small = small.reshape(-1, row_count, mod_size + table_part)
    col_count = small.shape[0]
    clip_mod = jnp.sum(small[:, :, :mod_size], axis=1)
    clip_mod = clip_mod.reshape(col_count, clip_count, cols_ada).transpose(1, 0, 2)
    clip_mod = clip_mod.reshape(clip_count, col_count * cols_ada)
    table_all = small[:, :, mod_size:].reshape(col_count, -1)[:, :table_size]
    table_all = table_all.reshape(-1, REL).astype(BF16)
    window_mod = jnp.sum(member[:, :, None] * clip_mod[None], axis=1)
    window_mod = window_mod.reshape(window_count, 6, D)
    strips = bias_strips(table_all)

    if special:
        held = gather(own_units(qkv_weight, out_weight, up_weight, down_weight))
    else:
        whole = [
            lax.all_gather(
                lax.all_gather(weight, "dp", axis=1, tiled=True), "fsdp", axis=0, tiled=True
            )
            for weight in (qkv_weight, out_weight, up_weight, down_weight)
        ]
        held = units_of(*whole)

    token_rows = tokens.reshape(window_count * WIN, D)
    cotangent_rows = cotangent.reshape(window_count * WIN, D)
    normed, packed = enter(token_rows, window_mod, held)
    mixed, probs = attend(packed, strips, live_frames)
    output, grad_middle, grad_mixed, late_sums, part = middle(
        live_frames, token_rows, cotangent_rows, mixed, window_mod, held
    )
    grad_query, grad_key, grad_value, strip_grad = attend_back(packed, probs, grad_mixed)
    grad_tokens, early_sums, part = leave(
        live_frames,
        token_rows,
        window_mod,
        normed,
        grad_middle,
        grad_query,
        grad_key,
        grad_value,
        held,
        part,
    )
    grad_window_mod = (late_sums + early_sums)[:, :6].reshape(window_count, 6 * D)
    clip_part = lax.dot_general(
        member,
        grad_window_mod,
        (((0,), (0,)), ((), ())),
        precision=HIGHEST,
        preferred_element_type=F32,
    )
    table_part = strips_to_table(strip_grad)
    grad_clip_mod, grad_table_all = lax.psum((clip_part, table_part), ("dp", "fsdp"))
    clip_low = grad_clip_mod.astype(BF16)
    clip_cols = lax.dynamic_slice_in_dim(clip_low, col_block * cols_ada, cols_ada, 1)
    grad_ada_weight = lax.dot_general(
        act_rows, clip_cols, (((0,), (0,)), ((), ())), preferred_element_type=F32
    )
    grad_ada_bias = jnp.sum(clip_cols.astype(F32), axis=0)
    cond_part = lax.dot_general(
        clip_cols, ada_weight, (((1,), (1,)), ((), ())), preferred_element_type=F32
    )
    cond_placed = lax.dynamic_update_slice_in_dim(
        jnp.zeros((clip_count, D), F32), cond_part, row_block * rows_ada, 1
    )
    cond_total = lax.psum(cond_placed, ("dp", "fsdp"))
    _, silu_back = jax.vjp(jax.nn.silu, condition)
    grad_condition = silu_back(cond_total)[0]
    heads_own = rel_table.shape[0]
    grad_table = lax.dynamic_slice_in_dim(grad_table_all, col_block * heads_own, heads_own, 0)

    if special:
        grads = own_blocks(reduce(part))
    else:
        grads = [
            lax.psum_scatter(
                lax.psum_scatter(grad, "fsdp", scatter_dimension=0, tiled=True),
                "dp",
                scatter_dimension=1,
                tiled=True,
            ).astype(F32)
            for grad in weights_of(part)
        ]
    return (
        output.reshape(tokens.shape),
        grad_tokens.reshape(tokens.shape),
        grad_condition,
        grad_ada_weight,
        grad_ada_bias,
        *grads,
        grad_table,
    )


def solution(mesh):
    special = dict(mesh.shape) == {"dp": 8, "fsdp": 4}
    both = P(("dp", "fsdp"), None, None)
    weight = P("fsdp", "dp")
    in_specs = (both, P(), P(), weight, P("dp")) + (weight,) * 4 + (P("dp", None), both)
    out_specs = (both, both, P(), weight, P("dp")) + (weight,) * 4 + (P("dp", None),)
    return jax.shard_map(
        functools.partial(per_device, special),
        mesh=mesh,
        in_specs=in_specs,
        out_specs=out_specs,
        check_vma=False,
    )
```

time: 1920 us -> 791 us (0.41)
  other arithmetic: 590 us -> 8.78 us
  Pallas kernels: 0 us -> 518 us
  local copies, waits for them, and re-layouts: 505 us -> 43.2 us
  waiting for transfers between devices: 455 us -> 118 us
  matrix products: 166 us -> 7.36 us
  blocking collectives: 171 us -> 80.3 us
    scatter-add x1 -> x0, other arithmetic: 544 us -> none  [per_device(): table_part = jnp.zeros((H, REL), jnp.float32).at[:, index_table.reshape(-...]
    pallas_call x0 -> x7, Pallas kernels: none -> 518 us  [the longest x1 151 us: gather(): pl.pallas_call(gather_kernel, in_specs=[pl.BlockSpec(memory_space=pl.ANY)...]
    gather x2 -> x0, local copies, waits for them, and re-layouts: 373 us -> none  [per_device(): rel_bias = table_all.astype(jnp.float32)[:, index_table]]
    unnamed x21 -> x3, waiting for transfers between devices: 199 us -> 0.03 us
    all_gather x9 -> x0, waiting for transfers between devices: 183 us -> none  [the longest x1 63.4 us: per_device(): lax.all_gather(ada_weight, 'dp', axis=1, tiled=True)]
    dot_general x20 -> x3, matrix products: 163 us -> 4.24 us  [the longest x1 2.71 us: strips_to_table(): lax.dot_general(by_frame, pair_onehot().astype(F32), (((1,), (1,)), ((),...]
    psum x1, waiting for transfers between devices: 3.86 us -> 118 us  [per_device(): lax.psum((clip_part, table_part), ('dp', 'fsdp'))]
    all_gather x3 -> x0, blocking collectives: 91.4 us -> none  [the longest x1 30.5 us: per_device(): lax.all_gather(out_weight, 'dp', axis=1, tiled=True)]
  transfers between devices with their start and end apart: 18 -> 2, of which waited for: 9 -> 1; matrix products, arithmetic and copies ran while one was open for 63% -> 2% of each run, Pallas kernels for 0% -> 19%
where the time goes in v1:
time: 791 us; the launch traced here: 790 us
  Pallas kernels  518 us (65%)
  waiting for transfers between devices  118 us (15%)
  blocking collectives  80.3 us (10%)
  local copies, waits for them, and re-layouts  43.2 us (5%)
  between operations  14.6 us (2%)
  other arithmetic  8.78 us (1%)
    pallas_call x1, Pallas kernels, gather(): pl.pallas_call(gather_kernel, in_specs=[pl.BlockSpec(memory_space=pl.ANY)...  151 us
    pallas_call x1, Pallas kernels, reduce(): pl.pallas_call(reduce_kernel, in_specs=[pl.BlockSpec(memory_space=pl.ANY)...  124 us
    psum x1, waiting for transfers between devices, per_device(): lax.psum((clip_part, table_part), ('dp', 'fsdp'))  118 us
    pallas_call x1, Pallas kernels, middle(): pl.pallas_call(middle_kernel, in_specs=[pl.BlockSpec(memory_space=pltpu.S...  85.8 us
    pallas_call x1, Pallas kernels, attend(): pl.pallas_call(attend_kernel, grid_spec=pltpu.PrefetchScalarGridSpec(num_...  60.7 us
    pallas_call x1, Pallas kernels, attend_back(): pl.pallas_call(attend_back_kernel, grid=(pairs, window_count), in_specs=[...  53.5 us
    psum x1, blocking collectives, per_device(): cond_total = lax.psum(cond_placed, ('dp', 'fsdp'))  40.3 us
    psum x1, blocking collectives, per_device(): lax.psum((clip_part, table_part), ('dp', 'fsdp'))  40.1 us
  transfers between devices with their start and end apart: 2, of which 1 were waited for; matrix products, arithmetic and copies ran while one was open for 2% of the time, Pallas kernels for 19%

profile of v1, /device:TPU:0, one launch (start us, length us, event | category | flops | bytes accessed | tf_op | source)
XLA Modules:
  0.0 790.3 jit_solution(7891050694176918944)
XLA Ops:
  7.3 0.8 add_divide_fusion
  8.0 0.7 fusion.26
  8.7 0.7 convert_select_fusion
  9.6 0.8 reshape.187
  10.7 0.7 copy-done.5
  11.7 0.7 fusion.30
  12.5 0.7 bitcast_subtract_fusion
  13.4 0.9 select_reduce_fusion
  14.4 1.1 copy.58
  15.7 1.1 copy.56
  16.9 1.0 copy.60
  17.9 1.0 pad_maximum_fusion.own_ref
  18.8 150.8 %gather.1 = bf16[12,4,2,2,2,256,128]{6,5,4,3,2,1,0:T(8,128)(2,1)} custom-call(bf16[12,256,128]{2,1,0:T(8,128)(2,1)} %pad_maximum_fusion.own_ref), custom_call_target="tpu_custom_call" | custom-call | tf_op jit(solution)/shard_map/gather/pallas_call | solution.py:849
  169.6 0.5 subtract_minimum_fusion.live_ref
  170.2 1.4 reshape.188
  172.7 1.4 convolution_convert_fusion
  174.1 3.5 reshape.198
  177.6 4.4 copy.61
  182.0 3.8 copy.62.strip_ref
  185.8 12.1 %enter.1 = (bf16[640,1024]{1,0:T(8,128)(2,1)S(1)}, bf16[3,640,1024]{2,1,0:T(8,128)(2,1)}) custom-call(bf16[640,1024]{1,0:T(8,128)(2,1)S(1)} %bitcast.64, f32[2,6,1024]{2,1,0:T(8,128)S(1)} %reshape.190.mod_ref, bf16[12,8,1024,128]{3,2,1,0:T(8,128)(2,1)} %bitcast.65), custom_call_target="tpu_custom_call" | custom-call | tf_op jit(solution)/shard_map/enter/pallas_call | solution.py:197
  197.9 1.1 copy-done.2
  199.0 60.7 %attend.1 = (bf16[640,1024]{1,0:T(8,128)(2,1)}, bf16[2,16,320,320]{3,2,1,0:T(8,128)(2,1)}) custom-call(s32[2]{0:T(128)} %subtract_minimum_fusion.live_ref, bf16[3,640,1024]{2,1,0:T(8,128)(2,1)} %get-tuple-element.26.query_ref.key_ref.value_ref, bf16[3,640,1024]{2,1,0:T(8,128)(2,1)} %get-tuple-element.26.query_ref.key_ref.value_ref, ...), custom_call_target="tpu_custom_call" | custom-call | tf_op jit(solution)/shard_map/attend/pallas_call | solution.py:247
  259.7 85.8 %middle.1 = (bf16[640,1024]{1,0:T(8,128)(2,1)}, f32[640,1024]{1,0:T(8,128)}, bf16[640,1024]{1,0:T(8,128)(2,1)}, f32[2,8,1024]{2,1,0:T(8,128)}, bf16[12,8,1024,128]{3,2,1,0:T(8,128)(2,1)}) custom-call(s32[2]{0:T(128)} %subtract_minimum_fusion.live_ref, bf16[640,1024]{1,0:T(8,128)(2,1)} %bitcast.62, bf16[640,1024]{1,0:T(8,128)(2,1)} %bitcast.74, ...), custom_call_target="tpu_custom_call" | custom-call | tf_op jit(solution)/shard_map/middle/pallas_call | solution.py:494
  345.5 53.5 %attend_back.1 = (bf16[640,1024]{1,0:T(8,128)(2,1)}, bf16[640,1024]{1,0:T(8,128)(2,1)}, bf16[640,1024]{1,0:T(8,128)(2,1)}, f32[16,64,576]{2,1,0:T(8,128)}) custom-call(bf16[3,640,1024]{2,1,0:T(8,128)(2,1)} %get-tuple-element.26.query_ref.key_ref.value_ref, bf16[3,640,1024]{2,1,0:T(8,128)(2,1)} %get-tuple-element.26.query_ref.key_ref.value_ref, ...), custom_call_target="tpu_custom_call" | custom-call | tf_op jit(solution)/shard_map/attend_back/pallas_call | solution.py:310
  399.0 31.7 %leave.1 = (f32[640,1024]{1,0:T(8,128)}, f32[2,8,1024]{2,1,0:T(8,128)}, bf16[12,8,1024,128]{3,2,1,0:T(8,128)(2,1)}) custom-call(s32[2]{0:T(128)} %subtract_minimum_fusion.live_ref, bf16[640,1024]{1,0:T(8,128)(2,1)} %bitcast.63, f32[2,6,1024]{2,1,0:T(8,128)} %copy-done.3, bf16[640,1024]{1,0:T(8,128)(2,1)} %copy-done.2, ...), custom_call_target="tpu_custom_call", output_to_operand_aliasing={{2}: (9, {})} | custom-call | tf_op jit(solution)/shard_map/leave/pallas_call | solution.py:607
  430.7 123.8 %reduce.1 = f32[12,256,128]{2,1,0:T(8,128)S(1)} custom-call(bf16[12,4,2,2,2,256,128]{6,5,4,3,2,1,0:T(8,128)(2,1)} %bitcast.68), custom_call_target="tpu_custom_call" | custom-call | tf_op jit(solution)/shard_map/reduce/pallas_call | solution.py:890
  554.6 0.9 fusion.34
  555.4 0.8 slice_bitcast_fusion.1
  556.2 0.7 slice_bitcast_fusion.2
  556.9 1.1 fusion.31
  558.0 40.1 %psum.21 = bf16[3,6144]{1,0:T(4,128)(2,1)} all-reduce(f32[3,6144]{1,0:T(4,128)} %fusion.31), channel_id=1, replica_groups=mesh['dp'=8,'fsdp'=4] {'dp','fsdp'}, use_global_device_ids=true, to_apply=%region_6.7 | all-reduce | flops 18432 | bytes 110592 | tf_op jit(solution)/shard_map/psum | solution.py:992
  598.1 1.3 convert_reduce_fusion
  599.4 1.2 fusion.35
  600.6 0.6 broadcast_in_dim.6
  601.2 0.8 convolution_dynamic-update-slice_fusion
  602.0 40.3 %psum.22 = f32[3,1024]{1,0:T(4,128)S(1)} all-reduce(f32[3,1024]{1,0:T(4,128)} %convolution_dynamic-update-slice_fusion), channel_id=1, replica_groups=mesh['dp'=8,'fsdp'=4] {'dp','fsdp'}, use_global_device_ids=true, to_apply=%region_7.8 | all-reduce | flops 3072 | bytes 24576 | tf_op jit(solution)/shard_map/psum | solution.py:1005
  642.3 3.6 copy.66
  645.9 6.1 copy.67
  652.0 3.9 dot_general.25
  656.0 2.7 fusion.15
  658.8 0.8 reshape.209
  659.7 0.6 fusion.24
  660.3 1.2 copy.64
  661.5 1.0 copy.70
  662.5 0.8 copy.65
  663.5 0.9 copy.69
  664.5 117.6 %all-reduce.5.cloned.1.call-done = f32[16,2025]{1,0:T(8,128)} async-done(((f32[16,2025]{1,0:T(8,128)}), f32[16,2025]{1,0:T(8,128)}) %all-reduce.5.cloned.1.call-update) | async-done | bytes 129616 | tf_op jit(solution)/shard_map/psum | solution.py:992
  782.0 1.5 constant_dynamic-slice_fusion
  (79 shorter events, 2.9 us)
Async XLA Ops:
  7.2 2.3 copy-start
  7.2 10.7 %copy-start.8 = (bf16[256,128]{1,0:T(8,128)(2,1)S(1)}, bf16[256,128]{1,0:T(8,128)(2,1)}, u32[]{:S(2)}) copy-start(bf16[256,128]{1,0:T(8,128)(2,1)} %param.17) | copy-start | bytes 196612
  7.2 163.0 %all-reduce.7.cloned.1.call-start = ((), (), s32[]{:S(2)}) async-start(), calls=%async_computation.1 | async-start | bytes 851968
  10.7 0.8 copy-start.5
  11.5 770.5 %all-reduce.5.cloned.1.call-start = ((), (), s32[]{:S(2)}) async-start(), calls=%async_computation | async-start | bytes 262144 | tf_op jit(solution)/shard_map/psum | solution.py:992
  11.5 161.1 %copy-start.11 = (s32[4096]{0:T(1024)}, s32[4096]{0:T(1024)S(1)}, u32[]{:S(2)}) copy-start(s32[4096]{0:T(1024)S(1)} %get-tuple-element.78) | copy-start | bytes 49156
  11.6 161.1 %copy-start.13 = (s32[4096]{0:T(1024)}, s32[4096]{0:T(1024)S(1)}, u32[]{:S(2)}) copy-start(s32[4096]{0:T(1024)S(1)} %get-tuple-element.79) | copy-start | bytes 49156
  11.6 161.1 %copy-start.15 = (s32[4096]{0:T(1024)}, s32[4096]{0:T(1024)S(1)}, u32[]{:S(2)}) copy-start(s32[4096]{0:T(1024)S(1)} %get-tuple-element.80) | copy-start | bytes 49156
  11.6 161.1 %copy-start.17 = (s32[4096]{0:T(1024)}, s32[4096]{0:T(1024)S(1)}, u32[]{:S(2)}) copy-start(s32[4096]{0:T(1024)S(1)} %get-tuple-element.81) | copy-start | bytes 49156
  11.6 161.1 %copy-start.19 = (pred[4096]{0:T(1024)(128)(4,1)}, pred[4096]{0:T(1024)(128)(4,1)S(1)}, u32[]{:S(2)}) copy-start(pred[4096]{0:T(1024)(128)(4,1)S(1)} %get-tuple-element.82) | copy-start | bytes 12292
  11.6 161.1 %copy-start.21 = (pred[4096]{0:T(1024)(128)(4,1)}, pred[4096]{0:T(1024)(128)(4,1)S(1)}, u32[]{:S(2)}) copy-start(pred[4096]{0:T(1024)(128)(4,1)S(1)} %get-tuple-element.83) | copy-start | bytes 12292
  172.0 13.8 %copy-start.3 = (f32[2,6,1024]{2,1,0:T(8,128)}, f32[2,6,1024]{2,1,0:T(8,128)S(1)}, u32[]{:S(2)}) copy-start(f32[2,6,1024]{2,1,0:T(8,128)S(1)} %reshape.190.mod_ref) | copy-start | bytes 147460
  177.6 8.3 %copy-start.1 = (bf16[2,320,1024]{2,1,0:T(8,128)(2,1)S(1)}, bf16[2,320,1024]{2,1,0:T(8,128)(2,1)}, u32[]{:S(2)}) copy-start(bf16[2,320,1024]{2,1,0:T(8,128)(2,1)} %param.11) | copy-start | bytes 3932164
  197.9 1.1 copy-start.2
  430.7 126.2 %copy-start.9 = (f32[2,8,1024]{2,1,0:T(8,128)S(1)}, f32[2,8,1024]{2,1,0:T(8,128)}, u32[]{:S(2)}) copy-start(f32[2,8,1024]{2,1,0:T(8,128)} %get-tuple-element.38) | copy-start | bytes 196612
  430.7 126.2 %copy-start.10 = (f32[2,8,1024]{2,1,0:T(8,128)S(1)}, f32[2,8,1024]{2,1,0:T(8,128)}, u32[]{:S(2)}) copy-start(f32[2,8,1024]{2,1,0:T(8,128)} %get-tuple-element.39) | copy-start | bytes 196612
  554.6 87.7 %copy-start.4 = (f32[16,64,576]{2,1,0:T(8,128)S(1)}, f32[16,64,576]{2,1,0:T(8,128)}, u32[]{:S(2)}) copy-start(f32[16,64,576]{2,1,0:T(8,128)} %get-tuple-element.41) | copy-start | bytes 7077892
  652.0 3.9 copy-start.12
  652.0 3.9 copy-start.14
  652.0 3.9 copy-start.16
  652.0 3.9 copy-start.18
  652.0 3.9 copy-start.20
  652.0 3.9 copy-start.22
  656.0 3.7 copy-start.7
  658.7 4.7 copy-start.6
Sparse Core Ops, SparseCore 0:
  13.9 131.1 all-reduce.6
  659.8 122.2 all-reduce.4

commit v2 on v0

v2 whole, which is shorter than its diff:
```python
import functools

import jax
import jax.numpy as jnp
from jax import lax
from jax.experimental import pallas as pl
from jax.experimental.pallas import tpu as pltpu
from jax.sharding import PartitionSpec as P

D = 1024
H = 16
HD = 64
WT = 5
WSIDE = 8
WIN = 320
SPW = 16
CELLS = WSIDE * WSIDE
FRAMES = 2 * WT - 1
OFFSETS = (2 * WSIDE - 1) ** 2
REL = FRAMES * OFFSETS
LANES = 128
TILE = 256
SPREAD = 80
STRIP = 640

EPSILON = 1e-06
NEGATIVE = -1000000000.0
HIGHEST = lax.Precision.HIGHEST
F32 = jnp.float32
BF16 = jnp.bfloat16
MESH = pl.DeviceIdType.MESH
MIB = 2**20

QKV, OUT, UP, DOWN, UNITS = 0, 3, 4, 8, 12
SHARE = 256
HALF = 128


def window_layout(clip_frames, first_window, window_count):
    slab_count = 1 + (clip_frames > WT).astype(jnp.int32)
    starts = jnp.cumsum(slab_count, dtype=jnp.int32) - slab_count
    global_window = first_window + jnp.arange(window_count, dtype=jnp.int32)
    slab_of = global_window // SPW
    owners = jnp.sum((starts[None, :] <= slab_of[:, None]).astype(jnp.int32), axis=1) - 1
    clip_ids = jnp.arange(clip_frames.shape[0], dtype=jnp.int32)
    member = (owners[:, None] == clip_ids[None, :]).astype(jnp.int32)
    clip_start = jnp.sum(member * starts[None, :], axis=1)
    own_frames = jnp.sum(member * clip_frames[None, :], axis=1)
    inner_slab = slab_of - clip_start
    return (jnp.minimum(own_frames - WT * inner_slab, WT), member)


def offset_spread():
    side_span = 2 * WSIDE - 1
    shape = (OFFSETS, WSIDE * LANES)
    offset = lax.broadcasted_iota(jnp.int32, shape, 0)
    place = lax.broadcasted_iota(jnp.int32, shape, 1)
    own, row, other = place // LANES, place // WSIDE % (LANES // WSIDE), place % WSIDE
    row_diff, col_diff = side_span - 1 - row, own - other + (WSIDE - 1)
    return ((row < side_span) & (row_diff * side_span + col_diff == offset)).astype(BF16)


def spread_table(table):
    heads = table.shape[0]
    by_frame = table.reshape(heads, FRAMES, OFFSETS)[:, ::-1].reshape(heads * FRAMES, OFFSETS)
    spread = jnp.dot(by_frame, offset_spread(), preferred_element_type=F32).astype(BF16)
    spread = spread.reshape(heads, FRAMES * WSIDE, LANES)
    return jnp.pad(spread, ((0, 0), (0, SPREAD - FRAMES * WSIDE), (0, 0)))


def gather_table(spread):
    heads = spread.shape[0]
    by_frame = spread[:, : FRAMES * WSIDE].reshape(heads * FRAMES, WSIDE * LANES)
    sums = lax.dot_general(
        by_frame,
        offset_spread().astype(F32),
        (((1,), (1,)), ((), ())),
        precision=HIGHEST,
        preferred_element_type=F32,
    )
    return sums.reshape(heads, FRAMES, OFFSETS)[:, ::-1].reshape(heads, FRAMES * OFFSETS)


def units_of(qkv, out, up, down):
    return jnp.concatenate(
        [
            qkv.reshape(D, 8, 3, LANES).transpose(2, 1, 0, 3),
            out.reshape(D, 8, 1, LANES).transpose(2, 1, 0, 3),
            up.reshape(D, 8, 4, LANES).transpose(2, 1, 0, 3),
            down.reshape(8, 4, LANES, 8, LANES).transpose(1, 3, 0, 2, 4).reshape(4, 8, D, LANES),
        ]
    )


def weights_of(units):
    def columns(part):
        return part.transpose(2, 1, 0, 3).reshape(D, -1)

    down = units[DOWN:].reshape(4, 8, 8, LANES, LANES).transpose(2, 0, 3, 1, 4)
    return (
        columns(units[QKV:OUT]),
        columns(units[OUT:UP]),
        columns(units[UP:DOWN]),
        down.reshape(4 * D, D),
    )


def own_blocks(shares):
    def columns(part):
        return part.transpose(1, 0, 2).reshape(SHARE, -1)

    down = shares[DOWN:].reshape(4, 2, LANES, LANES).transpose(1, 0, 2, 3).reshape(4 * SHARE, LANES)
    return (columns(shares[QKV:OUT]), columns(shares[OUT:UP]), columns(shares[UP:DOWN]), down)


def dot(left, right):
    return jnp.dot(left, right, preferred_element_type=F32)


def dot_rows(left, right):
    return lax.dot_general(left, right, (((1,), (1,)), ((), ())), preferred_element_type=F32)


def dot_tokens(left, right):
    return lax.dot_general(left, right, (((0,), (0,)), ((), ())), preferred_element_type=F32)


def tile(index):
    return pl.ds(pl.multiple_of(index * TILE, TILE), TILE)


def two_columns(unit, index):
    return jnp.concatenate([unit[index, x].reshape(D, LANES) for x in range(2)], axis=1)


def put_columns(unit, index, values):
    for x in range(2):
        unit[index, x] = values[:, x * LANES : (x + 1) * LANES].reshape(2, 2, SHARE, LANES)


def some_rows(unit, index):
    row, core = index // 2, index % 2
    blocks = [unit[block // 2, block % 2, row, core] for block in range(8)]
    return jnp.concatenate(blocks, axis=1)


def loop(count, body):
    def step(index, carry):
        body(index)
        return carry

    lax.fori_loop(0, count, step, 0)


def vmem():
    return pl.BlockSpec(memory_space=pltpu.VMEM)


def anywhere():
    return pl.BlockSpec(memory_space=pl.ANY)


def smem():
    return pl.BlockSpec(memory_space=pltpu.SMEM)


def shape(dtype, *sizes):
    return jax.ShapeDtypeStruct(sizes, dtype)


def params(collective=None, limit=58):
    if collective is None:
        return pltpu.CompilerParams(vmem_limit_bytes=limit * MIB)
    return pltpu.CompilerParams(
        vmem_limit_bytes=limit * MIB, collective_id=collective, has_side_effects=True
    )


def centered(values):
    center = values - jnp.mean(values, axis=-1, keepdims=True)
    spread = jnp.mean(center * center, axis=-1, keepdims=True)
    root = lax.rsqrt(spread + EPSILON)
    return center * root, root


def norm_back(grad_normed, normal, root, scale):
    grad = grad_normed * (1.0 + scale)
    mean = jnp.mean(grad, axis=-1, keepdims=True)
    along = jnp.mean(grad * normal, axis=-1, keepdims=True)
    return root * (grad - mean - normal * along)


def each_rows(mod_ref, live_ref, body, rows=16):
    for window in range(mod_ref.shape[0]):
        live = live_ref[window] * CELLS

        def step(index, window=window, live=live):
            at = pl.ds(pl.multiple_of(window * WIN + index * rows, rows), rows)
            mods = [mod_ref[window, k : k + 1, :] for k in range(6)]
            slot = index * rows + lax.broadcasted_iota(jnp.int32, (rows, 1), 0)
            body(window, at, mods, slot < live)

        loop(WIN // rows, step)


def add_sums(sums_ref, window, which, values):
    sums_ref[window, which : which + 1, :] += jnp.sum(values, axis=0, keepdims=True)


class Place:
    def __init__(self):
        column, row = lax.axis_index("dp"), lax.axis_index("fsdp")
        self.z, self.x, self.y, self.c = column // 2, column % 2, row // 2, row % 2

    def at(self, z=None, x=None, y=None, c=None):
        z = self.z if z is None else z
        x = self.x if x is None else x
        y = self.y if y is None else y
        c = self.c if c is None else c
        return (z * 2 + x, y * 2 + c)

    def far(self, k):
        return lax.rem(self.z + k, 4)

    def greet(self):
        peers = [self.at(z=self.far(k)) for k in (1, 2, 3)]
        peers += [self.at(x=1 - self.x), self.at(y=1 - self.y), self.at(c=1 - self.c)]
        barrier = pltpu.get_barrier_semaphore()
        for peer in peers:
            pl.semaphore_signal(barrier, inc=1, device_id=peer, device_id_type=MESH)
        pl.semaphore_wait(barrier, len(peers))


class Gather:
    def __init__(self, place, held, units, scratch):
        self.place, self.held, self.units = place, held, units
        self.send, self.recv = scratch

    @staticmethod
    def scratch(count):
        return [pltpu.SemaphoreType.DMA((count, 8))] * 2

    def copies(self, index, stage):
        p, held = self.place, self.held.at[self.units[index]]

        def copy(slot, ref, device):
            return pltpu.make_async_remote_copy(
                src_ref=ref,
                dst_ref=ref,
                send_sem=self.send.at[index, slot],
                recv_sem=self.recv.at[index, slot],
                device_id=device,
                device_id_type=MESH,
            )

        if stage == 1:
            return [copy(k - 1, held.at[p.z, p.x, p.y, p.c], p.at(z=p.far(k))) for k in (1, 2, 3)]
        if stage == 2:
            return [
                copy(3, held.at[:, p.x, p.y, p.c, :HALF], p.at(x=1 - p.x)),
                copy(4, held.at[:, p.x, p.y, p.c, HALF:], p.at(y=1 - p.y)),
            ]
        if stage == 3:
            return [
                copy(5, held.at[:, :, p.y, p.c, :HALF], p.at(y=1 - p.y)),
                copy(6, held.at[:, p.x, :, p.c, HALF:], p.at(x=1 - p.x)),
            ]
        return [copy(7, held.at[:, :, :, p.c], p.at(c=1 - p.c))]

    def start(self, index, stage):
        for copy in self.copies(index, stage):
            copy.start()

    def arrive(self, index, stage):
        for copy in self.copies(index, stage):
            copy.wait_recv()

    def sent(self):
        for index in range(len(self.units)):
            for stage in (1, 2, 3, 4):
                for copy in self.copies(index, stage):
                    copy.wait_send()

    def actions(self):
        count = len(self.units)

        def begin():
            for index in range(min(2, count)):
                self.start(index, 1)

        def tick(step):
            if step + 2 < count:
                self.start(step + 2, 1)
            for stage in (1, 2, 3):
                index = step + 1 - stage
                if 0 <= index < count:
                    self.arrive(index, stage)
                    self.start(index, stage + 1)

        return [begin] + [functools.partial(tick, step) for step in range(count + 2)]


class Reduce:
    def __init__(self, place, part, total, units, scratch):
        self.place, self.part, self.total, self.units = place, part, total, units
        self.own, self.core, self.side, self.corner, self.distant = scratch[:5]
        self.send, self.recv, self.load = scratch[5:]

    @staticmethod
    def scratch(count):
        return [
            pltpu.VMEM((2, 4, 2, 2, SHARE, LANES), BF16),
            pltpu.VMEM((count, 4, 2, 2, SHARE, LANES), BF16),
            pltpu.VMEM((count, 2, 4, 2, HALF, LANES), BF16),
            pltpu.VMEM((count, 2, 4, HALF, LANES), BF16),
            pltpu.VMEM((count, 3, 2, HALF, LANES), BF16),
            pltpu.SemaphoreType.DMA((count, 8)),
            pltpu.SemaphoreType.DMA((count, 8)),
            pltpu.SemaphoreType.DMA((2,)),
        ]

    def own_copy(self, index):
        slot = index % 2
        return pltpu.make_async_copy(
            self.part.at[self.units[index], :, :, :, self.place.c],
            self.own.at[slot],
            self.load.at[slot],
        )

    def copies(self, index, stage):
        p, part = self.place, self.part.at[self.units[index]]

        def copy(slot, source, target, device):
            return pltpu.make_async_remote_copy(
                src_ref=source,
                dst_ref=target,
                send_sem=self.send.at[index, slot],
                recv_sem=self.recv.at[index, slot],
                device_id=device,
                device_id_type=MESH,
            )

        core, side, corner = self.core.at[index], self.side.at[index], self.corner.at[index]
        if stage == 1:
            return [copy(0, part.at[:, :, :, 1 - p.c], core, p.at(c=1 - p.c))]
        if stage == 2:
            return [
                copy(1, core.at[:, :, 1 - p.y, :HALF], side.at[0], p.at(y=1 - p.y)),
                copy(2, core.at[:, 1 - p.x, :, HALF:], side.at[1], p.at(x=1 - p.x)),
            ]
        if stage == 3:
            return [
                copy(3, side.at[0, :, 1 - p.x], corner.at[0], p.at(x=1 - p.x)),
                copy(4, side.at[1, :, 1 - p.y], corner.at[1], p.at(y=1 - p.y)),
            ]
        return [
            copy(4 + k, corner.at[:, p.far(k)], self.distant.at[index, k - 1], p.at(z=p.far(k)))
            for k in (1, 2, 3)
        ]

    def start(self, index, stage):
        for copy in self.copies(index, stage):
            copy.start()
        if stage == 1:
            self.own_copy(index).start()

    def sent(self):
        for index in range(len(self.units)):
            for stage in (1, 2, 3, 4):
                for copy in self.copies(index, stage):
                    copy.wait_send()

    def combine(self, index, stage):
        p = self.place
        core, side, corner = self.core.at[index], self.side.at[index], self.corner.at[index]

        def plus(left, right):
            return (left.astype(F32) + right.astype(F32)).astype(BF16)

        def from_core(step):
            z, x, y = step // 4, step // 2 % 2, step % 2
            core[z, x, y] = plus(core[z, x, y], self.own[index % 2, z, x, y])

        def from_side(step):
            z, b = step // 2, step % 2
            side[0, z, b] = plus(side[0, z, b], core[z, b, p.y, :HALF])
            side[1, z, b] = plus(side[1, z, b], core[z, p.x, b, HALF:])

        def from_corner(z):
            corner[0, z] = plus(corner[0, z], side[0, z, p.x])
            corner[1, z] = plus(corner[1, z], side[1, z, p.y])

        def from_far(half):
            total = corner[half, p.z].astype(F32)
            for k in range(3):
                total = total + self.distant[index, k, half].astype(F32)
            self.total[index, pl.ds(pl.multiple_of(half * HALF, HALF), HALF), :] = total

        steps = {1: (16, from_core), 2: (8, from_side), 3: (4, from_corner), 4: (2, from_far)}
        loop(*steps[stage])

    def advance(self, index, stage):
        for copy in self.copies(index, stage):
            copy.wait_recv()
        if stage == 1:
            self.own_copy(index).wait()
        self.combine(index, stage)
        if stage < 4:
            self.start(index, stage + 1)

    def actions(self):
        count = len(self.units)

        def begin():
            for index in range(min(2, count)):
                self.start(index, 1)

        def tick(step):
            for stage in (1, 2, 3, 4):
                index = step + 1 - stage
                if 0 <= index < count:
                    self.advance(index, stage)
                    if stage == 1 and index + 2 < count:
                        self.start(index + 2, 1)

        return [begin] + [functools.partial(tick, step) for step in range(count + 3)]


class Small:
    def __init__(self, place, values, scratch):
        self.place, self.values = place, values
        self.from_core, self.from_x, self.from_y, self.from_z, self.send, self.recv = scratch

    @staticmethod
    def scratch(rows):
        return [
            pltpu.VMEM((4, 2, rows, LANES), F32),
            pltpu.VMEM((4, rows, LANES), F32),
            pltpu.VMEM((4, rows, LANES), F32),
            pltpu.VMEM((3, rows, LANES), F32),
            pltpu.SemaphoreType.DMA((6,)),
            pltpu.SemaphoreType.DMA((6,)),
        ]

    def copies(self, stage):
        p, values = self.place, self.values

        def copy(slot, source, target, device):
            return pltpu.make_async_remote_copy(
                src_ref=source,
                dst_ref=target,
                send_sem=self.send.at[slot],
                recv_sem=self.recv.at[slot],
                device_id=device,
                device_id_type=MESH,
            )

        if stage == 1:
            return [copy(0, values, self.from_core, p.at(c=1 - p.c))]
        if stage == 2:
            return [copy(1, values.at[:, 1 - p.x], self.from_x, p.at(x=1 - p.x))]
        if stage == 3:
            return [copy(2, values.at[:, p.x], self.from_y, p.at(y=1 - p.y))]
        return [
            copy(2 + k, values.at[p.far(k), p.x], self.from_z.at[k - 1], p.at(z=p.far(k)))
            for k in (1, 2, 3)
        ]

    def start(self, stage):
        for copy in self.copies(stage):
            copy.start()

    def advance(self, stage):
        p, values = self.place, self.values
        for copy in self.copies(stage):
            copy.wait()
        if stage == 1:
            values[...] += self.from_core[...]
        elif stage == 2:
            values[:, p.x] += self.from_x[...]
        elif stage == 3:
            values[:, p.x] += self.from_y[...]
        else:
            return values[p.z, p.x] + self.from_z[0] + self.from_z[1] + self.from_z[2]
        self.start(stage + 1)
        return None


class Copies:
    def __init__(self, send, recv):
        self.send, self.recv, self.count = send, recv, 0

    def __call__(self, source, target, device):
        slot = self.count
        self.count += 1
        copy = pltpu.make_async_remote_copy(
            src_ref=source,
            dst_ref=target,
            send_sem=self.send.at[slot],
            recv_sem=self.recv.at[slot],
            device_id=device,
            device_id_type=MESH,
        )
        copy.start()
        return copy


def spread_actions(plan, points):
    spread = [[] for _ in range(points)]
    for index, action in enumerate(plan):
        spread[min(points - 1, index * points // len(plan))].append(action)
    return spread


class Refs:
    pass


def call(kernel, name, inputs, outputs, scratch, aliases=(), collective=None, grid=None, limit=58):
    names = list(inputs) + list(outputs)
    flat = []
    for value in scratch.values():
        flat += value if isinstance(value, list) else [value]

    def body(*refs):
        held = Refs()
        rest = list(refs)
        for key in names:
            setattr(held, key, rest.pop(0))
        for key, value in scratch.items():
            if isinstance(value, list):
                setattr(held, key, [rest.pop(0) for _ in value])
            else:
                setattr(held, key, rest.pop(0))
        kernel(held)

    extra = {} if grid is None else {"grid": grid}
    result = pl.pallas_call(
        body,
        in_specs=[spec for _, spec in inputs.values()],
        out_specs=[spec for _, spec in outputs.values()],
        out_shape=[out for out, _ in outputs.values()],
        scratch_shapes=flat,
        input_output_aliases={
            list(inputs).index(one): list(outputs).index(other) for one, other in aliases
        },
        compiler_params=params(collective, limit),
        name=name,
        **extra,
    )(*[array for array, _ in inputs.values()])
    out = Refs()
    for key, value in zip(outputs, result, strict=True):
        setattr(out, key, value)
    return out


SPLIT = (4, 2, 2, 2, SHARE, LANES)
MOD_ROWS = 48
FIRST = (QKV, QKV + 1, QKV + 2)
SECOND = (OUT, UP, DOWN, UP + 1, DOWN + 1, UP + 2, DOWN + 2)
THIRD = (UP + 3, DOWN + 3)
EARLY = (DOWN, UP, DOWN + 1, UP + 1, DOWN + 2)
LATE = (UP + 2, DOWN + 3, UP + 3, OUT)


def enter_norm(refs):
    rows = 32
    for window in range(refs.mod.shape[0]):
        shift, scale = refs.mod[window, 0:1, :], refs.mod[window, 1:2, :]

        def step(index, window=window, shift=shift, scale=scale):
            at = pl.ds(pl.multiple_of(window * WIN + index * rows, rows), rows)
            normal, _ = centered(refs.tokens[at, :].astype(F32))
            refs.normed[at, :] = (normal * (1.0 + scale) + shift).astype(BF16)

        loop(WIN // rows, step)


def enter_unit(refs, j, held):
    fetch = pltpu.make_async_copy(held, refs.unit, refs.fetch)
    fetch.start()
    fetch.wait()

    def project(index):
        refs.packed[j, :, tile(index)] = dot(
            refs.normed[...], two_columns(refs.unit, index)
        ).astype(BF16)

    loop(4, project)


def enter_plain_kernel(refs):
    enter_norm(refs)
    for j in range(3):
        enter_unit(refs, j, refs.held.at[QKV + j])


def enter_kernel(refs):
    place = Place()
    place.greet()
    z, x, y, c = place.z, place.x, place.y, place.c

    own = []
    blocks = [(refs.qkv, j) for j in range(3)] + [(refs.out, 0)] + [(refs.up, j) for j in range(4)]
    for unit, (source, j) in enumerate(blocks):
        own.append((source.at[:, j * LANES : (j + 1) * LANES], refs.held.at[unit, z, x, y, c]))
    for j in range(4):
        for half in range(2):
            first = half * 512 + j * LANES
            own.append(
                (
                    refs.down.at[first : first + LANES],
                    refs.held.at[DOWN + j, z, x, y, c, half * HALF : (half + 1) * HALF],
                )
            )
    own = [
        pltpu.make_async_copy(source, target, refs.own_sem.at[index])
        for index, (source, target) in enumerate(own)
    ]
    for copy in own:
        copy.start()
    work = Gather(place, refs.held, FIRST, refs.gather)
    ticks = work.actions()
    small = Copies(*refs.small)
    copy = small(refs.mod_part, refs.from_core, place.at(c=1 - c))
    refs.table[z, x, c] = refs.table_own[c]
    for one in own:
        one.wait()
    ticks[0]()
    copy.wait()
    refs.mod_sum[...] = refs.mod_part[...] + refs.from_core[...]
    copy = small(refs.mod_sum, refs.from_y, place.at(y=1 - y))
    ticks[1]()
    copy.wait()
    refs.mods[z, x] = refs.mod_sum[...] + refs.from_y[...]
    copies = [
        small(refs.mods.at[z, x], refs.mods.at[z, x], place.at(x=1 - x)),
        small(refs.table.at[z, x, c], refs.table.at[z, x, c], place.at(x=1 - x)),
    ]
    for copy in copies:
        copy.wait()
    mods = [
        small(refs.mods.at[z], refs.mods.at[z], place.at(z=place.far(k))) for k in (1, 2, 3)
    ]
    tables = [
        small(refs.table.at[z, :, c], refs.table.at[z, :, c], place.at(z=place.far(k)))
        for k in (1, 2, 3)
    ]
    ticks[2]()
    for copy in mods:
        copy.wait()
    for window in range(refs.mod.shape[0]):
        for block in range(48):
            which, column = divmod(block, 8)
            part = refs.mods[block // 12, block // 6 % 2, block % 6 * 8 : block % 6 * 8 + 8, :]
            refs.mod[window, which : which + 1, column * LANES : (column + 1) * LANES] = jnp.sum(
                part * refs.member[window], axis=0, keepdims=True
            )
    enter_norm(refs)
    ticks[3]()
    for copy in tables:
        copy.wait()
    last = small(refs.table.at[:, :, c], refs.table.at[:, :, c], place.at(c=1 - c))
    for j in range(3):
        if j > 0:
            ticks[3 + j]()
        work.arrive(j, 4)
        enter_unit(refs, j, refs.held.at[QKV + j])
    last.wait()
    work.sent()


def attend_kernel(refs):
    work = None
    step = pl.program_id(0) * 2 + pl.program_id(1)
    if hasattr(refs, "gather"):
        place = Place()
        work = Gather(place, refs.held, SECOND, refs.gather)
        steps = spread_actions(work.actions(), 16)
        steps[0].insert(0, place.greet)
        for index, actions in enumerate(steps):
            if actions:

                @pl.when(step == index)
                def _(actions=actions):
                    for action in actions:
                        action()

    @pl.when(pl.program_id(1) == 0)
    def _():
        for head in range(2):
            spread = refs.table[head].astype(F32)
            for frame in range(FRAMES):
                block = spread[frame * WSIDE : (frame + 1) * WSIDE]
                for row in range(WSIDE):
                    first = (WSIDE - 1 - row) * WSIDE
                    refs.strip[
                        head, row * WSIDE : (row + 1) * WSIDE, frame * CELLS : (frame + 1) * CELLS
                    ] = block[:, first : first + CELLS]

    live = refs.live[pl.program_id(1)] * CELLS
    key_live = lax.broadcasted_iota(jnp.int32, (1, WIN), 1) < live
    for head in range(2):
        lanes = slice(head * HD, (head + 1) * HD)
        query = refs.query[:, lanes] * BF16(HD ** (-0.5))
        keys = refs.key[:, lanes]
        values = refs.value[:, lanes]
        for frame in range(WT):
            rows = slice(frame * CELLS, (frame + 1) * CELLS)
            first = (WT - 1 - frame) * CELLS
            scores = dot_rows(query[rows], keys) + refs.strip[head, :, first : first + WIN]
            scores = jnp.where(key_live, scores, NEGATIVE)
            shifted = jnp.exp(scores - jnp.max(scores, axis=-1, keepdims=True))
            totals = jnp.sum(shifted, axis=-1, keepdims=True)
            probs = (shifted * (1.0 / totals)).astype(BF16)
            refs.probs[head, rows] = probs
            refs.mixed[rows, lanes] = dot(probs, values).astype(BF16)

    if work is not None:

        @pl.when(step == 15)
        def _():
            for index in range(len(SECOND)):
                work.arrive(index, 4)
            work.sent()


def packed_block(part):
    pairs = H // 2
    return pl.BlockSpec(
        (None, WIN, LANES),
        lambda pair, window: (
            lax.rem(part * pairs + pair, 3),
            window,
            lax.div(part * pairs + pair, 3),
        ),
    )


def attend_back_kernel(refs):
    work = None
    step = pl.program_id(0) * 2 + pl.program_id(1)
    if hasattr(refs, "reduce"):
        place = Place()
        work = Reduce(place, refs.part, refs.total, LATE, refs.reduce)
        steps = spread_actions(work.actions(), 15)
        steps[0].insert(0, place.greet)
        for index, actions in enumerate(steps):
            if actions:

                @pl.when(step == index)
                def _(actions=actions):
                    for action in actions:
                        action()

    @pl.when(pl.program_id(1) == 0)
    def _():
        refs.strip[...] = jnp.zeros_like(refs.strip)

    for head in range(2):
        lanes = slice(head * HD, (head + 1) * HD)
        scale = BF16(HD ** (-0.5))
        query = refs.query[:, lanes] * scale
        keys = refs.key[:, lanes] * scale
        values = refs.value[:, lanes]
        grad = refs.grad[:, lanes]
        probs = refs.probs[head]
        refs.gv[:, lanes] = dot_tokens(grad, probs).T.astype(BF16)
        pieces = []
        for frame in range(WT):
            rows = slice(frame * CELLS, (frame + 1) * CELLS)
            first = (WT - 1 - frame) * CELLS
            grad_probs = dot_rows(grad[rows], values)
            weight = probs[rows].astype(F32)
            product = weight * grad_probs
            total = jnp.sum(product, axis=-1, keepdims=True)
            grad_scores = (product - weight * total).astype(BF16)
            refs.strip[head, :, first : first + WIN] += grad_scores.astype(F32)
            refs.gq[rows, lanes] = dot(grad_scores, keys).astype(BF16)
            pieces.append(grad_scores)
        refs.gk[:, lanes] = dot_tokens(query, jnp.concatenate(pieces, axis=0)).T.astype(BF16)

    @pl.when(pl.program_id(1) == pl.num_programs(1) - 1)
    def _():
        refs.table[...] = jnp.zeros_like(refs.table)
        for head in range(2):
            for frame in range(FRAMES):
                for row in range(WSIDE):
                    first = (WSIDE - 1 - row) * WSIDE
                    refs.table[
                        head, frame * WSIDE : (frame + 1) * WSIDE, first : first + CELLS
                    ] += refs.strip[
                        head, row * WSIDE : (row + 1) * WSIDE, frame * CELLS : (frame + 1) * CELLS
                    ]

    if work is not None:

        @pl.when(step == 15)
        def _():
            work.sent()


def middle_kernel(refs):
    order = [OUT] + [unit for j in range(4) for unit in (UP + j, DOWN + j)] + [OUT]
    gathering = reducing = None
    points = {}
    if hasattr(refs, "gather"):
        place = Place()
        place.greet()
        gathering = Gather(place, refs.held_out, THIRD, refs.gather)
        reducing = Reduce(place, refs.part, refs.total, EARLY, refs.reduce)
        for index, action in enumerate(gathering.actions()):
            points.setdefault((0, 1, 3, 5, 6)[index], []).append(action)
        ready = {DOWN: 4, UP: 5, DOWN + 1: 8, UP + 1: 9, DOWN + 2: 12}
        begun = -2
        for index, unit in enumerate(EARLY):
            begun = max(begun + 2, ready[unit])
            points.setdefault(begun, []).append(functools.partial(reducing.start, index, 1))
            for stage in (1, 2, 3, 4):
                points.setdefault(begun + 2 * stage - 1, []).append(
                    functools.partial(reducing.advance, index, stage)
                )

    held = refs.held_out if gathering is not None else refs.held
    count = [0]

    def pump():
        for action in points.pop(count[0], []):
            action()
        count[0] += 1

    def fetch(step):
        return pltpu.make_async_copy(
            held.at[order[step]], refs.unit.at[step % 4], refs.fetch.at[step % 4]
        )

    def start_fetch(step):
        if gathering is not None and order[step] in THIRD:
            gathering.arrive(THIRD.index(order[step]), 4)
        fetch(step).start()

    def put(slot, unit):
        return pltpu.make_async_copy(refs.made.at[slot], refs.part.at[unit], refs.made_sem.at[slot])

    for step in range(3):
        start_fetch(step)
    pump()
    refs.sums[...] = jnp.zeros_like(refs.sums)
    refs.mlp[...] = jnp.zeros_like(refs.mlp)
    refs.grad_normed[...] = jnp.zeros_like(refs.grad_normed)
    fetch(0).wait()

    def project(index):
        refs.attended[:, tile(index)] = dot(refs.mixed[...], two_columns(refs.unit.at[0], index))

    loop(4, project)
    pump()

    def modulate(window, at, mods, live):
        middle = refs.tokens[at, :].astype(F32) + mods[2] * refs.attended[at, :]
        normal, _ = centered(middle)
        refs.normed[at, :] = (normal * (1.0 + mods[4]) + mods[3]).astype(BF16)
        grad = jnp.where(live, refs.cotangent[at, :].astype(F32), 0.0)
        refs.grad_low[at, :] = (mods[5] * grad).astype(BF16)

    each_rows(refs.mod, refs.live, modulate)
    pump()
    for j in range(4):
        step = 1 + 2 * j
        up, down = refs.unit.at[step % 4], refs.unit.at[(step + 1) % 4]
        fetch(step).wait()
        fetch(step + 1).wait()
        start_fetch(step + 2)
        if j < 3:
            start_fetch(step + 3)

        def hide(index, up=up, down=down):
            hidden = dot(refs.normed[...], two_columns(up, index))
            bend = jnp.tanh(0.7978845608028654 * (hidden + 0.044715 * hidden * hidden * hidden))
            refs.activated[:, tile(index)] = (0.5 * hidden * (1.0 + bend)).astype(BF16)
            slope = 0.5 * (1.0 + bend) + 0.5 * hidden * (1.0 - bend * bend) * (
                0.7978845608028654 * (1.0 + 3.0 * 0.044715 * hidden * hidden)
            )
            grad_activated = dot_rows(refs.grad_low[...], some_rows(down, index))
            refs.grad_hidden[:, tile(index)] = (grad_activated * slope).astype(BF16)

        loop(4, hide)
        pump()

        def down_gradient(index):
            made = dot_tokens(refs.activated[:, tile(index)], refs.grad_low[...]).astype(BF16)
            for block in range(8):
                refs.made[0, block // 2, block % 2, index // 2, index % 2] = made[
                    :, block * LANES : (block + 1) * LANES
                ]

        loop(4, down_gradient)
        put(0, DOWN + j).start()
        put(0, DOWN + j).wait()
        pump()

        def up_gradient(index):
            made = dot_tokens(refs.normed[...], refs.grad_hidden[:, tile(index)]).astype(BF16)
            put_columns(refs.made.at[1], index, made)

        loop(4, up_gradient)
        put(1, UP + j).start()
        put(1, UP + j).wait()
        pump()

        def out_of_mlp(index, up=up, down=down):
            refs.mlp[:, tile(index)] += dot(refs.activated[...], two_columns(down, index))
            refs.grad_normed[:, tile(index)] += dot_rows(
                refs.grad_hidden[...], some_rows(up, index)
            )

        loop(4, out_of_mlp)
        pump()

    def join(window, at, mods, live):
        attended = refs.attended[at, :]
        middle = refs.tokens[at, :].astype(F32) + mods[2] * attended
        normal, root = centered(middle)
        mlp = refs.mlp[at, :]
        refs.output[at, :] = jnp.where(live, middle + mods[5] * mlp, 0.0).astype(BF16)
        grad_result = jnp.where(live, refs.cotangent[at, :].astype(F32), 0.0)
        grad_normed = refs.grad_normed[at, :]
        grad_middle = grad_result + norm_back(grad_normed, normal, root, mods[4])
        refs.grad_middle[at, :] = grad_middle
        refs.grad_low[at, :] = (mods[2] * grad_middle).astype(BF16)
        add_sums(refs.sums, window, 2, grad_middle * attended)
        add_sums(refs.sums, window, 3, grad_normed)
        add_sums(refs.sums, window, 4, grad_normed * normal)
        add_sums(refs.sums, window, 5, grad_result * mlp)

    each_rows(refs.mod, refs.live, join)
    pump()
    fetch(9).wait()

    def back(index):
        made = dot_tokens(refs.mixed[...], refs.grad_low[:, tile(index)]).astype(BF16)
        put_columns(refs.made.at[0], index, made)
        refs.grad_mixed[:, tile(index)] = dot_rows(
            refs.grad_low[...], some_rows(refs.unit.at[1], index)
        ).astype(BF16)

    loop(4, back)
    put(0, OUT).start()
    put(0, OUT).wait()
    while points:
        pump()
    if gathering is not None:
        gathering.sent()
        reducing.sent()


def leave_unit(refs, j, held, made):
    sources = (refs.gq, refs.gk, refs.gv)
    fetch = pltpu.make_async_copy(held, refs.unit, refs.fetch)
    fetch.start()
    for block in range(8):
        part, column = divmod(3 * block + j, 8)
        refs.packed[:, block * LANES : (block + 1) * LANES] = sources[part][
            :, column * LANES : (column + 1) * LANES
        ]

    def weight(index):
        grad = dot_tokens(refs.normed[...], refs.packed[:, tile(index)]).astype(BF16)
        put_columns(made, index, grad)

    loop(4, weight)
    fetch.wait()


def leave_back(refs):
    def back(index):
        refs.grad_normed[:, tile(index)] += dot_rows(refs.packed[...], some_rows(refs.unit, index))

    loop(4, back)


def leave_norm(refs):
    def join(window, at, mods, live):
        normal, root = centered(refs.tokens[at, :].astype(F32))
        grad_normed = refs.grad_normed[at, :]
        refs.grad_tokens[at, :] = refs.grad_middle[at, :] + norm_back(
            grad_normed, normal, root, mods[1]
        )
        add_sums(refs.sums, window, 0, grad_normed)
        add_sums(refs.sums, window, 1, grad_normed * normal)

    each_rows(refs.mod, refs.live, join)


def leave_plain_kernel(refs):
    refs.sums[...] = jnp.zeros_like(refs.sums)
    refs.grad_normed[...] = jnp.zeros_like(refs.grad_normed)
    for j in range(3):
        leave_unit(refs, j, refs.held.at[QKV + j], refs.made)
        put = pltpu.make_async_copy(refs.made, refs.part.at[j], refs.made_sem)
        put.start()
        leave_back(refs)
        put.wait()
    leave_norm(refs)


def leave_kernel(refs):
    place = Place()
    place.greet()
    z, x, y, c = place.z, place.x, place.y, place.c
    work = Reduce(place, refs.made, refs.total, (0, 1, 2), refs.reduce)
    refs.table[...] = refs.table_part[...]
    table = Small(place, refs.table, refs.table_small)
    clip = Small(place, refs.clip, refs.clip_small)
    table.start(1)
    refs.sums[...] = refs.late_sums[...]
    refs.grad_normed[...] = jnp.zeros_like(refs.grad_normed)
    leave_unit(refs, 0, refs.held.at[QKV], refs.made.at[0])
    work.start(0, 1)
    table.advance(1)
    leave_back(refs)
    work.advance(0, 1)
    leave_unit(refs, 1, refs.held.at[QKV + 1], refs.made.at[1])
    work.start(1, 1)
    table.advance(2)
    leave_back(refs)
    work.advance(1, 1)
    work.advance(0, 2)
    leave_unit(refs, 2, refs.held.at[QKV + 2], refs.made.at[2])
    work.start(2, 1)
    table.advance(3)
    leave_back(refs)
    work.advance(2, 1)
    work.advance(1, 2)
    work.advance(0, 3)
    leave_norm(refs)
    for block in range(48):
        which, column = divmod(block, 8)
        part = jnp.zeros((8, LANES), F32)
        for window in range(refs.mod.shape[0]):
            sums = refs.sums[window, which : which + 1, column * LANES : (column + 1) * LANES]
            part = part + refs.member[window] * sums
        refs.clip[block // 12, block // 6 % 2, block % 6 * 8 : block % 6 * 8 + 8, :] = part
    clip.start(1)
    work.advance(2, 2)
    work.advance(1, 3)
    clip.advance(1)
    work.advance(0, 4)
    refs.table_total[...] = table.advance(4)
    clip.advance(2)
    clip.advance(3)
    work.advance(2, 3)
    work.advance(1, 4)
    total = clip.advance(4)
    refs.clip_total[...] = total
    low = total.astype(BF16)
    cond = jnp.zeros((8, SHARE), F32)
    for block in range(6):
        cond = cond + dot_rows(
            low[block * 8 : block * 8 + 8], refs.ada[:, block * LANES : (block + 1) * LANES]
        )
    small = Copies(*refs.cond_small)
    refs.cond[y, c] = cond
    small(refs.cond.at[y, c], refs.cond.at[y, c], place.at(c=1 - c)).wait()
    small(refs.cond.at[y], refs.cond.at[y], place.at(y=1 - y)).wait()
    small(refs.cond, refs.cond_x, place.at(x=1 - x)).wait()
    refs.cond_z[z] = refs.cond[...] + refs.cond_x[...]
    copies = [
        small(refs.cond_z.at[z], refs.cond_z.at[z], place.at(z=place.far(k))) for k in (1, 2, 3)
    ]
    work.advance(2, 4)
    for copy in copies:
        copy.wait()
    refs.cond_total[...] = refs.cond_z[0] + refs.cond_z[1] + refs.cond_z[2] + refs.cond_z[3]
    work.sent()


def enter(special, tokens, held, mod, own, mod_part, member, table):
    rows = tokens.shape[0]
    inputs = {"tokens": (tokens, vmem())}
    outputs = {
        "normed": (shape(BF16, rows, D), vmem()),
        "packed": (shape(BF16, 3, rows, D), vmem()),
    }
    scratch = {"unit": pltpu.VMEM(SPLIT, BF16), "fetch": pltpu.SemaphoreType.DMA}
    if not special:
        inputs |= {"held": (held, anywhere()), "mod": (mod, vmem())}
        out = call(enter_plain_kernel, "enter_plain", inputs, outputs, scratch)
        out.mod, out.held = mod, held
        return out
    for name, block in zip(("qkv", "out", "up", "down"), own, strict=True):
        inputs[name] = (block, anywhere())
    inputs |= {
        "mod_part": (mod_part, vmem()),
        "member": (member, vmem()),
        "table_own": (table, vmem()),
    }
    outputs |= {
        "held": (shape(BF16, UNITS, *SPLIT), anywhere()),
        "mod": (shape(F32, member.shape[0], 8, D), vmem()),
        "table": (shape(BF16, 4, 2, *table.shape), vmem()),
    }
    rows_small = mod_part.shape[0]
    scratch |= {
        "own_sem": pltpu.SemaphoreType.DMA((16,)),
        "gather": Gather.scratch(len(FIRST)),
        "small": [pltpu.SemaphoreType.DMA((16,))] * 2,
        "from_core": pltpu.VMEM((rows_small, LANES), F32),
        "from_y": pltpu.VMEM((rows_small, LANES), F32),
        "mod_sum": pltpu.VMEM((rows_small, LANES), F32),
        "mods": pltpu.VMEM((4, 2, rows_small, LANES), F32),
    }
    return call(enter_kernel, "enter", inputs, outputs, scratch, collective=0)


def attend(special, packed, table, live_frames, held):
    window_count = live_frames.shape[0]
    rows = window_count * WIN
    inputs = {
        "live": (live_frames, smem()),
        "query": (packed, packed_block(0)),
        "key": (packed, packed_block(1)),
        "value": (packed, packed_block(2)),
        "table": (table, pl.BlockSpec((2, SPREAD, LANES), lambda p, w: (p, 0, 0))),
    }
    outputs = {
        "mixed": (shape(BF16, rows, D), pl.BlockSpec((WIN, LANES), lambda p, w: (w, p))),
        "probs": (
            shape(BF16, window_count, H, WIN, WIN),
            pl.BlockSpec((None, 2, WIN, WIN), lambda p, w: (w, p, 0, 0)),
        ),
    }
    scratch = {"strip": pltpu.VMEM((2, CELLS, STRIP), F32)}
    aliases, collective = (), None
    if special:
        inputs["held_in"] = (held, anywhere())
        outputs["held"] = (shape(BF16, UNITS, *SPLIT), anywhere())
        scratch["gather"] = Gather.scratch(len(SECOND))
        aliases, collective = (("held_in", "held"),), 1
    out = call(
        attend_kernel,
        "attend",
        inputs,
        outputs,
        scratch,
        aliases,
        collective,
        grid=(H // 2, window_count),
        limit=32,
    )
    if not special:
        out.held = held
    return out


def middle(special, live_frames, tokens, cotangent, mixed, mod, held):
    rows = tokens.shape[0]
    inputs = {
        "live": (live_frames, smem()),
        "tokens": (tokens, vmem()),
        "cotangent": (cotangent, vmem()),
        "mixed": (mixed, vmem()),
        "mod": (mod, vmem()),
        "held": (held, anywhere()),
    }
    outputs = {
        "output": (shape(BF16, rows, D), vmem()),
        "grad_middle": (shape(F32, rows, D), vmem()),
        "grad_mixed": (shape(BF16, rows, D), vmem()),
        "sums": (shape(F32, mod.shape[0], 8, D), vmem()),
        "part": (shape(BF16, UNITS, *SPLIT), anywhere()),
    }
    scratch = {
        "unit": pltpu.VMEM((4, *SPLIT), BF16),
        "attended": pltpu.VMEM((rows, D), F32),
        "normed": pltpu.VMEM((rows, D), BF16),
        "grad_low": pltpu.VMEM((rows, D), BF16),
        "mlp": pltpu.VMEM((rows, D), F32),
        "grad_normed": pltpu.VMEM((rows, D), F32),
        "activated": pltpu.VMEM((rows, D), BF16),
        "grad_hidden": pltpu.VMEM((rows, D), BF16),
        "made": pltpu.VMEM((2, *SPLIT), BF16),
        "fetch": pltpu.SemaphoreType.DMA((4,)),
        "made_sem": pltpu.SemaphoreType.DMA((2,)),
    }
    aliases, collective = (), None
    if special:
        outputs["held_out"] = (shape(BF16, UNITS, *SPLIT), anywhere())
        outputs["total"] = (shape(F32, len(EARLY), SHARE, LANES), vmem())
        scratch["gather"] = Gather.scratch(len(THIRD))
        scratch["reduce"] = Reduce.scratch(len(EARLY))
        aliases, collective = (("held", "held_out"),), 2
    return call(middle_kernel, "middle", inputs, outputs, scratch, aliases, collective, limit=60)


def attend_back(special, packed, probs, grad_mixed, part):
    window_count = probs.shape[0]
    rows = window_count * WIN

    def block():
        return pl.BlockSpec((WIN, LANES), lambda p, w: (w, p))

    inputs = {
        "query": (packed, packed_block(0)),
        "key": (packed, packed_block(1)),
        "value": (packed, packed_block(2)),
        "probs": (probs, pl.BlockSpec((None, 2, WIN, WIN), lambda p, w: (w, p, 0, 0))),
        "grad": (grad_mixed, block()),
    }
    outputs = {name: (shape(BF16, rows, D), block()) for name in ("gq", "gk", "gv")}
    outputs["table"] = (
        shape(F32, H, SPREAD, LANES),
        pl.BlockSpec((2, SPREAD, LANES), lambda p, w: (p, 0, 0)),
    )
    scratch = {"strip": pltpu.VMEM((2, CELLS, STRIP), F32)}
    collective = None
    if special:
        inputs["part"] = (part, anywhere())
        outputs["total"] = (
            shape(F32, len(LATE), SHARE, LANES),
            pl.BlockSpec((len(LATE), SHARE, LANES), lambda p, w: (0, 0, 0)),
        )
        scratch["reduce"] = Reduce.scratch(len(LATE))
        collective = 3
    return call(
        attend_back_kernel,
        "attend_back",
        inputs,
        outputs,
        scratch,
        collective=collective,
        grid=(H // 2, window_count),
        limit=40,
    )


def leave(special, live_frames, tokens, mod, normed, grad_middle, back, held, late_sums, ada, member):
    rows = tokens.shape[0]
    inputs = {
        "live": (live_frames, smem()),
        "tokens": (tokens, vmem()),
        "mod": (mod, vmem()),
        "normed": (normed, vmem()),
        "grad_middle": (grad_middle, vmem()),
        "gq": (back.gq, vmem()),
        "gk": (back.gk, vmem()),
        "gv": (back.gv, vmem()),
        "held": (held, anywhere()),
    }
    outputs = {"grad_tokens": (shape(F32, rows, D), vmem())}
    scratch = {
        "unit": pltpu.VMEM(SPLIT, BF16),
        "packed": pltpu.VMEM((rows, D), BF16),
        "grad_normed": pltpu.VMEM((rows, D), F32),
        "fetch": pltpu.SemaphoreType.DMA,
    }
    if not special:
        outputs["sums"] = (shape(F32, mod.shape[0], 8, D), vmem())
        outputs["part"] = (shape(BF16, 3, *SPLIT), anywhere())
        scratch["made"] = pltpu.VMEM(SPLIT, BF16)
        scratch["made_sem"] = pltpu.SemaphoreType.DMA
        return call(leave_plain_kernel, "leave_plain", inputs, outputs, scratch)
    inputs |= {
        "late_sums": (late_sums, vmem()),
        "table_part": (back.table.reshape(4, 2, 2 * SPREAD, LANES), vmem()),
        "ada": (ada, vmem()),
        "member": (member, vmem()),
    }
    outputs |= {
        "total": (shape(F32, 3, SHARE, LANES), vmem()),
        "clip_total": (shape(F32, MOD_ROWS, LANES), vmem()),
        "table_total": (shape(F32, 2 * SPREAD, LANES), vmem()),
        "cond_total": (shape(F32, 2, 2, 8, SHARE), vmem()),
    }
    scratch |= {
        "made": pltpu.VMEM((3, *SPLIT), BF16),
        "sums": pltpu.VMEM((mod.shape[0], 8, D), F32),
        "reduce": Reduce.scratch(3),
        "table": pltpu.VMEM((4, 2, 2 * SPREAD, LANES), F32),
        "table_small": Small.scratch(2 * SPREAD),
        "clip": pltpu.VMEM((4, 2, MOD_ROWS, LANES), F32),
        "clip_small": Small.scratch(MOD_ROWS),
        "cond": pltpu.VMEM((2, 2, 8, SHARE), F32),
        "cond_x": pltpu.VMEM((2, 2, 8, SHARE), F32),
        "cond_z": pltpu.VMEM((4, 2, 2, 8, SHARE), F32),
        "cond_small": [pltpu.SemaphoreType.DMA((8,))] * 2,
    }
    return call(leave_kernel, "leave", inputs, outputs, scratch, collective=4)


def per_device(
    special,
    tokens,
    condition,
    clip_frames,
    ada_weight,
    ada_bias,
    qkv_weight,
    out_weight,
    up_weight,
    down_weight,
    rel_table,
    cotangent,
):
    window_count = tokens.shape[0]
    clip_count = condition.shape[0]
    rows_ada, cols_ada = ada_weight.shape
    row_block = lax.axis_index("fsdp")
    col_block = lax.axis_index("dp")
    first_window = lax.axis_index(("dp", "fsdp")) * window_count
    live_frames, member_int = window_layout(clip_frames, first_window, window_count)
    member = member_int.astype(F32)
    activity_low = jax.nn.silu(condition).astype(BF16)
    act_rows = lax.dynamic_slice_in_dim(activity_low, row_block * rows_ada, rows_ada, 1)

    mod_part = jnp.dot(act_rows, ada_weight, preferred_element_type=F32)
    mod_part = mod_part + jnp.where(row_block == 0, ada_bias.astype(F32), 0.0)[None, :]
    token_rows = tokens.reshape(window_count * WIN, D)
    cotangent_rows = cotangent.reshape(window_count * WIN, D)
    own = (qkv_weight, out_weight, up_weight, down_weight)
    if special:
        clips = jnp.pad(mod_part, ((0, 8 - clip_count), (0, 0)))
        clips = clips.reshape(8, 6, LANES).transpose(1, 0, 2).reshape(MOD_ROWS, LANES)
        member_wide = jnp.pad(member, ((0, 0), (0, 8 - clip_count)))[:, :, None]
        member_wide = jnp.broadcast_to(member_wide, (window_count, 8, LANES))
        start = enter(
            True, token_rows, None, None, own, clips, member_wide, spread_table(rel_table)
        )
        table = start.table.reshape(H, SPREAD, LANES)
    else:
        member_wide = None
        clip_mod = lax.all_gather(lax.psum(mod_part, "fsdp"), "dp", axis=1, tiled=True)
        window_mod = jnp.sum(member[:, :, None] * clip_mod[None], axis=1)
        window_mod = jnp.pad(window_mod.reshape(window_count, 6, D), ((0, 0), (0, 2), (0, 0)))
        whole = [
            lax.all_gather(
                lax.all_gather(weight, "dp", axis=1, tiled=True), "fsdp", axis=0, tiled=True
            )
            for weight in own
        ]
        held = units_of(*whole).reshape(UNITS, *SPLIT)
        start = enter(False, token_rows, held, window_mod, None, None, None, None)
        table = spread_table(lax.all_gather(rel_table, "dp", axis=0, tiled=True))
    mod = start.mod
    across = attend(special, start.packed, table, live_frames, start.held)
    mid = middle(
        special, live_frames, token_rows, cotangent_rows, across.mixed, mod, across.held
    )
    back = attend_back(special, start.packed, across.probs, mid.grad_mixed, mid.part)
    held = mid.held_out if special else across.held
    end = leave(
        special,
        live_frames,
        token_rows,
        mod,
        start.normed,
        mid.grad_middle,
        back,
        held,
        mid.sums,
        ada_weight,
        member_wide,
    )
    if special:
        shares = [None] * UNITS
        for units, totals in ((EARLY, mid.total), (LATE, back.total), (FIRST, end.total)):
            for index, unit in enumerate(units):
                shares[unit] = totals[index]
        grads = own_blocks(jnp.stack(shares))
        clip_cols = end.clip_total.reshape(6, 8, LANES).transpose(1, 0, 2).reshape(8, cols_ada)
        clip_cols = clip_cols[:clip_count].astype(BF16)
        cond_total = end.cond_total.transpose(2, 0, 1, 3).reshape(8, D)[:clip_count]
        table_grad = gather_table(end.table_total.reshape(2, SPREAD, LANES))
    else:
        part = jnp.concatenate([end.part, mid.part[OUT:]])
        grads = [
            lax.psum_scatter(
                lax.psum_scatter(grad, "fsdp", scatter_dimension=0, tiled=True),
                "dp",
                scatter_dimension=1,
                tiled=True,
            ).astype(F32)
            for grad in weights_of(part.reshape(UNITS, 8, D, LANES))
        ]
        grad_mod = (mid.sums + end.sums)[:, :6].reshape(window_count, 6 * D)
        clip_part = lax.dot_general(
            member,
            grad_mod,
            (((0,), (0,)), ((), ())),
            precision=HIGHEST,
            preferred_element_type=F32,
        )
        clip_sum, table_sum = lax.psum((clip_part, gather_table(back.table)), ("dp", "fsdp"))
        clip_cols = lax.dynamic_slice_in_dim(
            clip_sum.astype(BF16), col_block * cols_ada, cols_ada, 1
        )
        heads_own = rel_table.shape[0]
        table_grad = lax.dynamic_slice_in_dim(table_sum, col_block * heads_own, heads_own, 0)
        cond_part = lax.dot_general(
            clip_cols, ada_weight, (((1,), (1,)), ((), ())), preferred_element_type=F32
        )
        cond_total = lax.all_gather(lax.psum(cond_part, "dp"), "fsdp", axis=1, tiled=True)
    grad_ada_weight = lax.dot_general(
        act_rows, clip_cols, (((0,), (0,)), ((), ())), preferred_element_type=F32
    )
    grad_ada_bias = jnp.sum(clip_cols.astype(F32), axis=0)
    _, silu_back = jax.vjp(jax.nn.silu, condition)
    return (
        mid.output.reshape(tokens.shape),
        end.grad_tokens.reshape(tokens.shape),
        silu_back(cond_total)[0],
        grad_ada_weight,
        grad_ada_bias,
        *grads,
        table_grad,
    )


def solution(mesh):
    special = dict(mesh.shape) == {"dp": 8, "fsdp": 4}
    both = P(("dp", "fsdp"), None, None)
    weight = P("fsdp", "dp")
    in_specs = (both, P(), P(), weight, P("dp")) + (weight,) * 4 + (P("dp", None), both)
    out_specs = (both, both, P(), weight, P("dp")) + (weight,) * 4 + (P("dp", None),)
    return jax.shard_map(
        functools.partial(per_device, special),
        mesh=mesh,
        in_specs=in_specs,
        out_specs=out_specs,
        check_vma=False,
    )
```

time: 1920 us -> 474 us (0.25)
  other arithmetic: 590 us -> 7.13 us
  local copies, waits for them, and re-layouts: 505 us -> 26.9 us
  waiting for transfers between devices: 455 us -> 0 us
  Pallas kernels: 0 us -> 436 us
  blocking collectives: 171 us -> 0 us
  matrix products: 166 us -> 3.1 us
    scatter-add x1 -> x0, other arithmetic: 544 us -> none  [per_device(): table_part = jnp.zeros((H, REL), jnp.float32).at[:, index_table.reshape(-...]
    pallas_call x0 -> x5, Pallas kernels: none -> 436 us  [call(): pl.pallas_call(body, in_specs=[spec for _, spec in inputs.values()], out_...]
    gather x2 -> x0, local copies, waits for them, and re-layouts: 373 us -> none  [per_device(): rel_bias = table_all.astype(jnp.float32)[:, index_table]]
    unnamed x21 -> x0, waiting for transfers between devices: 199 us -> none
    all_gather x9 -> x0, waiting for transfers between devices: 183 us -> none  [the longest x1 63.4 us: per_device(): lax.all_gather(ada_weight, 'dp', axis=1, tiled=True)]
    dot_general x22 -> x3, matrix products: 164 us -> 1.91 us  [the longest x1 1.16 us: per_device(): mod_part = jnp.dot(act_rows, ada_weight, preferred_element_type=F32)]
    all_gather x3 -> x0, blocking collectives: 91.4 us -> none  [the longest x1 30.5 us: per_device(): lax.all_gather(out_weight, 'dp', axis=1, tiled=True)]
    psum x2 -> x0, blocking collectives: 79.2 us -> none  [the longest x1 41.4 us: per_device(): cond_total = lax.psum(cond_placed, ('dp', 'fsdp'))]
  transfers between devices with their start and end apart: 18 -> 0, of which waited for: 9 -> 0; matrix products, arithmetic and copies ran while one was open for 63% -> 0% of each run, Pallas kernels for 0% -> 0%
where the time goes in v2:
time: 474 us
  Pallas kernels  436 us (92%)
  local copies, waits for them, and re-layouts  26.9 us (6%)
  other arithmetic  7.13 us (2%)
    pallas_call x5, Pallas kernels, call(): pl.pallas_call(body, in_specs=[spec for _, spec in inputs.values()], out_...  436 us
    unnamed x46, local copies, waits for them, and re-layouts  19.6 us

profile of v2, /device:TPU:0, one launch (start us, length us, event | category | flops | bytes accessed | tf_op | source)
XLA Modules:
  0.0 473.7 jit_solution(957757750745693582)
XLA Ops:
  0.7 0.7 fusion.19
  1.3 0.2 reduce-window.9
  1.5 0.7 bitcast_subtract_fusion
  2.2 0.2 fusion.17
  2.4 0.9 select_reduce_fusion
  3.4 0.7 convert_select_fusion
  4.0 0.7 broadcast_in_dim.6.refs_6_.refs_12_
  4.7 0.8 reshape.142
  5.5 0.1 rev.6
  5.7 0.7 add_divide_fusion
  6.4 0.7 fusion.16
  7.1 1.2 convolution_add_fusion
  8.3 0.6 pad_bitcast_fusion.refs_5_
  8.9 0.2 compare_and_fusion
  9.1 0.7 copy-done.17
  9.8 0.2 fusion
  10.0 0.6 pad.14.refs_7_
  10.7 84.3 %enter.1 = (bf16[640,1024]{1,0:T(8,128)(2,1)}, bf16[3,640,1024]{2,1,0:T(8,128)(2,1)}, bf16[12,4,2,2,2,256,128]{6,5,4,3,2,1,0:T(8,128)(2,1)}, f32[2,8,1024]{2,1,0:T(8,128)}, bf16[4,2,2,80,128]{4,3,2,1,0:T(8,128)(2,1)}) custom-call(bf16[640,1024]{1,0:T(8,128)(2,1)} %bitcast.50, bf16[256,384]{1,0:T(8,128)(2,1)} %refs_1_.1, bf16[256,128]{1,0:T(8,128)(2,1)} %refs_2_.1, ...), custom_call_target="tpu_custom_call" | custom-call | tf_op jit(solution)/shard_map/enter/pallas_call | solution.py:538
  95.0 2.1 copy-done
  97.1 1.0 copy-done.11
  98.1 90.5 %attend.1 = (bf16[640,1024]{1,0:T(8,128)(2,1)S(1)}, bf16[2,16,320,320]{3,2,1,0:T(8,128)(2,1)S(1)}, bf16[12,4,2,2,2,256,128]{6,5,4,3,2,1,0:T(8,128)(2,1)}) custom-call(s32[2]{0:T(128)S(1)} %subtract_minimum_fusion.refs_0_, bf16[3,640,1024]{2,1,0:T(8,128)(2,1)S(1)} %copy-done, bf16[3,640,1024]{2,1,0:T(8,128)(2,1)S(1)} %copy-done, ...), custom_call_target="tpu_custom_call", output_to_operand_aliasing={{2}: (5, {})} | custom-call | tf_op jit(solution)/shard_map/attend/pallas_call | solution.py:538
  188.6 3.0 copy-done.2
  191.6 1.1 copy-done.7
  192.7 114.6 %middle.1 = (bf16[640,1024]{1,0:T(8,128)(2,1)}, f32[640,1024]{1,0:T(8,128)}, bf16[640,1024]{1,0:T(8,128)(2,1)}, f32[2,8,1024]{2,1,0:T(8,128)}, bf16[12,4,2,2,2,2...) custom-call(s32[2]{0:T(128)} %copy-done.12, ...), custom_call_target="tpu_custom_call", output_to_operand_aliasing={{5}: (5, {})} | custom-call | tf_op jit(solution)/shard_map/middle/pallas_call | solution.py:538
  307.3 1.3 copy-done.3
  308.6 70.3 %attend_back.1 = (bf16[640,1024]{1,0:T(8,128)(2,1)S(1)}, bf16[640,1024]{1,0:T(8,128)(2,1)S(1)}, bf16[640,1024]{1,0:T(8,128)(2,1)S(1)}, f32[16,80,128]{2,1,0:T(8,128)S(1)}, f32[4,256,128]{2,1,0:T(8,128)S(1)}) custom-call(bf16[3,640,1024]{2,1,0:T(8,128)(2,1)S(1)} %copy-done.1, bf16[3,640,1024]{2,1,0:T(8,128)(2,1)S(1)} %copy-done.1, ...), custom_call_target="tpu_custom_call" | custom-call | tf_op jit(solution)/shard_map/attend_back/pallas_call | solution.py:538
  379.0 1.0 copy-done.4
  380.0 1.1 copy-done.5
  381.1 1.1 copy-done.6
  382.2 0.8 copy-done.8
  383.0 0.8 copy-done.9
  383.8 75.9 %leave.1 = (f32[640,1024]{1,0:T(8,128)}, f32[3,256,128]{2,1,0:T(8,128)}, f32[48,128]{1,0:T(8,128)}, f32[160,128]{1,0:T(8,128)}, f32[2,2,8,256]{3,2,1,0:T(8,128)}) custom-call(s32[2]{0:T(128)} %copy-done.12, bf16[640,1024]{1,0:T(8,128)(2,1)} %bitcast.52, f32[2,8,1024]{2,1,0:T(8,128)} %get-tuple-element.39.refs_4_.refs_2_, ...), custom_call_target="tpu_custom_call" | custom-call | tf_op jit(solution)/shard_map/leave/pallas_call | solution.py:538
  459.7 0.8 slice.62
  460.6 0.6 fusion.5
  461.2 1.4 convert_reduce_fusion
  462.6 0.9 slice.64
  463.5 0.5 fusion.2
  464.1 0.7 reshape.155
  464.8 0.2 copy.24
  465.0 0.9 copy.27
  465.9 0.7 fusion.21
  466.7 0.8 copy.26
  467.6 0.2 copy.25
  467.8 1.0 copy.28
  468.8 1.2 fusion.6
  470.0 1.1 copy.33
  471.1 1.2 copy-done.13
  472.2 1.5 copy.34
  (47 shorter events, 0.5 us)
Async XLA Ops:
  3.2 91.8 %copy-start.12 = (s32[2]{0:T(128)}, s32[2]{0:T(128)S(1)}, u32[]{:S(2)}) copy-start(s32[2]{0:T(128)S(1)} %subtract_minimum_fusion.refs_0_) | copy-start | bytes 28
  9.1 0.7 copy-start.17
  95.0 2.1 copy-start
  97.1 1.0 copy-start.11
  188.6 3.0 copy-start.2
  191.6 1.1 copy-start.7
  192.7 114.6 %copy-start.1 = (bf16[3,640,1024]{2,1,0:T(8,128)(2,1)S(1)}, bf16[3,640,1024]{2,1,0:T(8,128)(2,1)}, u32[]{:S(2)}) copy-start(bf16[3,640,1024]{2,1,0:T(8,128)(2,1)} %get-tuple-element.35.refs_1_.refs_2_.refs_3_.refs_0_) | copy-start | bytes 11796484
  307.3 1.3 copy-start.3
  378.9 1.1 copy-start.4
  380.0 1.1 copy-start.5
  381.1 1.1 copy-start.6
  382.2 0.8 copy-start.8
  383.0 0.8 copy-start.9
  383.8 76.8 %copy-start.19 = (f32[3,1024]{1,0:T(4,128)S(1)}, f32[3,1024]{1,0:T(4,128)}, u32[]{:S(2)}) copy-start(f32[3,1024]{1,0:T(4,128)} %param.12) | copy-start | bytes 36868
  383.8 79.7 %copy-start.18 = (pred[225,1024]{1,0:T(8,128)(4,1)S(1)}, pred[225,1024]{1,0:T(8,128)(4,1)}, u32[]{:S(2)}) copy-start(pred[225,1024]{1,0:T(8,128)(4,1)} %copy-done.17) | copy-start | bytes 691204
  459.7 5.1 %copy-start.16 = (f32[3,256,128]{2,1,0:T(8,128)S(1)}, f32[3,256,128]{2,1,0:T(8,128)}, u32[]{:S(2)}) copy-start(f32[3,256,128]{2,1,0:T(8,128)} %get-tuple-element.56) | copy-start | bytes 1179652
  461.2 4.7 copy-start.10
  464.8 1.8 copy-start.15
  467.6 1.2 copy-start.20
  467.6 2.4 copy-start.14
  470.0 2.2 copy-start.13

commit v3 on v2

v3 whole, which is shorter than its diff:
```python
import functools

import jax
import jax.numpy as jnp
from jax import lax
from jax.experimental import pallas as pl
from jax.experimental.pallas import tpu as pltpu
from jax.sharding import PartitionSpec as P

D = 1024
H = 16
HD = 64
WT = 5
WSIDE = 8
WIN = 320
SPW = 16
CELLS = WSIDE * WSIDE
FRAMES = 2 * WT - 1
OFFSETS = (2 * WSIDE - 1) ** 2
REL = FRAMES * OFFSETS
LANES = 128
TILE = 256
SPREAD = 80
STRIP = 640

EPSILON = 1e-06
NEGATIVE = -1000000000.0
HIGHEST = lax.Precision.HIGHEST
F32 = jnp.float32
BF16 = jnp.bfloat16
MESH = pl.DeviceIdType.MESH
MIB = 2**20

QKV, OUT, UP, DOWN, UNITS = 0, 3, 4, 8, 12
SHARE = 256
HALF = 128


def window_layout(clip_frames, first_window, window_count):
    slab_count = 1 + (clip_frames > WT).astype(jnp.int32)
    starts = jnp.cumsum(slab_count, dtype=jnp.int32) - slab_count
    global_window = first_window + jnp.arange(window_count, dtype=jnp.int32)
    slab_of = global_window // SPW
    owners = jnp.sum((starts[None, :] <= slab_of[:, None]).astype(jnp.int32), axis=1) - 1
    clip_ids = jnp.arange(clip_frames.shape[0], dtype=jnp.int32)
    member = (owners[:, None] == clip_ids[None, :]).astype(jnp.int32)
    clip_start = jnp.sum(member * starts[None, :], axis=1)
    own_frames = jnp.sum(member * clip_frames[None, :], axis=1)
    inner_slab = slab_of - clip_start
    return (jnp.minimum(own_frames - WT * inner_slab, WT), member)


def offset_spread():
    side_span = 2 * WSIDE - 1
    shape = (OFFSETS, WSIDE * LANES)
    offset = lax.broadcasted_iota(jnp.int32, shape, 0)
    place = lax.broadcasted_iota(jnp.int32, shape, 1)
    own, row, other = place // LANES, place // WSIDE % (LANES // WSIDE), place % WSIDE
    row_diff, col_diff = side_span - 1 - row, own - other + (WSIDE - 1)
    return ((row < side_span) & (row_diff * side_span + col_diff == offset)).astype(BF16)


def spread_table(table):
    heads = table.shape[0]
    by_frame = table.reshape(heads, FRAMES, OFFSETS)[:, ::-1].reshape(heads * FRAMES, OFFSETS)
    spread = jnp.dot(by_frame, offset_spread(), preferred_element_type=F32).astype(BF16)
    spread = spread.reshape(heads, FRAMES * WSIDE, LANES)
    return jnp.pad(spread, ((0, 0), (0, SPREAD - FRAMES * WSIDE), (0, 0)))


def gather_table(spread):
    heads = spread.shape[0]
    by_frame = spread[:, : FRAMES * WSIDE].reshape(heads * FRAMES, WSIDE * LANES)
    sums = lax.dot_general(
        by_frame,
        offset_spread().astype(F32),
        (((1,), (1,)), ((), ())),
        precision=HIGHEST,
        preferred_element_type=F32,
    )
    return sums.reshape(heads, FRAMES, OFFSETS)[:, ::-1].reshape(heads, FRAMES * OFFSETS)


def units_of(qkv, out, up, down):
    return jnp.concatenate(
        [
            qkv.reshape(D, 8, 3, LANES).transpose(2, 1, 0, 3),
            out.reshape(D, 8, 1, LANES).transpose(2, 1, 0, 3),
            up.reshape(D, 8, 4, LANES).transpose(2, 1, 0, 3),
            down.reshape(8, 4, LANES, 8, LANES).transpose(1, 3, 0, 2, 4).reshape(4, 8, D, LANES),
        ]
    )


def weights_of(units):
    def columns(part):
        return part.transpose(2, 1, 0, 3).reshape(D, -1)

    down = units[DOWN:].reshape(4, 8, 8, LANES, LANES).transpose(2, 0, 3, 1, 4)
    return (
        columns(units[QKV:OUT]),
        columns(units[OUT:UP]),
        columns(units[UP:DOWN]),
        down.reshape(4 * D, D),
    )


def own_blocks(shares):
    def columns(part):
        return part.transpose(1, 0, 2).reshape(SHARE, -1)

    down = shares[DOWN:].reshape(4, 2, LANES, LANES).transpose(1, 0, 2, 3).reshape(4 * SHARE, LANES)
    return (columns(shares[QKV:OUT]), columns(shares[OUT:UP]), columns(shares[UP:DOWN]), down)


def dot(left, right):
    return jnp.dot(left, right, preferred_element_type=F32)


def dot_rows(left, right):
    return lax.dot_general(left, right, (((1,), (1,)), ((), ())), preferred_element_type=F32)


def dot_tokens(left, right):
    return lax.dot_general(left, right, (((0,), (0,)), ((), ())), preferred_element_type=F32)


def half(index):
    return pl.ds(pl.multiple_of(index * 512, 512), 512)


def four_columns(unit, index):
    blocks = [unit[2 * index + x // 2, x % 2].reshape(D, LANES) for x in range(4)]
    return jnp.concatenate(blocks, axis=1)


def half_rows(unit, index):
    blocks = [unit[block // 2, block % 2, index].reshape(512, LANES) for block in range(8)]
    return jnp.concatenate(blocks, axis=1)


def put_columns(unit, index, values):
    for x in range(4):
        unit[2 * index + x // 2, x % 2] = values[:, x * LANES : (x + 1) * LANES].reshape(2, 2, SHARE, LANES)


def loop(count, body):
    def step(index, carry):
        body(index)
        return carry

    lax.fori_loop(0, count, step, 0)


def vmem():
    return pl.BlockSpec(memory_space=pltpu.VMEM)


def anywhere():
    return pl.BlockSpec(memory_space=pl.ANY)


def smem():
    return pl.BlockSpec(memory_space=pltpu.SMEM)


def shape(dtype, *sizes):
    return jax.ShapeDtypeStruct(sizes, dtype)


def params(collective=None, limit=58):
    if collective is None:
        return pltpu.CompilerParams(vmem_limit_bytes=limit * MIB)
    return pltpu.CompilerParams(
        vmem_limit_bytes=limit * MIB, collective_id=collective, has_side_effects=True
    )


def centered(values):
    center = values - jnp.mean(values, axis=-1, keepdims=True)
    spread = jnp.mean(center * center, axis=-1, keepdims=True)
    root = lax.rsqrt(spread + EPSILON)
    return center * root, root


def norm_back(grad_normed, normal, root, scale):
    grad = grad_normed * (1.0 + scale)
    mean = jnp.mean(grad, axis=-1, keepdims=True)
    along = jnp.mean(grad * normal, axis=-1, keepdims=True)
    return root * (grad - mean - normal * along)


def each_rows(mod_ref, live_ref, body, rows=32):
    for window in range(mod_ref.shape[0]):
        live = live_ref[window] * CELLS

        def step(index, window=window, live=live):
            at = pl.ds(pl.multiple_of(window * WIN + index * rows, rows), rows)
            mods = [mod_ref[window, k : k + 1, :] for k in range(6)]
            slot = index * rows + lax.broadcasted_iota(jnp.int32, (rows, 1), 0)
            body(window, at, mods, slot < live)

        loop(WIN // rows, step)


def add_sums(sums_ref, window, which, values):
    sums_ref[window, which : which + 1, :] += jnp.sum(values, axis=0, keepdims=True)


class Place:
    def __init__(self):
        column, row = lax.axis_index("dp"), lax.axis_index("fsdp")
        self.z, self.x, self.y, self.c = column // 2, column % 2, row // 2, row % 2

    def at(self, z=None, x=None, y=None, c=None):
        z = self.z if z is None else z
        x = self.x if x is None else x
        y = self.y if y is None else y
        c = self.c if c is None else c
        return (z * 2 + x, y * 2 + c)

    def far(self, k):
        return lax.rem(self.z + k, 4)

    def greet(self):
        peers = [self.at(z=self.far(k)) for k in (1, 2, 3)]
        peers += [self.at(x=1 - self.x), self.at(y=1 - self.y), self.at(c=1 - self.c)]
        barrier = pltpu.get_barrier_semaphore()
        for peer in peers:
            pl.semaphore_signal(barrier, inc=1, device_id=peer, device_id_type=MESH)
        pl.semaphore_wait(barrier, len(peers))


class Moves:
    def __init__(self, place, stages, scratch):
        self.place = place
        self.send, self.recv = scratch
        self.first, count = {}, 0
        for unit, stage in stages:
            self.first[unit, stage] = count
            count += self.counts[unit in SIDEWAYS][stage - 1]
        self.flying = []

    @classmethod
    def semaphores(cls, stages):
        count = sum(cls.counts[unit in SIDEWAYS][stage - 1] for unit, stage in stages)
        return [pltpu.SemaphoreType.DMA((count,))] * 2

    def made(self, unit, stage, moves):
        copies = []
        for index, (source, target, device) in enumerate(moves):
            slot = self.first[unit, stage] + index
            copies.append(
                pltpu.make_async_remote_copy(
                    src_ref=source,
                    dst_ref=target,
                    send_sem=self.send.at[slot],
                    recv_sem=self.recv.at[slot],
                    device_id=device,
                    device_id_type=MESH,
                )
            )
        return copies

    def begin(self, unit, stage):
        for copy in self.copies(unit, stage):
            copy.start()
        self.flying.append((unit, stage))

    def arrive(self, unit, stage):
        if (unit, stage) in self.flying:
            self.flying.remove((unit, stage))
            for copy in self.copies(unit, stage):
                copy.wait_recv()

    def sent(self):
        for unit, stage in self.first:
            for copy in self.copies(unit, stage):
                copy.wait_send()


class Gather(Moves):
    counts = ((3, 2, 2, 1), (2, 6, 2, 1))

    def __init__(self, place, held, stages, scratch):
        super().__init__(place, stages, scratch)
        self.held = held

    def copies(self, unit, stage):
        p, held = self.place, self.held.at[unit]
        at_x, at_y, at_core = p.at(x=1 - p.x), p.at(y=1 - p.y), p.at(c=1 - p.c)
        own = held.at[p.z, p.x, p.y, p.c]
        if stage == 4:
            refs = [(held.at[:, :, :, p.c], at_core)]
        elif stage == 3:
            refs = [
                (held.at[:, :, p.y, p.c, :HALF], at_y),
                (held.at[:, p.x, :, p.c, HALF:], at_x),
            ]
        elif unit in SIDEWAYS and stage == 1:
            refs = [(own.at[:HALF], at_x), (own.at[HALF:], at_y)]
        elif unit in SIDEWAYS:
            refs = []
            for k in (1, 2, 3):
                refs.append((held.at[p.z, :, p.y, p.c, :HALF], p.at(z=p.far(k))))
                refs.append((held.at[p.z, p.x, :, p.c, HALF:], p.at(z=p.far(k))))
        elif stage == 1:
            refs = [(own, p.at(z=p.far(k))) for k in (1, 2, 3)]
        else:
            refs = [
                (held.at[:, p.x, p.y, p.c, :HALF], at_x),
                (held.at[:, p.x, p.y, p.c, HALF:], at_y),
            ]
        return self.made(unit, stage, [(ref, ref, device) for ref, device in refs])

    def advance(self, unit, stage):
        self.arrive(unit, stage - 1)
        self.begin(unit, stage)

    def finish(self):
        for unit, stage in list(self.flying):
            self.arrive(unit, stage)
        self.sent()


class Reduce(Moves):
    counts = ((1, 2, 2, 3), (1, 2, 6, 2))

    def __init__(self, place, part, total, units, scratch):
        stages = [(unit, stage) for unit in units for stage in (1, 2, 3, 4)]
        super().__init__(place, stages, scratch[6:])
        self.part, self.total, self.units = part, total, units
        self.own, self.core, self.side, self.corner, self.distant, self.load = scratch[:6]

    @classmethod
    def scratch(cls, units):
        count = len(units)
        return [
            pltpu.VMEM((OWN_SLOTS, 4, 2, 2, SHARE, LANES), BF16),
            pltpu.VMEM((count, 4, 2, 2, SHARE, LANES), BF16),
            pltpu.VMEM((count, 2, 4, 2, HALF, LANES), BF16),
            pltpu.VMEM((count, 2, 4, HALF, LANES), BF16),
            pltpu.VMEM((count, 3, 2, 2, HALF, LANES), BF16),
            pltpu.SemaphoreType.DMA((OWN_SLOTS,)),
        ] + cls.semaphores([(unit, stage) for unit in units for stage in (1, 2, 3, 4)])

    def own_copy(self, unit):
        slot = self.units.index(unit) % OWN_SLOTS
        return pltpu.make_async_copy(
            self.part(unit).at[:, :, :, self.place.c], self.own.at[slot], self.load.at[slot]
        )

    def copies(self, unit, stage):
        p, index = self.place, self.units.index(unit)
        at_x, at_y, at_core = p.at(x=1 - p.x), p.at(y=1 - p.y), p.at(c=1 - p.c)
        core, side, corner = self.core.at[index], self.side.at[index], self.corner.at[index]
        distant = self.distant.at[index]
        if stage == 1:
            moves = [(self.part(unit).at[:, :, :, 1 - p.c], core, at_core)]
        elif stage == 2:
            moves = [
                (core.at[:, :, 1 - p.y, :HALF], side.at[0], at_y),
                (core.at[:, 1 - p.x, :, HALF:], side.at[1], at_x),
            ]
        elif unit in SIDEWAYS and stage == 3:
            moves = []
            for k in (1, 2, 3):
                for half in range(2):
                    source = side.at[half, p.far(k)]
                    moves.append((source, distant.at[k - 1, half], p.at(z=p.far(k))))
        elif unit in SIDEWAYS:
            moves = [
                (corner.at[0, 1 - p.x], corner.at[0, 2], at_x),
                (corner.at[1, 1 - p.y], corner.at[1, 2], at_y),
            ]
        elif stage == 3:
            moves = [
                (side.at[0, :, 1 - p.x], corner.at[0], at_x),
                (side.at[1, :, 1 - p.y], corner.at[1], at_y),
            ]
        else:
            moves = [
                (corner.at[:, p.far(k)], distant.at[k - 1, 0], p.at(z=p.far(k)))
                for k in (1, 2, 3)
            ]
        return self.made(unit, stage, moves)

    def begin(self, unit, stage):
        super().begin(unit, stage)
        if stage == 1:
            self.own_copy(unit).start()

    def combine(self, unit, stage):
        p, index = self.place, self.units.index(unit)
        core, side, corner = self.core.at[index], self.side.at[index], self.corner.at[index]
        distant = self.distant.at[index]

        def plus(left, right):
            return (left.astype(F32) + right.astype(F32)).astype(BF16)

        def from_core(step):
            z, x, y = step // 4, step // 2 % 2, step % 2
            core[z, x, y] = plus(core[z, x, y], self.own[index % OWN_SLOTS, z, x, y])

        def from_side(step):
            z, b = step // 2, step % 2
            side[0, z, b] = plus(side[0, z, b], core[z, b, p.y, :HALF])
            side[1, z, b] = plus(side[1, z, b], core[z, p.x, b, HALF:])

        def from_corner(z):
            corner[0, z] = plus(corner[0, z], side[0, z, p.x])
            corner[1, z] = plus(corner[1, z], side[1, z, p.y])

        def from_far(half):
            total = corner[half, p.z].astype(F32)
            for k in range(3):
                total = total + distant[k, 0, half].astype(F32)
            self.total[index, pl.ds(pl.multiple_of(half * HALF, HALF), HALF), :] = total

        def sideways_far(half):
            for b in range(2):
                total = side[half, p.z, b].astype(F32)
                for k in range(3):
                    total = total + distant[k, half, b].astype(F32)
                corner[half, b] = total.astype(BF16)

        def sideways_last():
            self.total[index, :HALF, :] = corner[0, p.x].astype(F32) + corner[0, 2].astype(F32)
            self.total[index, HALF:, :] = corner[1, p.y].astype(F32) + corner[1, 2].astype(F32)

        if unit in SIDEWAYS and stage == 3:
            loop(2, sideways_far)
        elif unit in SIDEWAYS and stage == 4:
            sideways_last()
        else:
            steps = {1: (16, from_core), 2: (8, from_side), 3: (4, from_corner), 4: (2, from_far)}
            loop(*steps[stage])

    def advance(self, unit, stage):
        self.arrive(unit, stage)
        if stage == 1:
            self.own_copy(unit).wait()
        self.combine(unit, stage)
        if stage < 4:
            self.begin(unit, stage + 1)


class Small:
    def __init__(self, place, values, scratch):
        self.place, self.values = place, values
        self.from_core, self.from_x, self.from_y, self.from_z, self.send, self.recv = scratch

    @staticmethod
    def scratch(rows):
        return [
            pltpu.VMEM((4, 2, rows, LANES), F32),
            pltpu.VMEM((4, rows, LANES), F32),
            pltpu.VMEM((4, rows, LANES), F32),
            pltpu.VMEM((3, rows, LANES), F32),
            pltpu.SemaphoreType.DMA((6,)),
            pltpu.SemaphoreType.DMA((6,)),
        ]

    def copies(self, stage):
        p, values = self.place, self.values

        def copy(slot, source, target, device):
            return pltpu.make_async_remote_copy(
                src_ref=source,
                dst_ref=target,
                send_sem=self.send.at[slot],
                recv_sem=self.recv.at[slot],
                device_id=device,
                device_id_type=MESH,
            )

        if stage == 1:
            return [copy(0, values, self.from_core, p.at(c=1 - p.c))]
        if stage == 2:
            return [copy(1, values.at[:, 1 - p.x], self.from_x, p.at(x=1 - p.x))]
        if stage == 3:
            return [copy(2, values.at[:, p.x], self.from_y, p.at(y=1 - p.y))]
        return [
            copy(2 + k, values.at[p.far(k), p.x], self.from_z.at[k - 1], p.at(z=p.far(k)))
            for k in (1, 2, 3)
        ]

    def start(self, stage):
        for copy in self.copies(stage):
            copy.start()

    def advance(self, stage):
        p, values = self.place, self.values
        for copy in self.copies(stage):
            copy.wait()
        if stage == 1:
            values[...] += self.from_core[...]
        elif stage == 2:
            values[:, p.x] += self.from_x[...]
        elif stage == 3:
            values[:, p.x] += self.from_y[...]
        else:
            return values[p.z, p.x] + self.from_z[0] + self.from_z[1] + self.from_z[2]
        self.start(stage + 1)
        return None


class Copies:
    def __init__(self, send, recv):
        self.send, self.recv, self.count = send, recv, 0

    def __call__(self, source, target, device):
        slot = self.count
        self.count += 1
        copy = pltpu.make_async_remote_copy(
            src_ref=source,
            dst_ref=target,
            send_sem=self.send.at[slot],
            recv_sem=self.recv.at[slot],
            device_id=device,
            device_id_type=MESH,
        )
        copy.start()
        return copy


class Refs:
    pass


def call(kernel, name, inputs, outputs, scratch, aliases=(), collective=None, grid=None, limit=58):
    names = list(inputs) + list(outputs)
    flat = []
    for value in scratch.values():
        flat += value if isinstance(value, list) else [value]

    def body(*refs):
        held = Refs()
        rest = list(refs)
        for key in names:
            setattr(held, key, rest.pop(0))
        for key, value in scratch.items():
            if isinstance(value, list):
                setattr(held, key, [rest.pop(0) for _ in value])
            else:
                setattr(held, key, rest.pop(0))
        kernel(held)

    extra = {} if grid is None else {"grid": grid}
    result = pl.pallas_call(
        body,
        in_specs=[spec for _, spec in inputs.values()],
        out_specs=[spec for _, spec in outputs.values()],
        out_shape=[out for out, _ in outputs.values()],
        scratch_shapes=flat,
        input_output_aliases={
            list(inputs).index(one): list(outputs).index(other) for one, other in aliases
        },
        compiler_params=params(collective, limit),
        name=name,
        **extra,
    )(*[array for array, _ in inputs.values()])
    out = Refs()
    for key, value in zip(outputs, result, strict=True):
        setattr(out, key, value)
    return out


SPLIT = (4, 2, 2, 2, SHARE, LANES)
MOD_ROWS = 48
OWN_SLOTS = 4
ORDER = (0, 1, 2, 3, 4, 8, 5, 9, 6, 10, 7, 11)
SIDEWAYS = ()
ENTER = (
    ((0, 1),),
    ((1, 1), (0, 2)),
    ((2, 1), (1, 2), (0, 3)),
    ((3, 1), (2, 2), (1, 3), (0, 4)),
    ((4, 1), (3, 2), (2, 3), (1, 4)),
    ((5, 1), (4, 2), (3, 3), (2, 4)),
)
ATTEND = {
    0: ((6, 1), (5, 2), (4, 3), (3, 4)),
    3: ((7, 1), (6, 2), (5, 3), (4, 4)),
    6: ((8, 1), (7, 2), (6, 3), (5, 4)),
}
MIDDLE = {
    0: ((9, 1), (8, 2), (7, 3), (6, 4)),
    2: ((10, 1), (9, 2), (8, 3), (7, 4)),
    5: ((11, 1), (10, 2), (9, 3), (8, 4)),
    7: ((11, 2), (10, 3), (9, 4)),
    9: ((11, 3), (10, 4)),
    11: ((11, 4),),
}
EARLY = (DOWN, UP, DOWN + 1)
LATE = (UP + 1, DOWN + 2, UP + 2, DOWN + 3, UP + 3, OUT, QKV, QKV + 1, QKV + 2)


def gather_stages(points):
    return [(ORDER[index], stage) for point in points for index, stage in point]


def enter_norm(refs):
    rows = 32
    for window in range(refs.mod.shape[0]):
        shift, scale = refs.mod[window, 0:1, :], refs.mod[window, 1:2, :]

        def step(index, window=window, shift=shift, scale=scale):
            at = pl.ds(pl.multiple_of(window * WIN + index * rows, rows), rows)
            normal, _ = centered(refs.tokens[at, :].astype(F32))
            refs.normed[at, :] = (normal * (1.0 + scale) + shift).astype(BF16)

        loop(WIN // rows, step)


def enter_unit(refs, j, held):
    fetch = pltpu.make_async_copy(held, refs.unit, refs.fetch)
    fetch.start()
    fetch.wait()

    def project(index):
        refs.packed[j, :, half(index)] = dot(
            refs.normed[...], four_columns(refs.unit, index)
        ).astype(BF16)

    loop(2, project)


def enter_plain_kernel(refs):
    enter_norm(refs)
    for j in range(3):
        enter_unit(refs, j, refs.held.at[QKV + j])


def enter_kernel(refs):
    place = Place()
    place.greet()
    z, x, y, c = place.z, place.x, place.y, place.c

    own = []
    for unit in range(UNITS):
        if unit >= DOWN:
            first = (unit - DOWN) * LANES
            for half in range(2):
                at = slice(half * 512 + first, half * 512 + first + LANES)
                refs.own[unit, half * HALF : (half + 1) * HALF] = refs.down[at, :]
        else:
            source, start = (
                (refs.qkv, QKV) if unit < OUT else (refs.out, OUT) if unit < UP else (refs.up, UP)
            )
            first = (unit - start) * LANES
            refs.own[unit] = source[:, first : first + LANES]
        own.append(
            pltpu.make_async_copy(
                refs.own.at[unit], refs.held.at[unit, z, x, y, c], refs.own_sem.at[unit]
            )
        )
        own[-1].start()
    work = Gather(place, refs.held, gather_stages(ENTER), refs.gather)
    points = list(ENTER)

    def tick():
        for index, stage in points.pop(0):
            work.advance(ORDER[index], stage)

    small = Copies(*refs.small)
    copy = small(refs.mod_part, refs.from_core, place.at(c=1 - c))
    for one in own:
        one.wait()
    tick()
    refs.table[z, x, c] = refs.table_own[c]
    copy.wait()
    refs.mod_sum[...] = refs.mod_part[...] + refs.from_core[...]
    copy = small(refs.mod_sum, refs.from_y, place.at(y=1 - y))
    copy.wait()
    refs.mods[z, x] = refs.mod_sum[...] + refs.from_y[...]
    copies = [
        small(refs.mods.at[z, x], refs.mods.at[z, x], place.at(x=1 - x)),
        small(refs.table.at[z, x, c], refs.table.at[z, x, c], place.at(x=1 - x)),
    ]
    copies[0].wait()
    mods = [
        small(refs.mods.at[z], refs.mods.at[z], place.at(z=place.far(k))) for k in (1, 2, 3)
    ]
    tick()
    copies[1].wait()
    tick()
    for copy in mods:
        copy.wait()
    for window in range(refs.mod.shape[0]):
        for block in range(48):
            which, column = divmod(block, 8)
            part = refs.mods[block // 12, block // 6 % 2, block % 6 * 8 : block % 6 * 8 + 8, :]
            refs.mod[window, which : which + 1, column * LANES : (column + 1) * LANES] = jnp.sum(
                part * refs.member[window], axis=0, keepdims=True
            )
    enter_norm(refs)
    tick()
    tables = [
        small(refs.table.at[z, :, c], refs.table.at[z, :, c], place.at(z=place.far(k)))
        for k in (1, 2, 3)
    ]
    work.arrive(QKV, 4)
    enter_unit(refs, 0, refs.held.at[QKV])
    tick()
    work.arrive(QKV + 1, 4)
    enter_unit(refs, 1, refs.held.at[QKV + 1])
    tick()
    for copy in tables:
        copy.wait()
    last = small(refs.table.at[:, :, c], refs.table.at[:, :, c], place.at(c=1 - c))
    work.arrive(QKV + 2, 4)
    enter_unit(refs, 2, refs.held.at[QKV + 2])
    last.wait()
    work.finish()


def attend_kernel(refs):
    work = None
    step = pl.program_id(0)
    if hasattr(refs, "gather"):
        place = Place()
        work = Gather(place, refs.held, gather_stages(ATTEND.values()), refs.gather)
        for at, stages in ATTEND.items():

            @pl.when(step == at)
            def _(at=at, stages=stages):
                if at == 0:
                    place.greet()
                for index, stage in stages:
                    work.advance(ORDER[index], stage)

    for head in range(2):
        spread = refs.table[head].astype(F32)
        for frame in range(FRAMES):
            block = spread[frame * WSIDE : (frame + 1) * WSIDE]
            for row in range(WSIDE):
                first = (WSIDE - 1 - row) * WSIDE
                refs.strip[
                    head, row * WSIDE : (row + 1) * WSIDE, frame * CELLS : (frame + 1) * CELLS
                ] = block[:, first : first + CELLS]
        for frame in range(WT):
            first = (WT - 1 - frame) * CELLS
            refs.bias[head, frame * CELLS : (frame + 1) * CELLS, :] = refs.strip[
                head, :, first : first + WIN
            ]

    for window in range(refs.live.shape[0]):
        rows = slice(window * WIN, (window + 1) * WIN)
        live = refs.live[window] * CELLS
        key_live = lax.broadcasted_iota(jnp.int32, (1, WIN), 1) < live
        for head in range(2):
            lanes = slice(head * HD, (head + 1) * HD)
            query = refs.query[rows, lanes] * BF16(HD ** (-0.5))
            scores = dot_rows(query, refs.key[rows, lanes]) + refs.bias[head]
            scores = jnp.where(key_live, scores, NEGATIVE)
            shifted = jnp.exp(scores - jnp.max(scores, axis=-1, keepdims=True))
            totals = jnp.sum(shifted, axis=-1, keepdims=True)
            probs = (shifted * (1.0 / totals)).astype(BF16)
            refs.probs[window, head] = probs
            refs.mixed[rows, lanes] = dot(probs, refs.value[rows, lanes]).astype(BF16)

    if work is not None:

        @pl.when(step == 7)
        def _():
            work.finish()


def packed_block(part, rows):
    pairs = H // 2
    return pl.BlockSpec(
        (None, rows, LANES),
        lambda pair: (
            lax.rem(part * pairs + pair, 3),
            0,
            lax.div(part * pairs + pair, 3),
        ),
    )


def attend_back_pair(refs, pair):
    scale = BF16(HD ** (-0.5))
    refs.spread[...] = jnp.zeros_like(refs.spread)
    refs.strip[...] = jnp.zeros_like(refs.strip)
    windows = refs.probs.shape[0]
    results = [[[None] * windows for _ in range(2)] for _ in range(3)]
    for head in range(2):
        lanes = slice(head * HD, (head + 1) * HD)
        bias = None
        for window in range(windows):
            rows = slice(window * WIN, (window + 1) * WIN)
            grad = refs.grad[rows, lanes]
            probs = refs.probs[window, head]
            results[2][head][window] = dot_tokens(grad, probs).T.astype(BF16)
            grad_probs = dot_rows(grad, refs.value[rows, lanes])
            weight = probs.astype(F32)
            product = weight * grad_probs
            total = jnp.sum(product, axis=-1, keepdims=True)
            grad_scores = (product - weight * total).astype(BF16)
            wide = grad_scores.astype(F32)
            bias = wide if bias is None else bias + wide
            results[0][head][window] = dot(grad_scores, refs.key[rows, lanes] * scale).astype(BF16)
            query = refs.query[rows, lanes] * scale
            results[1][head][window] = dot_tokens(query, grad_scores).T.astype(BF16)
        for frame in range(WT):
            first = (WT - 1 - frame) * CELLS
            refs.strip[head, :, first : first + WIN] += bias[frame * CELLS : (frame + 1) * CELLS]
        for frame in range(FRAMES):
            for row in range(WSIDE):
                first = (WSIDE - 1 - row) * WSIDE
                refs.spread[
                    head, frame * WSIDE : (frame + 1) * WSIDE, first : first + CELLS
                ] += refs.strip[
                    head, row * WSIDE : (row + 1) * WSIDE, frame * CELLS : (frame + 1) * CELLS
                ]
    for part in range(3):
        block = part * (H // 2) + pair
        lanes = pl.ds(pl.multiple_of(lax.div(block, 3) * LANES, LANES), LANES)
        for window in range(windows):
            rows = slice(window * WIN, (window + 1) * WIN)
            both = [results[part][head][window] for head in range(2)]
            refs.grad_packed[lax.rem(block, 3), rows, lanes] = jnp.concatenate(both, axis=1)


def middle_kernel(refs):
    order = [OUT] + [unit for j in range(4) for unit in (UP + j, DOWN + j)] + [OUT]
    gathering = reducing = None
    points = {}
    waiting = set()
    if hasattr(refs, "gather"):
        place = Place()
        place.greet()
        gathering = Gather(place, refs.held_out, gather_stages(MIDDLE.values()), refs.gather)
        reducing = Reduce(place, lambda unit: refs.part.at[unit], refs.total, EARLY, refs.reduce)
        for stages in MIDDLE.values():
            waiting |= {ORDER[index] for index, stage in stages if stage == 4}
        for unit, times in zip(
            EARLY, ((7, 9, 13, 16, 19), (9, 11, 15, 18, 20), (11, 13, 17, 20, 21)), strict=True
        ):
            points.setdefault(times[0], []).append(functools.partial(reducing.begin, unit, 1))
            for stage in (1, 2, 3, 4):
                points.setdefault(times[stage], []).append(
                    functools.partial(reducing.advance, unit, stage)
                )

    held = refs.held_out if gathering is not None else refs.held
    count = [0]

    def pump():
        for index, stage in MIDDLE.get(count[0], ()) if gathering is not None else ():
            gathering.advance(ORDER[index], stage)
            if stage == 4:
                waiting.discard(ORDER[index])
        for action in points.pop(count[0], []):
            action()
        count[0] += 1

    def fetch(step):
        return pltpu.make_async_copy(
            held.at[order[step]], refs.unit.at[step % 4], refs.fetch.at[step % 4]
        )

    def start_fetch(step):
        if gathering is not None:
            assert order[step] not in waiting
            gathering.arrive(order[step], 4)
        fetch(step).start()

    def put(slot, unit):
        return pltpu.make_async_copy(refs.made.at[slot], refs.part.at[unit], refs.made_sem.at[slot])

    for step in range(3):
        start_fetch(step)
    pump()
    refs.sums[...] = jnp.zeros_like(refs.sums)
    refs.mlp[...] = jnp.zeros_like(refs.mlp)
    refs.grad_normed[...] = jnp.zeros_like(refs.grad_normed)
    fetch(0).wait()

    def project(index):
        refs.attended[:, half(index)] = dot(refs.mixed[...], four_columns(refs.unit.at[0], index))

    loop(2, project)
    pump()

    def modulate(window, at, mods, live):
        middle = refs.tokens[at, :].astype(F32) + mods[2] * refs.attended[at, :]
        normal, _ = centered(middle)
        refs.normed[at, :] = (normal * (1.0 + mods[4]) + mods[3]).astype(BF16)
        grad = jnp.where(live, refs.cotangent[at, :].astype(F32), 0.0)
        refs.grad_low[at, :] = (mods[5] * grad).astype(BF16)

    each_rows(refs.mod, refs.live, modulate)
    pump()
    for j in range(4):
        step = 1 + 2 * j
        up, down = refs.unit.at[step % 4], refs.unit.at[(step + 1) % 4]
        fetch(step).wait()
        fetch(step + 1).wait()
        start_fetch(step + 2)

        def hide(index, up=up, down=down):
            hidden = dot(refs.normed[...], four_columns(up, index))
            bend = jnp.tanh(0.7978845608028654 * (hidden + 0.044715 * hidden * hidden * hidden))
            refs.activated[:, half(index)] = (0.5 * hidden * (1.0 + bend)).astype(BF16)
            slope = 0.5 * (1.0 + bend) + 0.5 * hidden * (1.0 - bend * bend) * (
                0.7978845608028654 * (1.0 + 3.0 * 0.044715 * hidden * hidden)
            )
            grad_activated = dot_rows(refs.grad_low[...], half_rows(down, index))
            refs.grad_hidden[:, half(index)] = (grad_activated * slope).astype(BF16)

        loop(2, hide)
        if j > 0:
            put(1, UP + j - 1).wait()
        pump()

        def down_gradient(index):
            made = dot_tokens(refs.activated[:, half(index)], refs.grad_low[...]).astype(BF16)
            for block in range(8):
                refs.made[0, block // 2, block % 2, index] = made[
                    :, block * LANES : (block + 1) * LANES
                ].reshape(2, SHARE, LANES)

        loop(2, down_gradient)
        put(0, DOWN + j).start()
        pump()

        def up_gradient(index):
            made = dot_tokens(refs.normed[...], refs.grad_hidden[:, half(index)]).astype(BF16)
            put_columns(refs.made.at[1], index, made)

        loop(2, up_gradient)
        put(0, DOWN + j).wait()
        put(1, UP + j).start()
        pump()
        if j < 3:
            start_fetch(step + 3)

        def out_of_mlp(index, up=up, down=down):
            refs.mlp[:, half(index)] += dot(refs.activated[...], four_columns(down, index))
            refs.grad_normed[:, half(index)] += dot_rows(
                refs.grad_hidden[...], half_rows(up, index)
            )

        loop(2, out_of_mlp)
        pump()

    put(1, UP + 3).wait()

    def join(window, at, mods, live):
        attended = refs.attended[at, :]
        middle = refs.tokens[at, :].astype(F32) + mods[2] * attended
        normal, root = centered(middle)
        mlp = refs.mlp[at, :]
        refs.output[at, :] = jnp.where(live, middle + mods[5] * mlp, 0.0).astype(BF16)
        grad_result = jnp.where(live, refs.cotangent[at, :].astype(F32), 0.0)
        grad_normed = refs.grad_normed[at, :]
        grad_middle = grad_result + norm_back(grad_normed, normal, root, mods[4])
        refs.grad_middle[at, :] = grad_middle
        refs.grad_low[at, :] = (mods[2] * grad_middle).astype(BF16)
        add_sums(refs.sums, window, 2, grad_middle * attended)
        add_sums(refs.sums, window, 3, grad_normed)
        add_sums(refs.sums, window, 4, grad_normed * normal)
        add_sums(refs.sums, window, 5, grad_result * mlp)

    each_rows(refs.mod, refs.live, join)
    pump()
    fetch(9).wait()

    def back(index):
        made = dot_tokens(refs.mixed[...], refs.grad_low[:, half(index)]).astype(BF16)
        put_columns(refs.made.at[0], index, made)
        refs.grad_mixed[:, half(index)] = dot_rows(
            refs.grad_low[...], half_rows(refs.unit.at[1], index)
        ).astype(BF16)

    loop(2, back)
    put(0, OUT).start()
    put(0, OUT).wait()
    while points:
        pump()
    if gathering is not None:
        gathering.finish()
        reducing.sent()


def leave_weight(refs, j, made):
    def weight(index):
        grad = dot_tokens(refs.normed[...], refs.grad_packed[j, :, half(index)]).astype(BF16)
        put_columns(made, index, grad)

    loop(2, weight)


def leave_back(refs, j):
    def back(index):
        refs.grad_normed[:, half(index)] += dot_rows(
            refs.grad_packed[j], half_rows(refs.unit, index)
        )

    loop(2, back)


def leave_norm(refs):
    def join(window, at, mods, live):
        normal, root = centered(refs.tokens[at, :].astype(F32))
        grad_normed = refs.grad_normed[at, :]
        refs.grad_tokens[at, :] = refs.grad_middle[at, :] + norm_back(
            grad_normed, normal, root, mods[1]
        )
        add_sums(refs.sums, window, 0, grad_normed)
        add_sums(refs.sums, window, 1, grad_normed * normal)

    each_rows(refs.mod, refs.live, join)


def back_plain_kernel(refs):
    step = pl.program_id(0)

    @pl.when(step < H // 2)
    def _():
        attend_back_pair(refs, jnp.minimum(step, H // 2 - 1))

    @pl.when(step == H // 2)
    def _():
        refs.sums[...] = jnp.zeros_like(refs.sums)
        refs.grad_normed[...] = jnp.zeros_like(refs.grad_normed)
        for j in range(3):
            fetch = pltpu.make_async_copy(refs.held.at[QKV + j], refs.unit, refs.fetch)
            fetch.start()
            leave_weight(refs, j, refs.made)
            put = pltpu.make_async_copy(refs.made, refs.part.at[j], refs.made_sem)
            put.start()
            fetch.wait()
            leave_back(refs, j)
            put.wait()
        leave_norm(refs)


def back_kernel(refs):
    place = Place()
    z, x, y, c = place.z, place.x, place.y, place.c
    step = pl.program_id(0)
    work = Reduce(
        place,
        lambda unit: refs.made.at[unit] if unit < OUT else refs.part.at[unit],
        refs.total,
        LATE,
        refs.reduce,
    )
    table = Small(place, refs.table, refs.table_small)
    clip = Small(place, refs.clip, refs.clip_small)

    events = []
    for index, unit in enumerate(LATE):
        start = max(0, 2 * index - 2) if unit >= OUT else 9 + unit
        events.append((start, 0, functools.partial(work.begin, unit, 1)))
        for stage in (1, 2, 3, 4):
            time = max(1 + 2 * index, start + 1) + 3 * (stage - 1)
            events.append((time, stage, functools.partial(work.advance, unit, stage)))
    events.sort(key=lambda event: event[:2])

    def run(until):
        while events and events[0][0] < until:
            events.pop(0)[2]()

    for number in range(H // 2):

        @pl.when(step == number)
        def _(number=number):
            if number == 0:
                place.greet()
            run(number + 1)

    @pl.when(step < H // 2)
    def _():
        pair = jnp.minimum(step, H // 2 - 1)
        attend_back_pair(refs, pair)
        refs.table[lax.div(pair, 2), lax.rem(pair, 2)] = refs.spread[...].reshape(
            2 * SPREAD, LANES
        )

    @pl.when(step == H // 2)
    def _():
        table.start(1)
        refs.sums[...] = refs.late_sums[...]
        refs.grad_normed[...] = jnp.zeros_like(refs.grad_normed)

        def fetch(j):
            return pltpu.make_async_copy(refs.held.at[QKV + j], refs.unit, refs.fetch)

        fetch(0).start()
        run(9)
        leave_weight(refs, 0, refs.made.at[0])
        run(10)
        leave_weight(refs, 1, refs.made.at[1])
        run(11)
        table.advance(1)
        leave_weight(refs, 2, refs.made.at[2])
        run(12)
        fetch(0).wait()
        leave_back(refs, 0)
        fetch(1).start()
        run(13)
        table.advance(2)
        fetch(1).wait()
        leave_back(refs, 1)
        fetch(2).start()
        run(14)
        table.advance(3)
        fetch(2).wait()
        leave_back(refs, 2)
        run(15)
        leave_norm(refs)
        for block in range(48):
            which, column = divmod(block, 8)
            part = jnp.zeros((8, LANES), F32)
            for window in range(refs.mod.shape[0]):
                sums = refs.sums[window, which : which + 1, column * LANES : (column + 1) * LANES]
                part = part + refs.member[window] * sums
            refs.clip[block // 12, block // 6 % 2, block % 6 * 8 : block % 6 * 8 + 8, :] = part
        clip.start(1)
        run(17)
        clip.advance(1)
        refs.table_total[...] = table.advance(4)
        run(18)
        clip.advance(2)
        run(19)
        clip.advance(3)
        run(20)
        total = clip.advance(4)
        refs.clip_total[...] = total
        low = total.astype(BF16)
        cond = jnp.zeros((8, SHARE), F32)
        for block in range(6):
            cond = cond + dot_rows(
                low[block * 8 : block * 8 + 8], refs.ada[:, block * LANES : (block + 1) * LANES]
            )
        small = Copies(*refs.cond_small)
        refs.cond[y, c] = cond
        copy = small(refs.cond.at[y, c], refs.cond.at[y, c], place.at(c=1 - c))
        run(21)
        copy.wait()
        copy = small(refs.cond.at[y], refs.cond.at[y], place.at(y=1 - y))
        run(22)
        copy.wait()
        copy = small(refs.cond, refs.cond_x, place.at(x=1 - x))
        run(23)
        copy.wait()
        refs.cond_z[z] = refs.cond[...] + refs.cond_x[...]
        copies = [
            small(refs.cond_z.at[z], refs.cond_z.at[z], place.at(z=place.far(k)))
            for k in (1, 2, 3)
        ]
        run(100)
        for copy in copies:
            copy.wait()
        refs.cond_total[...] = refs.cond_z[0] + refs.cond_z[1] + refs.cond_z[2] + refs.cond_z[3]
        work.sent()


def enter(special, tokens, held, mod, own, mod_part, member, table):
    rows = tokens.shape[0]
    inputs = {"tokens": (tokens, vmem())}
    outputs = {
        "normed": (shape(BF16, rows, D), vmem()),
        "packed": (shape(BF16, 3, rows, D), vmem()),
    }
    scratch = {"unit": pltpu.VMEM(SPLIT, BF16), "fetch": pltpu.SemaphoreType.DMA}
    if not special:
        inputs |= {"held": (held, anywhere()), "mod": (mod, vmem())}
        out = call(enter_plain_kernel, "enter_plain", inputs, outputs, scratch)
        out.mod, out.held = mod, held
        return out
    for name, block in zip(("qkv", "out", "up", "down"), own, strict=True):
        inputs[name] = (block, vmem())
    inputs |= {
        "mod_part": (mod_part, vmem()),
        "member": (member, vmem()),
        "table_own": (table, vmem()),
    }
    outputs |= {
        "held": (shape(BF16, UNITS, *SPLIT), anywhere()),
        "mod": (shape(F32, member.shape[0], 8, D), vmem()),
        "table": (shape(BF16, 4, 2, *table.shape), vmem()),
    }
    rows_small = mod_part.shape[0]
    scratch |= {
        "own": pltpu.VMEM((UNITS, SHARE, LANES), BF16),
        "own_sem": pltpu.SemaphoreType.DMA((UNITS,)),
        "gather": Gather.semaphores(gather_stages(ENTER)),
        "small": [pltpu.SemaphoreType.DMA((16,))] * 2,
        "from_core": pltpu.VMEM((rows_small, LANES), F32),
        "from_y": pltpu.VMEM((rows_small, LANES), F32),
        "mod_sum": pltpu.VMEM((rows_small, LANES), F32),
        "mods": pltpu.VMEM((4, 2, rows_small, LANES), F32),
    }
    return call(enter_kernel, "enter", inputs, outputs, scratch, collective=0)


def attend(special, packed, table, live_frames, held):
    window_count = live_frames.shape[0]
    rows = window_count * WIN
    inputs = {
        "live": (live_frames, smem()),
        "query": (packed, packed_block(0, rows)),
        "key": (packed, packed_block(1, rows)),
        "value": (packed, packed_block(2, rows)),
        "table": (table, pl.BlockSpec((2, SPREAD, LANES), lambda p: (p, 0, 0))),
    }
    outputs = {
        "mixed": (shape(BF16, rows, D), pl.BlockSpec((rows, LANES), lambda p: (0, p))),
        "probs": (
            shape(BF16, window_count, H, WIN, WIN),
            pl.BlockSpec((window_count, 2, WIN, WIN), lambda p: (0, p, 0, 0)),
        ),
    }
    scratch = {
        "strip": pltpu.VMEM((2, CELLS, STRIP), F32),
        "bias": pltpu.VMEM((2, WIN, WIN), F32),
    }
    aliases, collective = (), None
    if special:
        inputs["held_in"] = (held, anywhere())
        outputs["held"] = (shape(BF16, UNITS, *SPLIT), anywhere())
        scratch["gather"] = Gather.semaphores(gather_stages(ATTEND.values()))
        aliases, collective = (("held_in", "held"),), 1
    out = call(
        attend_kernel,
        "attend",
        inputs,
        outputs,
        scratch,
        aliases,
        collective,
        grid=(H // 2,),
        limit=32,
    )
    if not special:
        out.held = held
    return out


def middle(special, live_frames, tokens, cotangent, mixed, mod, held):
    rows = tokens.shape[0]
    inputs = {
        "live": (live_frames, smem()),
        "tokens": (tokens, vmem()),
        "cotangent": (cotangent, vmem()),
        "mixed": (mixed, vmem()),
        "mod": (mod, vmem()),
        "held": (held, anywhere()),
    }
    outputs = {
        "output": (shape(BF16, rows, D), vmem()),
        "grad_middle": (shape(F32, rows, D), vmem()),
        "grad_mixed": (shape(BF16, rows, D), vmem()),
        "sums": (shape(F32, mod.shape[0], 8, D), vmem()),
        "part": (shape(BF16, UNITS, *SPLIT), anywhere()),
    }
    scratch = {
        "unit": pltpu.VMEM((4, *SPLIT), BF16),
        "attended": pltpu.VMEM((rows, D), F32),
        "normed": pltpu.VMEM((rows, D), BF16),
        "grad_low": pltpu.VMEM((rows, D), BF16),
        "mlp": pltpu.VMEM((rows, D), F32),
        "grad_normed": pltpu.VMEM((rows, D), F32),
        "activated": pltpu.VMEM((rows, D), BF16),
        "grad_hidden": pltpu.VMEM((rows, D), BF16),
        "made": pltpu.VMEM((2, *SPLIT), BF16),
        "fetch": pltpu.SemaphoreType.DMA((4,)),
        "made_sem": pltpu.SemaphoreType.DMA((2,)),
    }
    aliases, collective = (), None
    if special:
        outputs["held_out"] = (shape(BF16, UNITS, *SPLIT), anywhere())
        outputs["total"] = (shape(F32, len(EARLY), SHARE, LANES), vmem())
        scratch["gather"] = Gather.semaphores(gather_stages(MIDDLE.values()))
        scratch["reduce"] = Reduce.scratch(EARLY)
        aliases, collective = (("held", "held_out"),), 2
    return call(middle_kernel, "middle", inputs, outputs, scratch, aliases, collective, limit=60)


def back(
    special, live_frames, tokens, mod, start, probs, mid, held, ada, member
):
    window_count = probs.shape[0]
    rows = window_count * WIN
    pairs = H // 2

    def last(pair):
        return jnp.minimum(pair, pairs - 1)

    def whole(array):
        return pl.BlockSpec(array.shape, lambda p: (0,) * len(array.shape), pipeline_mode=pl.Buffered(1))

    def packed_pair(part):
        block = packed_block(part, rows)
        return pl.BlockSpec(block.block_shape, lambda p: block.index_map(last(p)))

    inputs = {
        "live": (live_frames, smem()),
        "query": (start.packed, packed_pair(0)),
        "key": (start.packed, packed_pair(1)),
        "value": (start.packed, packed_pair(2)),
        "probs": (
            probs,
            pl.BlockSpec((window_count, 2, WIN, WIN), lambda p: (0, last(p), 0, 0)),
        ),
        "grad": (mid.grad_mixed, pl.BlockSpec((rows, LANES), lambda p: (0, last(p)))),
        "held": (held, anywhere()),
    }
    for name, array in (
        ("tokens", tokens),
        ("mod", mod),
        ("normed", start.normed),
        ("grad_middle", mid.grad_middle),
    ):
        inputs[name] = (array, whole(array))

    def result(*sizes):
        made = shape(F32, *sizes)
        return made, whole(made)

    outputs = {"grad_tokens": result(rows, D)}
    scratch = {
        "strip": pltpu.VMEM((2, CELLS, STRIP), F32),
        "grad_packed": pltpu.VMEM((3, rows, D), BF16),
        "unit": pltpu.VMEM(SPLIT, BF16),
        "grad_normed": pltpu.VMEM((rows, D), F32),
        "fetch": pltpu.SemaphoreType.DMA,
    }
    if not special:
        outputs["sums"] = result(window_count, 8, D)
        outputs["part"] = (shape(BF16, 3, *SPLIT), anywhere())
        outputs["spread"] = (
            shape(F32, H, SPREAD, LANES),
            pl.BlockSpec((2, SPREAD, LANES), lambda p: (last(p), 0, 0)),
        )
        scratch["made"] = pltpu.VMEM(SPLIT, BF16)
        scratch["made_sem"] = pltpu.SemaphoreType.DMA
        return call(
            back_plain_kernel, "back_plain", inputs, outputs, scratch, grid=(pairs + 1,)
        )
    inputs |= {
        "late_sums": (mid.sums, whole(mid.sums)),
        "ada": (ada, whole(ada)),
        "member": (member, whole(member)),
        "part": (mid.part, anywhere()),
    }
    outputs |= {
        "total": result(len(LATE), SHARE, LANES),
        "clip_total": result(MOD_ROWS, LANES),
        "table_total": result(2 * SPREAD, LANES),
        "cond_total": result(2, 2, 8, SHARE),
    }
    scratch |= {
        "spread": pltpu.VMEM((2, SPREAD, LANES), F32),
        "made": pltpu.VMEM((3, *SPLIT), BF16),
        "sums": pltpu.VMEM((window_count, 8, D), F32),
        "reduce": Reduce.scratch(LATE),
        "table": pltpu.VMEM((4, 2, 2 * SPREAD, LANES), F32),
        "table_small": Small.scratch(2 * SPREAD),
        "clip": pltpu.VMEM((4, 2, MOD_ROWS, LANES), F32),
        "clip_small": Small.scratch(MOD_ROWS),
        "cond": pltpu.VMEM((2, 2, 8, SHARE), F32),
        "cond_x": pltpu.VMEM((2, 2, 8, SHARE), F32),
        "cond_z": pltpu.VMEM((4, 2, 2, 8, SHARE), F32),
        "cond_small": [pltpu.SemaphoreType.DMA((8,))] * 2,
    }
    return call(
        back_kernel,
        "back",
        inputs,
        outputs,
        scratch,
        collective=3,
        grid=(pairs + 1,),
        limit=62,
    )


def per_device(
    special,
    tokens,
    condition,
    clip_frames,
    ada_weight,
    ada_bias,
    qkv_weight,
    out_weight,
    up_weight,
    down_weight,
    rel_table,
    cotangent,
):
    window_count = tokens.shape[0]
    clip_count = condition.shape[0]
    rows_ada, cols_ada = ada_weight.shape
    row_block = lax.axis_index("fsdp")
    col_block = lax.axis_index("dp")
    first_window = lax.axis_index(("dp", "fsdp")) * window_count
    live_frames, member_int = window_layout(clip_frames, first_window, window_count)
    member = member_int.astype(F32)
    activity_low = jax.nn.silu(condition).astype(BF16)
    act_rows = lax.dynamic_slice_in_dim(activity_low, row_block * rows_ada, rows_ada, 1)

    mod_part = jnp.dot(act_rows, ada_weight, preferred_element_type=F32)
    mod_part = mod_part + jnp.where(row_block == 0, ada_bias.astype(F32), 0.0)[None, :]
    token_rows = tokens.reshape(window_count * WIN, D)
    cotangent_rows = cotangent.reshape(window_count * WIN, D)
    own = (qkv_weight, out_weight, up_weight, down_weight)
    if special:
        clips = jnp.pad(mod_part, ((0, 8 - clip_count), (0, 0)))
        clips = clips.reshape(8, 6, LANES).transpose(1, 0, 2).reshape(MOD_ROWS, LANES)
        member_wide = jnp.pad(member, ((0, 0), (0, 8 - clip_count)))[:, :, None]
        member_wide = jnp.broadcast_to(member_wide, (window_count, 8, LANES))
        start = enter(
            True, token_rows, None, None, own, clips, member_wide, spread_table(rel_table)
        )
        table = start.table.reshape(H, SPREAD, LANES)
    else:
        member_wide = None
        clip_mod = lax.all_gather(lax.psum(mod_part, "fsdp"), "dp", axis=1, tiled=True)
        window_mod = jnp.sum(member[:, :, None] * clip_mod[None], axis=1)
        window_mod = jnp.pad(window_mod.reshape(window_count, 6, D), ((0, 0), (0, 2), (0, 0)))
        whole = [
            lax.all_gather(
                lax.all_gather(weight, "dp", axis=1, tiled=True), "fsdp", axis=0, tiled=True
            )
            for weight in own
        ]
        held = units_of(*whole).reshape(UNITS, *SPLIT)
        start = enter(False, token_rows, held, window_mod, None, None, None, None)
        table = spread_table(lax.all_gather(rel_table, "dp", axis=0, tiled=True))
    mod = start.mod
    across = attend(special, start.packed, table, live_frames, start.held)
    mid = middle(
        special, live_frames, token_rows, cotangent_rows, across.mixed, mod, across.held
    )
    held = mid.held_out if special else across.held
    end = back(
        special,
        live_frames,
        token_rows,
        mod,
        start,
        across.probs,
        mid,
        held,
        ada_weight,
        member_wide,
    )
    if special:
        shares = [None] * UNITS
        for units, totals in ((EARLY, mid.total), (LATE, end.total)):
            for index, unit in enumerate(units):
                shares[unit] = totals[index]
        grads = own_blocks(jnp.stack(shares))
        clip_cols = end.clip_total.reshape(6, 8, LANES).transpose(1, 0, 2).reshape(8, cols_ada)
        clip_cols = clip_cols[:clip_count].astype(BF16)
        cond_total = end.cond_total.transpose(2, 0, 1, 3).reshape(8, D)[:clip_count]
        table_grad = gather_table(end.table_total.reshape(2, SPREAD, LANES))
    else:
        part = jnp.concatenate([end.part, mid.part[OUT:]])
        grads = [
            lax.psum_scatter(
                lax.psum_scatter(grad, "fsdp", scatter_dimension=0, tiled=True),
                "dp",
                scatter_dimension=1,
                tiled=True,
            ).astype(F32)
            for grad in weights_of(part.reshape(UNITS, 8, D, LANES))
        ]
        grad_mod = (mid.sums + end.sums)[:, :6].reshape(window_count, 6 * D)
        clip_part = lax.dot_general(
            member,
            grad_mod,
            (((0,), (0,)), ((), ())),
            precision=HIGHEST,
            preferred_element_type=F32,
        )
        clip_sum, table_sum = lax.psum((clip_part, gather_table(end.spread)), ("dp", "fsdp"))
        clip_cols = lax.dynamic_slice_in_dim(
            clip_sum.astype(BF16), col_block * cols_ada, cols_ada, 1
        )
        heads_own = rel_table.shape[0]
        table_grad = lax.dynamic_slice_in_dim(table_sum, col_block * heads_own, heads_own, 0)
        cond_part = lax.dot_general(
            clip_cols, ada_weight, (((1,), (1,)), ((), ())), preferred_element_type=F32
        )
        cond_total = lax.all_gather(lax.psum(cond_part, "dp"), "fsdp", axis=1, tiled=True)
    grad_ada_weight = lax.dot_general(
        act_rows, clip_cols, (((0,), (0,)), ((), ())), preferred_element_type=F32
    )
    grad_ada_bias = jnp.sum(clip_cols.astype(F32), axis=0)
    _, silu_back = jax.vjp(jax.nn.silu, condition)
    return (
        mid.output.reshape(tokens.shape),
        end.grad_tokens.reshape(tokens.shape),
        silu_back(cond_total)[0],
        grad_ada_weight,
        grad_ada_bias,
        *grads,
        table_grad,
    )


def solution(mesh):
    special = dict(mesh.shape) == {"dp": 8, "fsdp": 4}
    both = P(("dp", "fsdp"), None, None)
    weight = P("fsdp", "dp")
    in_specs = (both, P(), P(), weight, P("dp")) + (weight,) * 4 + (P("dp", None), both)
    out_specs = (both, both, P(), weight, P("dp")) + (weight,) * 4 + (P("dp", None),)
    return jax.shard_map(
        functools.partial(per_device, special),
        mesh=mesh,
        in_specs=in_specs,
        out_specs=out_specs,
        check_vma=False,
    )
```

time: 474 us -> 353 us (0.74)
  Pallas kernels: 436 us -> 316 us
  local copies, waits for them, and re-layouts: 26.9 us -> 21.2 us
    pallas_call x5 -> x4, Pallas kernels: 436 us -> 316 us  [call(): pl.pallas_call(body, in_specs=[spec for _, spec in inputs.values()], out_...]
    unnamed x46 -> x26, local copies, waits for them, and re-layouts: 19.6 us -> 12.8 us
where the time goes in v3:
time: 353 us; the launch traced here: 348 us
  Pallas kernels  316 us (90%)
  local copies, waits for them, and re-layouts  21.2 us (6%)
  other arithmetic  7.04 us (2%)
    pallas_call x4, Pallas kernels, call(): pl.pallas_call(body, in_specs=[spec for _, spec in inputs.values()], out_...  316 us
    unnamed x26, local copies, waits for them, and re-layouts  12.8 us

profile of v3, /device:TPU:0, one launch (start us, length us, event | category | flops | bytes accessed | tf_op | source)
XLA Modules:
  0.0 348.1 jit_solution(7381146287547813048)
XLA Ops:
  0.7 0.7 fusion.19
  1.3 0.2 reduce-window.9
  1.5 0.7 bitcast_subtract_fusion
  2.2 0.2 fusion.17
  2.4 0.9 select_reduce_fusion
  3.2 0.0 copy-start.4
  3.3 0.1 convert_convert_fusion
  3.4 0.7 convert_select_fusion
  4.0 0.7 broadcast_in_dim.6.refs_6_.refs_13_
  4.7 0.8 reshape.139
  5.5 0.1 rev.6
  5.7 0.7 add_divide_fusion
  6.4 0.7 fusion.16
  7.1 1.2 convolution_add_fusion
  8.3 0.6 pad_bitcast_fusion.refs_5_
  8.9 0.2 compare_and_fusion
  9.1 0.2 fusion
  9.3 0.6 pad.14.refs_7_
  10.0 65.2 %enter.1 = (bf16[640,1024]{1,0:T(8,128)(2,1)}, bf16[3,640,1024]{2,1,0:T(8,128)(2,1)}, bf16[12,4,2,2,2,256,128]{6,5,4,3,2,1,0:T(8,128)(2,1)}, f32[2,8,1024]{2,1,0:T(8,128)}, bf16[4,2,2,80,128]{4,3,2,1,0:T(8,128)(2,1)}) custom-call(bf16[640,1024]{1,0:T(8,128)(2,1)} %bitcast.49, bf16[256,384]{1,0:T(8,128)(2,1)} %refs_1_.1, bf16[256,128]{1,0:T(8,128)(2,1)} %refs_2_.1, ...), custom_call_target="tpu_custom_call" | custom-call | tf_op jit(solution)/shard_map/enter/pallas_call | solution.py:550
  75.1 0.0 copy-done.4
  75.1 0.0 copy-start
  75.2 2.1 copy-done
  77.3 1.0 copy-done.3
  78.2 34.7 %attend.1 = (bf16[640,1024]{1,0:T(8,128)(2,1)S(1)}, bf16[2,16,320,320]{3,2,1,0:T(8,128)(2,1)S(1)}, bf16[12,4,2,2,2,256,128]{6,5,4,3,2,1,0:T(8,128)(2,1)}) custom-call(s32[2]{0:T(128)S(1)} %subtract_minimum_fusion.refs_0_, bf16[3,640,1024]{2,1,0:T(8,128)(2,1)S(1)} %copy-done, bf16[3,640,1024]{2,1,0:T(8,128)(2,1)S(1)} %copy-done, ...), custom_call_target="tpu_custom_call", output_to_operand_aliasing={{2}: (5, {})} | custom-call | tf_op jit(solution)/shard_map/attend/pallas_call | solution.py:550
  113.0 0.0 copy-start.1
  113.0 3.0 copy-done.1
  116.0 1.1 copy-done.2
  117.1 98.2 %middle.1 = (bf16[640,1024]{1,0:T(8,128)(2,1)}, f32[640,1024]{1,0:T(8,128)}, bf16[640,1024]{1,0:T(8,128)(2,1)}, f32[2,8,1024]{2,1,0:T(8,128)}, bf16[12,4,2,2,2,2...) custom-call(s32[2]{0:T(128)} %copy-done.4, ...), custom_call_target="tpu_custom_call", output_to_operand_aliasing={{5}: (5, {})} | custom-call | tf_op jit(solution)/shard_map/middle/pallas_call | solution.py:550
  215.3 0.0 copy-start.9
  215.3 117.7 %back.1 = (f32[640,1024]{1,0:T(8,128)}, f32[9,256,128]{2,1,0:T(8,128)}, f32[48,128]{1,0:T(8,128)}, f32[160,128]{1,0:T(8,128)}, f32[2,2,8,256]{3,2,1,0:T(8,128)}) custom-call(s32[2]{0:T(128)} %copy-done.4, bf16[3,640,1024]{2,1,0:T(8,128)(2,1)} %get-tuple-element.30.refs_1_.refs_2_.refs_3_, bf16[3,640,1024]{2,1,0:T(8,128)(2,1)} %get-tuple-element.30.refs_1_.refs_2_.refs_3_, ...), custom_call_target="tpu_custom_call" | custom-call | tf_op jit(solution)/shard_map/back/pallas_call | solution.py:550
  333.0 0.9 slice.65
  333.9 0.6 fusion.5
  334.5 1.3 convert_reduce_fusion
  335.8 0.9 slice.67
  336.7 0.5 fusion.2
  337.2 0.1 rev.7
  337.3 0.7 reshape.151
  338.0 1.0 slice_bitcast_fusion
  339.1 0.7 fusion.20
  339.8 0.2 copy.24
  340.0 0.9 copy.27
  341.0 0.8 copy.26
  341.9 0.2 copy.25
  342.1 1.0 copy.28
  343.1 1.2 fusion.6
  344.3 1.1 copy.33
  345.3 1.2 copy-done.5
  346.5 1.5 copy.34
  (27 shorter events, 0.3 us)
Async XLA Ops:
  3.2 71.9 %copy-start.4 = (s32[2]{0:T(128)}, s32[2]{0:T(128)S(1)}, u32[]{:S(2)}) copy-start(s32[2]{0:T(128)S(1)} %subtract_minimum_fusion.refs_0_) | copy-start | bytes 28
  75.1 2.1 copy-start
  77.3 1.0 copy-start.3
  113.0 3.1 copy-start.1
  116.0 1.1 copy-start.2
  215.3 118.6 %copy-start.9 = (f32[3,1024]{1,0:T(4,128)S(1)}, f32[3,1024]{1,0:T(4,128)}, u32[]{:S(2)}) copy-start(f32[3,1024]{1,0:T(4,128)} %param.12) | copy-start | bytes 36868
  333.0 6.1 %copy-start.7 = (f32[9,256,128]{2,1,0:T(8,128)S(1)}, f32[9,256,128]{2,1,0:T(8,128)}, u32[]{:S(2)}) copy-start(f32[9,256,128]{2,1,0:T(8,128)} %get-tuple-element.47) | copy-start | bytes 3538948
  339.1 1.8 copy-start.8
  341.8 1.2 copy-start.10
  341.8 2.4 copy-start.6
  344.3 2.2 copy-start.5

commit v4 on v3

--- a/solution.py
+++ b/solution.py
@@ -21,6 +21,7 @@
 LANES = 128
 TILE = 256
 SPREAD = 80
+WIDE = 96
 STRIP = 640
 
 EPSILON = 1e-06
@@ -34,6 +35,85 @@
 QKV, OUT, UP, DOWN, UNITS = 0, 3, 4, 8, 12
 SHARE = 256
 HALF = 128
+
+
+SPLIT = (4, 2, 2, 2, SHARE, LANES)
+CLIP_ROWS = 4
+MOD_ROWS = 6 * CLIP_ROWS
+OWN_SLOTS = 4
+ORDER = (0, 1, 2, 3, 4, 8, 5, 9, 6, 10, 7, 11)
+GATHER_ASIDE = (UP + 3, DOWN + 3)
+REDUCE_ASIDE = (DOWN, UP + 2)
+ENTER = (
+    ((0, 1),),
+    ((1, 1), (0, 2)),
+    ((2, 1), (1, 2), (0, 3)),
+    ((3, 1), (2, 2), (1, 3), (0, 4)),
+    ((4, 1), (3, 2), (2, 3), (1, 4), (10, 1), (11, 1)),
+    ((5, 1), (6, 1), (4, 2), (3, 3), (2, 4), (10, 2), (11, 2)),
+)
+ATTEND = {
+    0: ((7, 1), (5, 2), (4, 3), (3, 4), (10, 3)),
+    3: ((8, 1), (6, 2), (5, 3), (4, 4)),
+    6: ((7, 2), (6, 3), (5, 4)),
+}
+MIDDLE = {
+    0: ((9, 1), (8, 2), (7, 3), (6, 4), (10, 4)),
+    2: ((9, 2), (8, 3), (7, 4), (11, 3)),
+    5: ((9, 3), (8, 4)),
+    7: ((9, 4),),
+    12: ((11, 4),),
+}
+EARLY = (DOWN, UP, DOWN + 1, UP + 1, DOWN + 2)
+DONE = EARLY[:4]
+EARLY_POINTS = {
+    6: ((DOWN, 0),),
+    8: ((UP, 0), (DOWN, 1)),
+    9: ((UP, 1),),
+    10: ((DOWN + 1, 0),),
+    11: ((DOWN + 1, 1),),
+    12: ((UP + 1, 0), (UP, 2)),
+    13: ((UP + 1, 1),),
+    14: ((DOWN + 2, 0), (DOWN + 1, 2), (UP, 3)),
+    15: ((DOWN + 2, 1),),
+    16: ((DOWN + 1, 3), (UP + 1, 2)),
+    17: ((DOWN, 2), (UP, 4)),
+    18: ((UP + 1, 3), (DOWN + 2, 2)),
+    19: ((DOWN, 3), (DOWN + 1, 4)),
+    20: ((DOWN, 4), (UP + 1, 4)),
+}
+LATE = (UP + 2, DOWN + 3, UP + 3, OUT, QKV, QKV + 1, QKV + 2)
+LATE_POINTS = {
+    0: ((DOWN + 2, -3), (UP + 2, 0), (DOWN + 3, 0), (UP + 3, 0)),
+    1: ((UP + 2, 1), (DOWN + 3, 1)),
+    2: ((UP + 3, 1), (OUT, 0)),
+    3: ((DOWN + 2, 3),),
+    4: ((OUT, 1), (DOWN + 3, 2)),
+    6: ((UP + 3, 2),),
+    7: ((DOWN + 3, 3),),
+    9: ((QKV, 0), (OUT, 2), (UP + 3, 3), (UP + 2, 2)),
+    10: ((QKV + 1, 0), (QKV, 1)),
+    11: ((QKV + 2, 0), (QKV + 1, 1), (OUT, 3), (DOWN + 2, 4)),
+    12: ((QKV + 2, 1), (DOWN + 3, 4)),
+    13: ((QKV, 2), (UP + 2, 3)),
+    14: ((UP + 3, 4),),
+    16: ((QKV + 1, 2), (QKV, 3)),
+    17: ((UP + 2, 4), (OUT, 4)),
+    18: ((QKV + 2, 2),),
+    20: ((QKV + 1, 3),),
+    22: ((QKV + 2, 3), (QKV, 4)),
+    24: ((QKV + 1, 4), (QKV + 2, 4)),
+}
+
+
+def reduce_stages(points):
+    moves = [move for at in sorted(points) for move in points[at]]
+    started = [(unit, 3 if stage == -3 else stage + 1) for unit, stage in moves if stage < 4]
+    return [(unit, stage) for unit, stage in started if stage > 3 or (unit, stage) in moves or stage < 3]
+
+
+def gather_stages(points):
+    return [(ORDER[index], stage) for point in points for index, stage in point]
 
 
 def window_layout(clip_frames, first_window, window_count):
@@ -105,14 +185,6 @@
     )
 
 
-def own_blocks(shares):
-    def columns(part):
-        return part.transpose(1, 0, 2).reshape(SHARE, -1)
-
-    down = shares[DOWN:].reshape(4, 2, LANES, LANES).transpose(1, 0, 2, 3).reshape(4 * SHARE, LANES)
-    return (columns(shares[QKV:OUT]), columns(shares[OUT:UP]), columns(shares[UP:DOWN]), down)
-
-
 def dot(left, right):
     return jnp.dot(left, right, preferred_element_type=F32)
 
@@ -190,7 +262,7 @@
     return root * (grad - mean - normal * along)
 
 
-def each_rows(mod_ref, live_ref, body, rows=32):
+def each_rows(mod_ref, live_ref, body, rows=32, pump=lambda window: None):
     for window in range(mod_ref.shape[0]):
         live = live_ref[window] * CELLS
 
@@ -201,6 +273,7 @@
             body(window, at, mods, slot < live)
 
         loop(WIN // rows, step)
+        pump(window)
 
 
 def add_sums(sums_ref, window, which, values):
@@ -222,13 +295,33 @@
     def far(self, k):
         return lax.rem(self.z + k, 4)
 
-    def greet(self):
-        peers = [self.at(z=self.far(k)) for k in (1, 2, 3)]
-        peers += [self.at(x=1 - self.x), self.at(y=1 - self.y), self.at(c=1 - self.c)]
+    def shifted(self, dz, dx, dy, dc):
+        def other(index, change):
+            return 1 - index if change else index
+
+        return self.at(self.far(dz), other(self.x, dx), other(self.y, dy), other(self.c, dc))
+
+    def greet(self, far_ones=()):
+        near = [(1, 0, 0, 0), (2, 0, 0, 0), (3, 0, 0, 0), (0, 1, 0, 0), (0, 0, 1, 0), (0, 0, 0, 1)]
+        peers = near + [change for change in far_ones if change not in near]
         barrier = pltpu.get_barrier_semaphore()
-        for peer in peers:
-            pl.semaphore_signal(barrier, inc=1, device_id=peer, device_id_type=MESH)
+        for change in peers:
+            pl.semaphore_signal(
+                barrier, inc=1, device_id=self.shifted(*change), device_id_type=MESH
+            )
         pl.semaphore_wait(barrier, len(peers))
+
+
+EVERYONE = [
+    (dz, dx, dy, dc)
+    for dz in range(4)
+    for dx in range(2)
+    for dy in range(2)
+    for dc in range(2)
+    if (dz, dx, dy, dc) != (0, 0, 0, 0)
+]
+ALONG_ZX = [change for change in EVERYONE if change[2:] == (0, 0)]
+ALONG_YC = [change for change in EVERYONE if change[:2] == (0, 0)]
 
 
 class Moves:
@@ -238,12 +331,12 @@
         self.first, count = {}, 0
         for unit, stage in stages:
             self.first[unit, stage] = count
-            count += self.counts[unit in SIDEWAYS][stage - 1]
+            count += self.counts[unit in self.aside][stage - 1]
         self.flying = []
 
     @classmethod
     def semaphores(cls, stages):
-        count = sum(cls.counts[unit in SIDEWAYS][stage - 1] for unit, stage in stages)
+        count = sum(cls.counts[unit in cls.aside][stage - 1] for unit, stage in stages)
         return [pltpu.SemaphoreType.DMA((count,))] * 2
 
     def made(self, unit, stage, moves):
@@ -280,7 +373,8 @@
 
 
 class Gather(Moves):
-    counts = ((3, 2, 2, 1), (2, 6, 2, 1))
+    counts = ((3, 2, 2, 1), (2, 2, 3, 1))
+    aside = GATHER_ASIDE
 
     def __init__(self, place, held, stages, scratch):
         super().__init__(place, stages, scratch)
@@ -292,25 +386,27 @@
         own = held.at[p.z, p.x, p.y, p.c]
         if stage == 4:
             refs = [(held.at[:, :, :, p.c], at_core)]
-        elif stage == 3:
+        elif unit in self.aside and stage == 1:
+            refs = [(own.at[:HALF], at_x), (own.at[HALF:], at_y)]
+        elif unit in self.aside and stage == 2:
+            refs = [
+                (held.at[p.z, :, p.y, p.c, :HALF], at_y),
+                (held.at[p.z, p.x, :, p.c, HALF:], at_x),
+            ]
+        elif unit in self.aside:
+            refs = [(held.at[p.z, :, :, p.c], p.at(z=p.far(k))) for k in (1, 2, 3)]
+        elif stage == 1:
+            refs = [(own, p.at(z=p.far(k))) for k in (1, 2, 3)]
+        elif stage == 2:
+            refs = [
+                (held.at[:, p.x, p.y, p.c, :HALF], at_x),
+                (held.at[:, p.x, p.y, p.c, HALF:], at_y),
+            ]
+        else:
             refs = [
                 (held.at[:, :, p.y, p.c, :HALF], at_y),
                 (held.at[:, p.x, :, p.c, HALF:], at_x),
             ]
-        elif unit in SIDEWAYS and stage == 1:
-            refs = [(own.at[:HALF], at_x), (own.at[HALF:], at_y)]
-        elif unit in SIDEWAYS:
-            refs = []
-            for k in (1, 2, 3):
-                refs.append((held.at[p.z, :, p.y, p.c, :HALF], p.at(z=p.far(k))))
-                refs.append((held.at[p.z, p.x, :, p.c, HALF:], p.at(z=p.far(k))))
-        elif stage == 1:
-            refs = [(own, p.at(z=p.far(k))) for k in (1, 2, 3)]
-        else:
-            refs = [
-                (held.at[:, p.x, p.y, p.c, :HALF], at_x),
-                (held.at[:, p.x, p.y, p.c, HALF:], at_y),
-            ]
         return self.made(unit, stage, [(ref, ref, device) for ref, device in refs])
 
     def advance(self, unit, stage):
@@ -324,54 +420,72 @@
 
 
 class Reduce(Moves):
-    counts = ((1, 2, 2, 3), (1, 2, 6, 2))
-
-    def __init__(self, place, part, total, units, scratch):
-        stages = [(unit, stage) for unit in units for stage in (1, 2, 3, 4)]
-        super().__init__(place, stages, scratch[6:])
-        self.part, self.total, self.units = part, total, units
-        self.own, self.core, self.side, self.corner, self.distant, self.load = scratch[:6]
+    counts = ((1, 2, 2, 3), (1, 3, 2, 2))
+    aside = REDUCE_ASIDE
+
+    def __init__(self, place, part, points, store, buffers, scratch):
+        super().__init__(place, reduce_stages(points), scratch[2:])
+        self.part, self.store, self.buffers = part, store, buffers
+        self.own, self.load = scratch[:2]
+        self.slots, self.loaded = {}, []
 
     @classmethod
-    def scratch(cls, units):
-        count = len(units)
+    def scratch(cls, points):
         return [
             pltpu.VMEM((OWN_SLOTS, 4, 2, 2, SHARE, LANES), BF16),
-            pltpu.VMEM((count, 4, 2, 2, SHARE, LANES), BF16),
-            pltpu.VMEM((count, 2, 4, 2, HALF, LANES), BF16),
-            pltpu.VMEM((count, 2, 4, HALF, LANES), BF16),
-            pltpu.VMEM((count, 3, 2, 2, HALF, LANES), BF16),
             pltpu.SemaphoreType.DMA((OWN_SLOTS,)),
-        ] + cls.semaphores([(unit, stage) for unit in units for stage in (1, 2, 3, 4)])
+        ] + cls.semaphores(reduce_stages(points))
+
+    @staticmethod
+    def core_shape(count):
+        return (count, 4, 2, 2, SHARE, LANES)
+
+    @staticmethod
+    def side_shape(count):
+        return (count, 2, 4, 2, HALF, LANES)
+
+    @staticmethod
+    def corner_shape(count):
+        return (count, 2, 4, HALF, LANES)
+
+    @staticmethod
+    def distant_shape(count):
+        return (count, 3, 2, HALF, LANES)
+
+    @staticmethod
+    def aside_shape(count):
+        return (count, 3, 2, 2, SHARE, LANES)
 
     def own_copy(self, unit):
-        slot = self.units.index(unit) % OWN_SLOTS
+        slot = self.slots.setdefault(unit, len(self.slots) % OWN_SLOTS)
         return pltpu.make_async_copy(
             self.part(unit).at[:, :, :, self.place.c], self.own.at[slot], self.load.at[slot]
         )
 
     def copies(self, unit, stage):
-        p, index = self.place, self.units.index(unit)
+        p = self.place
         at_x, at_y, at_core = p.at(x=1 - p.x), p.at(y=1 - p.y), p.at(c=1 - p.c)
-        core, side, corner = self.core.at[index], self.side.at[index], self.corner.at[index]
-        distant = self.distant.at[index]
-        if stage == 1:
+        core, side, corner, distant = self.buffers(unit)
+        if unit in self.aside and stage == 2:
+            moves = [
+                (core.at[p.far(k)], distant.at[k - 1], p.at(z=p.far(k))) for k in (1, 2, 3)
+            ]
+        elif unit in self.aside and stage == 3:
+            moves = [
+                (core.at[p.z, :, 1 - p.y, :HALF], side.at[0, 0], at_y),
+                (core.at[p.z, 1 - p.x, :, HALF:], side.at[1, 0], at_x),
+            ]
+        elif unit in self.aside and stage == 4:
+            moves = [
+                (side.at[0, 0, 1 - p.x], side.at[0, 1, 0], at_x),
+                (side.at[1, 0, 1 - p.y], side.at[1, 1, 0], at_y),
+            ]
+        elif stage == 1:
             moves = [(self.part(unit).at[:, :, :, 1 - p.c], core, at_core)]
         elif stage == 2:
             moves = [
                 (core.at[:, :, 1 - p.y, :HALF], side.at[0], at_y),
                 (core.at[:, 1 - p.x, :, HALF:], side.at[1], at_x),
-            ]
-        elif unit in SIDEWAYS and stage == 3:
-            moves = []
-            for k in (1, 2, 3):
-                for half in range(2):
-                    source = side.at[half, p.far(k)]
-                    moves.append((source, distant.at[k - 1, half], p.at(z=p.far(k))))
-        elif unit in SIDEWAYS:
-            moves = [
-                (corner.at[0, 1 - p.x], corner.at[0, 2], at_x),
-                (corner.at[1, 1 - p.y], corner.at[1, 2], at_y),
             ]
         elif stage == 3:
             moves = [
@@ -380,8 +494,7 @@
             ]
         else:
             moves = [
-                (corner.at[:, p.far(k)], distant.at[k - 1, 0], p.at(z=p.far(k)))
-                for k in (1, 2, 3)
+                (corner.at[:, p.far(k)], distant.at[k - 1], p.at(z=p.far(k))) for k in (1, 2, 3)
             ]
         return self.made(unit, stage, moves)
 
@@ -389,18 +502,19 @@
         super().begin(unit, stage)
         if stage == 1:
             self.own_copy(unit).start()
+            assert self.slots[unit] not in self.loaded
+            self.loaded.append(self.slots[unit])
 
     def combine(self, unit, stage):
-        p, index = self.place, self.units.index(unit)
-        core, side, corner = self.core.at[index], self.side.at[index], self.corner.at[index]
-        distant = self.distant.at[index]
+        p = self.place
+        core, side, corner, distant = self.buffers(unit)
 
         def plus(left, right):
             return (left.astype(F32) + right.astype(F32)).astype(BF16)
 
         def from_core(step):
             z, x, y = step // 4, step // 2 % 2, step % 2
-            core[z, x, y] = plus(core[z, x, y], self.own[index % OWN_SLOTS, z, x, y])
+            core[z, x, y] = plus(core[z, x, y], self.own[self.slots[unit], z, x, y])
 
         def from_side(step):
             z, b = step // 2, step % 2
@@ -414,95 +528,42 @@
         def from_far(half):
             total = corner[half, p.z].astype(F32)
             for k in range(3):
-                total = total + distant[k, 0, half].astype(F32)
-            self.total[index, pl.ds(pl.multiple_of(half * HALF, HALF), HALF), :] = total
-
-        def sideways_far(half):
-            for b in range(2):
-                total = side[half, p.z, b].astype(F32)
-                for k in range(3):
-                    total = total + distant[k, half, b].astype(F32)
-                corner[half, b] = total.astype(BF16)
-
-        def sideways_last():
-            self.total[index, :HALF, :] = corner[0, p.x].astype(F32) + corner[0, 2].astype(F32)
-            self.total[index, HALF:, :] = corner[1, p.y].astype(F32) + corner[1, 2].astype(F32)
-
-        if unit in SIDEWAYS and stage == 3:
-            loop(2, sideways_far)
-        elif unit in SIDEWAYS and stage == 4:
-            sideways_last()
-        else:
-            steps = {1: (16, from_core), 2: (8, from_side), 3: (4, from_corner), 4: (2, from_far)}
-            loop(*steps[stage])
-
-    def advance(self, unit, stage):
+                total = total + distant[k, half].astype(F32)
+            self.store(unit, half, total)
+
+        def aside_far(step):
+            x, y = step // 2, step % 2
+            total = core[p.z, x, y].astype(F32)
+            for k in range(3):
+                total = total + distant[k, x, y].astype(F32)
+            core[p.z, x, y] = total.astype(BF16)
+
+        def aside_side(b):
+            side[0, 0, b] = plus(side[0, 0, b], core[p.z, b, p.y, :HALF])
+            side[1, 0, b] = plus(side[1, 0, b], core[p.z, p.x, b, HALF:])
+
+        if unit in self.aside and stage == 4:
+            for part, own in enumerate((p.x, p.y)):
+                total = side[part, 0, own].astype(F32) + side[part, 1, 0].astype(F32)
+                self.store(unit, part, total)
+            return
+        steps = {1: (16, from_core), 2: (8, from_side), 3: (4, from_corner), 4: (2, from_far)}
+        if unit in self.aside:
+            steps |= {2: (4, aside_far), 3: (2, aside_side)}
+        loop(*steps[stage])
+
+    def step(self, unit, stage):
+        if stage <= 0:
+            self.begin(unit, max(1, -stage))
+            return
         self.arrive(unit, stage)
         if stage == 1:
             self.own_copy(unit).wait()
         self.combine(unit, stage)
-        if stage < 4:
+        if stage == 1:
+            self.loaded.remove(self.slots[unit])
+        if (unit, stage + 1) in self.first:
             self.begin(unit, stage + 1)
-
-
-class Small:
-    def __init__(self, place, values, scratch):
-        self.place, self.values = place, values
-        self.from_core, self.from_x, self.from_y, self.from_z, self.send, self.recv = scratch
-
-    @staticmethod
-    def scratch(rows):
-        return [
-            pltpu.VMEM((4, 2, rows, LANES), F32),
-            pltpu.VMEM((4, rows, LANES), F32),
-            pltpu.VMEM((4, rows, LANES), F32),
-            pltpu.VMEM((3, rows, LANES), F32),
-            pltpu.SemaphoreType.DMA((6,)),
-            pltpu.SemaphoreType.DMA((6,)),
-        ]
-
-    def copies(self, stage):
-        p, values = self.place, self.values
-
-        def copy(slot, source, target, device):
-            return pltpu.make_async_remote_copy(
-                src_ref=source,
-                dst_ref=target,
-                send_sem=self.send.at[slot],
-                recv_sem=self.recv.at[slot],
-                device_id=device,
-                device_id_type=MESH,
-            )
-
-        if stage == 1:
-            return [copy(0, values, self.from_core, p.at(c=1 - p.c))]
-        if stage == 2:
-            return [copy(1, values.at[:, 1 - p.x], self.from_x, p.at(x=1 - p.x))]
-        if stage == 3:
-            return [copy(2, values.at[:, p.x], self.from_y, p.at(y=1 - p.y))]
-        return [
-            copy(2 + k, values.at[p.far(k), p.x], self.from_z.at[k - 1], p.at(z=p.far(k)))
-            for k in (1, 2, 3)
-        ]
-
-    def start(self, stage):
-        for copy in self.copies(stage):
-            copy.start()
-
-    def advance(self, stage):
-        p, values = self.place, self.values
-        for copy in self.copies(stage):
-            copy.wait()
-        if stage == 1:
-            values[...] += self.from_core[...]
-        elif stage == 2:
-            values[:, p.x] += self.from_x[...]
-        elif stage == 3:
-            values[:, p.x] += self.from_y[...]
-        else:
-            return values[p.z, p.x] + self.from_z[0] + self.from_z[1] + self.from_z[2]
-        self.start(stage + 1)
-        return None
 
 
 class Copies:
@@ -566,40 +627,6 @@
     return out
 
 
-SPLIT = (4, 2, 2, 2, SHARE, LANES)
-MOD_ROWS = 48
-OWN_SLOTS = 4
-ORDER = (0, 1, 2, 3, 4, 8, 5, 9, 6, 10, 7, 11)
-SIDEWAYS = ()
-ENTER = (
-    ((0, 1),),
-    ((1, 1), (0, 2)),
-    ((2, 1), (1, 2), (0, 3)),
-    ((3, 1), (2, 2), (1, 3), (0, 4)),
-    ((4, 1), (3, 2), (2, 3), (1, 4)),
-    ((5, 1), (4, 2), (3, 3), (2, 4)),
-)
-ATTEND = {
-    0: ((6, 1), (5, 2), (4, 3), (3, 4)),
-    3: ((7, 1), (6, 2), (5, 3), (4, 4)),
-    6: ((8, 1), (7, 2), (6, 3), (5, 4)),
-}
-MIDDLE = {
-    0: ((9, 1), (8, 2), (7, 3), (6, 4)),
-    2: ((10, 1), (9, 2), (8, 3), (7, 4)),
-    5: ((11, 1), (10, 2), (9, 3), (8, 4)),
-    7: ((11, 2), (10, 3), (9, 4)),
-    9: ((11, 3), (10, 4)),
-    11: ((11, 4),),
-}
-EARLY = (DOWN, UP, DOWN + 1)
-LATE = (UP + 1, DOWN + 2, UP + 2, DOWN + 3, UP + 3, OUT, QKV, QKV + 1, QKV + 2)
-
-
-def gather_stages(points):
-    return [(ORDER[index], stage) for point in points for index, stage in point]
-
-
 def enter_norm(refs):
     rows = 32
     for window in range(refs.mod.shape[0]):
@@ -632,11 +659,76 @@
         enter_unit(refs, j, refs.held.at[QKV + j])
 
 
+def act_rows(refs, place):
+    first = (place.y * 2 + place.c) * SHARE
+    value = refs.condition[:, pl.ds(pl.multiple_of(first, SHARE), SHARE)]
+    act = value / (1.0 + jnp.exp(-value))
+    return jnp.concatenate([act, jnp.zeros((8 - value.shape[0], SHARE), F32)], axis=0).astype(BF16)
+
+
+def enter_layout(refs):
+    windows, clips = refs.member.shape[0], refs.condition.shape[0]
+    frames = [refs.frames[clip] for clip in range(clips)]
+    starts = [0]
+    for count in frames:
+        starts.append(starts[-1] + 1 + jnp.where(count > WT, 1, 0))
+    device = lax.axis_index("dp") * lax.axis_size("fsdp") + lax.axis_index("fsdp")
+    refs.member[...] = jnp.zeros_like(refs.member)
+    for window in range(windows):
+        slab = (device * windows + window) // SPW
+        live = 0
+        for clip in range(clips):
+            mine = starts[clip] <= slab
+            if clip < clips - 1:
+                mine = mine & (slab < starts[clip + 1])
+            inner = frames[clip] - WT * (slab - starts[clip])
+            live = live + jnp.where(mine, jnp.minimum(inner, WT), 0)
+            refs.member[window, clip : clip + 1, :] = jnp.full(
+                (1, LANES), jnp.where(mine, 1.0, 0.0), F32
+            )
+        refs.live[window] = live
+
+
+def enter_table(refs):
+    refs.rows[...] = jnp.zeros_like(refs.rows)
+    table = refs.rel_table[...].astype(F32)
+    for head in range(2):
+        for frame in range(FRAMES):
+            first = (FRAMES - 1 - frame) * OFFSETS
+            row = head * (SPREAD // WSIDE) + frame
+            refs.rows[row : row + 1, :OFFSETS] = table[head : head + 1, first : first + OFFSETS]
+    shape_of = (TILE, WSIDE * LANES)
+    offset = lax.broadcasted_iota(jnp.int32, shape_of, 0)
+    place = lax.broadcasted_iota(jnp.int32, shape_of, 1)
+    own, row, other = place // LANES, place // WSIDE % (LANES // WSIDE), place % WSIDE
+    side_span = 2 * WSIDE - 1
+    row_diff, col_diff = side_span - 1 - row, own - other + (WSIDE - 1)
+    same = (row < side_span) & (row_diff * side_span + col_diff == offset)
+    spread = dot(refs.rows[...].astype(BF16), jnp.where(same, 1.0, 0.0).astype(BF16))
+    count = 2 * SPREAD // WSIDE
+    for own in range(WSIDE):
+        refs.spread[pl.ds(own, count, stride=WSIDE), :] = spread[
+            :count, own * LANES : (own + 1) * LANES
+        ]
+    for head in range(2):
+        refs.table_own[head] = refs.spread[head * SPREAD : (head + 1) * SPREAD, :].astype(BF16)
+
+
 def enter_kernel(refs):
     place = Place()
-    place.greet()
+    place.greet(ALONG_ZX + ALONG_YC)
     z, x, y, c = place.z, place.x, place.y, place.c
-
+    small = Copies(*refs.small)
+    mods = dot(act_rows(refs, place), refs.ada[...])
+    mods = mods + jnp.where((y == 0) & (c == 0), 1.0, 0.0) * refs.bias[...].astype(F32)
+    for block in range(6):
+        refs.mod_part[block * CLIP_ROWS : (block + 1) * CLIP_ROWS, :] = mods[
+            :CLIP_ROWS, block * LANES : (block + 1) * LANES
+        ]
+    refs.mod_parts[y, c] = refs.mod_part[...]
+    parts = [
+        small(refs.mod_part, refs.mod_parts.at[y, c], place.shifted(*change)) for change in ALONG_YC
+    ]
     own = []
     for unit in range(UNITS):
         if unit >= DOWN:
@@ -663,42 +755,39 @@
         for index, stage in points.pop(0):
             work.advance(ORDER[index], stage)
 
-    small = Copies(*refs.small)
-    copy = small(refs.mod_part, refs.from_core, place.at(c=1 - c))
-    for one in own:
+    own[0].wait()
+    tick()
+    enter_layout(refs)
+    enter_table(refs)
+    refs.table[z, x, c] = refs.table_own[c]
+    for copy in parts:
+        copy.wait()
+    refs.mods[z, x] = (
+        refs.mod_parts[0, 0] + refs.mod_parts[0, 1] + refs.mod_parts[1, 0] + refs.mod_parts[1, 1]
+    )
+    mods = [
+        small(refs.mods.at[z, x], refs.mods.at[z, x], place.shifted(*change))
+        for change in ALONG_ZX
+    ]
+    for one in own[1:]:
         one.wait()
     tick()
-    refs.table[z, x, c] = refs.table_own[c]
-    copy.wait()
-    refs.mod_sum[...] = refs.mod_part[...] + refs.from_core[...]
-    copy = small(refs.mod_sum, refs.from_y, place.at(y=1 - y))
-    copy.wait()
-    refs.mods[z, x] = refs.mod_sum[...] + refs.from_y[...]
-    copies = [
-        small(refs.mods.at[z, x], refs.mods.at[z, x], place.at(x=1 - x)),
-        small(refs.table.at[z, x, c], refs.table.at[z, x, c], place.at(x=1 - x)),
-    ]
-    copies[0].wait()
-    mods = [
-        small(refs.mods.at[z], refs.mods.at[z], place.at(z=place.far(k))) for k in (1, 2, 3)
-    ]
-    tick()
-    copies[1].wait()
     tick()
     for copy in mods:
         copy.wait()
     for window in range(refs.mod.shape[0]):
         for block in range(48):
             which, column = divmod(block, 8)
-            part = refs.mods[block // 12, block // 6 % 2, block % 6 * 8 : block % 6 * 8 + 8, :]
+            first = block % 6 * CLIP_ROWS
+            part = refs.mods[block // 12, block // 6 % 2, first : first + CLIP_ROWS, :]
             refs.mod[window, which : which + 1, column * LANES : (column + 1) * LANES] = jnp.sum(
                 part * refs.member[window], axis=0, keepdims=True
             )
     enter_norm(refs)
     tick()
     tables = [
-        small(refs.table.at[z, :, c], refs.table.at[z, :, c], place.at(z=place.far(k)))
-        for k in (1, 2, 3)
+        small(refs.table.at[z, x, c], refs.table.at[z, x, c], place.shifted(*change))
+        for change in ALONG_ZX
     ]
     work.arrive(QKV, 4)
     enter_unit(refs, 0, refs.held.at[QKV])
@@ -832,17 +921,26 @@
         place = Place()
         place.greet()
         gathering = Gather(place, refs.held_out, gather_stages(MIDDLE.values()), refs.gather)
-        reducing = Reduce(place, lambda unit: refs.part.at[unit], refs.total, EARLY, refs.reduce)
+
+        def buffers(unit):
+            index = EARLY.index(unit)
+            core, side = refs.core.at[index], refs.side.at[index]
+            if unit in REDUCE_ASIDE:
+                return core, side, None, refs.aside.at[0]
+            if unit not in DONE:
+                return core, side, None, None
+            return core, side, refs.corner.at[index], refs.distant.at[index]
+
+        def store(unit, part, values):
+            at = pl.ds(pl.multiple_of(part * HALF, HALF), HALF)
+            refs.total[DONE.index(unit), at, :] = values
+
+        reducing = Reduce(
+            place, lambda unit: refs.part.at[unit], EARLY_POINTS, store, buffers, refs.reduce
+        )
         for stages in MIDDLE.values():
             waiting |= {ORDER[index] for index, stage in stages if stage == 4}
-        for unit, times in zip(
-            EARLY, ((7, 9, 13, 16, 19), (9, 11, 15, 18, 20), (11, 13, 17, 20, 21)), strict=True
-        ):
-            points.setdefault(times[0], []).append(functools.partial(reducing.begin, unit, 1))
-            for stage in (1, 2, 3, 4):
-                points.setdefault(times[stage], []).append(
-                    functools.partial(reducing.advance, unit, stage)
-                )
+        points = {at: list(moves) for at, moves in EARLY_POINTS.items()}
 
     held = refs.held_out if gathering is not None else refs.held
     count = [0]
@@ -852,8 +950,8 @@
             gathering.advance(ORDER[index], stage)
             if stage == 4:
                 waiting.discard(ORDER[index])
-        for action in points.pop(count[0], []):
-            action()
+        for unit, stage in points.pop(count[0], ()):
+            reducing.step(unit, stage)
         count[0] += 1
 
     def fetch(step):
@@ -1002,7 +1100,7 @@
     loop(2, back)
 
 
-def leave_norm(refs):
+def leave_norm(refs, pump=lambda window: None):
     def join(window, at, mods, live):
         normal, root = centered(refs.tokens[at, :].astype(F32))
         grad_normed = refs.grad_normed[at, :]
@@ -1012,7 +1110,7 @@
         add_sums(refs.sums, window, 0, grad_normed)
         add_sums(refs.sums, window, 1, grad_normed * normal)
 
-    each_rows(refs.mod, refs.live, join)
+    each_rows(refs.mod, refs.live, join, pump=pump)
 
 
 def back_plain_kernel(refs):
@@ -1038,52 +1136,103 @@
         leave_norm(refs)
 
 
+def fold_spreads(refs):
+    heads = H * WIDE // WSIDE
+    shape_of = (WSIDE * LANES, TILE)
+    place = lax.broadcasted_iota(jnp.int32, shape_of, 0)
+    offset = lax.broadcasted_iota(jnp.int32, shape_of, 1)
+    own, row, other = place // LANES, place // WSIDE % (LANES // WSIDE), place % WSIDE
+    side_span = 2 * WSIDE - 1
+    row_diff, col_diff = side_span - 1 - row, own - other + (WSIDE - 1)
+    same = (row < side_span) & (row_diff * side_span + col_diff == offset)
+    onto = jnp.where(same, 1.0, 0.0).astype(BF16)
+    left = jnp.concatenate(
+        [refs.spreads[pl.ds(own, heads, stride=WSIDE), :] for own in range(WSIDE)], axis=1
+    )
+    total = jnp.zeros((heads, TILE), F32)
+    for _ in range(3):
+        low = left.astype(BF16)
+        total = total + dot(low, onto)
+        left = left - low.astype(F32)
+    rows = 2 * WIDE // WSIDE
+    for block in range(8):
+        refs.table[block // 2, block % 2] = total[block * rows : (block + 1) * rows]
+
+
 def back_kernel(refs):
     place = Place()
     z, x, y, c = place.z, place.x, place.y, place.c
     step = pl.program_id(0)
+
+    def buffers(unit):
+        every = (EARLY + LATE).index(unit)
+        late = every - len(EARLY)
+        if late < 0:
+            core, side = None, refs.side_in.at[every]
+        else:
+            core, side = refs.core.at[late], refs.side.at[late]
+        if unit in REDUCE_ASIDE:
+            return core, side, None, refs.aside.at[0]
+        return core, side, refs.corner.at[every], refs.distant.at[every]
+
+    def store(unit, part, values):
+        if unit >= DOWN:
+            first = part * 512 + (unit - DOWN) * LANES
+            refs.grad_down[pl.ds(pl.multiple_of(first, LANES), LANES), :] = values
+            return
+        target, start = (
+            (refs.grad_qkv, QKV)
+            if unit < OUT
+            else (refs.grad_out, OUT)
+            if unit < UP
+            else (refs.grad_up, UP)
+        )
+        column = (unit - start) * LANES
+        target[pl.ds(pl.multiple_of(part * HALF, HALF), HALF), column : column + LANES] = values
+
     work = Reduce(
         place,
         lambda unit: refs.made.at[unit] if unit < OUT else refs.part.at[unit],
-        refs.total,
-        LATE,
+        LATE_POINTS,
+        store,
+        buffers,
         refs.reduce,
     )
-    table = Small(place, refs.table, refs.table_small)
-    clip = Small(place, refs.clip, refs.clip_small)
-
-    events = []
-    for index, unit in enumerate(LATE):
-        start = max(0, 2 * index - 2) if unit >= OUT else 9 + unit
-        events.append((start, 0, functools.partial(work.begin, unit, 1)))
-        for stage in (1, 2, 3, 4):
-            time = max(1 + 2 * index, start + 1) + 3 * (stage - 1)
-            events.append((time, stage, functools.partial(work.advance, unit, stage)))
-    events.sort(key=lambda event: event[:2])
+    small = Copies(*refs.small)
+
+    events = [(at, move) for at in sorted(LATE_POINTS) for move in LATE_POINTS[at]]
 
     def run(until):
         while events and events[0][0] < until:
-            events.pop(0)[2]()
+            work.step(*events.pop(0)[1])
 
     for number in range(H // 2):
 
         @pl.when(step == number)
         def _(number=number):
             if number == 0:
-                place.greet()
+                place.greet(EVERYONE)
             run(number + 1)
 
     @pl.when(step < H // 2)
     def _():
         pair = jnp.minimum(step, H // 2 - 1)
         attend_back_pair(refs, pair)
-        refs.table[lax.div(pair, 2), lax.rem(pair, 2)] = refs.spread[...].reshape(
-            2 * SPREAD, LANES
-        )
+        for head in range(2):
+            at = pl.ds(pl.multiple_of((pair * 2 + head) * WIDE, WIDE), WIDE)
+            refs.spreads[at, :] = refs.spread[head]
 
     @pl.when(step == H // 2)
     def _():
-        table.start(1)
+        for index, unit in enumerate(DONE):
+            for part in range(2):
+                store(unit, part, refs.done[index, part * HALF : (part + 1) * HALF, :])
+        fold_spreads(refs)
+        table = []
+        for dz, dx, dy, dc in ALONG_ZX:
+            source = refs.table.at[place.far(dz), 1 - x if dx else x]
+            table.append(small(source, refs.table_zx.at[z, x], place.shifted(dz, dx, dy, dc)))
+        refs.table_zx[z, x] = refs.table[z, x]
         refs.sums[...] = refs.late_sums[...]
         refs.grad_normed[...] = jnp.zeros_like(refs.grad_normed)
 
@@ -1096,72 +1245,117 @@
         run(10)
         leave_weight(refs, 1, refs.made.at[1])
         run(11)
-        table.advance(1)
         leave_weight(refs, 2, refs.made.at[2])
         run(12)
         fetch(0).wait()
         leave_back(refs, 0)
         fetch(1).start()
         run(13)
-        table.advance(2)
         fetch(1).wait()
         leave_back(refs, 1)
         fetch(2).start()
         run(14)
-        table.advance(3)
         fetch(2).wait()
         leave_back(refs, 2)
         run(15)
-        leave_norm(refs)
+        leave_norm(refs, lambda window: run(17 + window))
+        for copy in table:
+            copy.wait()
+        total = refs.table_zx[0, 0]
+        for block in range(1, 8):
+            total = total + refs.table_zx[block // 2, block % 2]
+        refs.table_own[...] = total
+        refs.table_yc[y, c] = total
+        table = [
+            small(refs.table_own, refs.table_yc.at[y, c], place.shifted(*change))
+            for change in ALONG_YC
+        ]
         for block in range(48):
             which, column = divmod(block, 8)
-            part = jnp.zeros((8, LANES), F32)
+            part = jnp.zeros((CLIP_ROWS, LANES), F32)
             for window in range(refs.mod.shape[0]):
                 sums = refs.sums[window, which : which + 1, column * LANES : (column + 1) * LANES]
                 part = part + refs.member[window] * sums
-            refs.clip[block // 12, block // 6 % 2, block % 6 * 8 : block % 6 * 8 + 8, :] = part
-        clip.start(1)
-        run(17)
-        clip.advance(1)
-        refs.table_total[...] = table.advance(4)
-        run(18)
-        clip.advance(2)
+            first = block % 6 * CLIP_ROWS
+            refs.clip[block // 12, block // 6 % 2, first : first + CLIP_ROWS, :] = part
+        copies = []
+        for dz, dx, dy, dc in ALONG_ZX:
+            source = refs.clip.at[place.far(dz), 1 - x if dx else x]
+            copies.append(small(source, refs.clip_zx.at[z, x], place.shifted(dz, dx, dy, dc)))
+        refs.clip_zx[z, x] = refs.clip[z, x]
         run(19)
-        clip.advance(3)
-        run(20)
-        total = clip.advance(4)
-        refs.clip_total[...] = total
-        low = total.astype(BF16)
+        for copy in copies:
+            copy.wait()
+        total = refs.clip_zx[0, 0]
+        for block in range(1, 8):
+            total = total + refs.clip_zx[block // 2, block % 2]
+        refs.clip_own[...] = total
+        refs.clip_yc[y, c] = total
+        copies = [
+            small(refs.clip_own, refs.clip_yc.at[y, c], place.shifted(*change))
+            for change in ALONG_YC
+        ]
+        run(21)
+        for copy in copies:
+            copy.wait()
+        total = refs.clip_yc[0, 0] + refs.clip_yc[0, 1] + refs.clip_yc[1, 0] + refs.clip_yc[1, 1]
+        total = jnp.concatenate([total, jnp.zeros((8, LANES), F32)], axis=0)
         cond = jnp.zeros((8, SHARE), F32)
+        lows = []
         for block in range(6):
-            cond = cond + dot_rows(
-                low[block * 8 : block * 8 + 8], refs.ada[:, block * LANES : (block + 1) * LANES]
+            lows.append(total[block * CLIP_ROWS : block * CLIP_ROWS + 8].astype(BF16))
+            lanes = slice(block * LANES, (block + 1) * LANES)
+            cond = cond + dot_rows(lows[-1], refs.ada[:, lanes])
+        clips = refs.condition.shape[0]
+        refs.cond_own[...] = jnp.zeros_like(refs.cond_own)
+        for row in range(2 * clips):
+            clip, side = divmod(row, 2)
+            refs.cond_own[row : row + 1, :] = cond[
+                clip : clip + 1, side * LANES : (side + 1) * LANES
+            ]
+        refs.cond_all[z, x, y, c] = refs.cond_own[...]
+        copies = [
+            small(refs.cond_own, refs.cond_all.at[z, x, y, c], place.shifted(*change))
+            for change in EVERYONE
+        ]
+        for block, low in enumerate(lows):
+            lanes = slice(block * LANES, (block + 1) * LANES)
+            refs.grad_ada[:, lanes] = dot_tokens(act_rows(refs, place), low)
+            refs.grad_bias[block : block + 1, :] = jnp.sum(
+                low[:CLIP_ROWS].astype(F32), axis=0, keepdims=True
             )
-        small = Copies(*refs.cond_small)
-        refs.cond[y, c] = cond
-        copy = small(refs.cond.at[y, c], refs.cond.at[y, c], place.at(c=1 - c))
-        run(21)
-        copy.wait()
-        copy = small(refs.cond.at[y], refs.cond.at[y], place.at(y=1 - y))
-        run(22)
-        copy.wait()
-        copy = small(refs.cond, refs.cond_x, place.at(x=1 - x))
         run(23)
-        copy.wait()
-        refs.cond_z[z] = refs.cond[...] + refs.cond_x[...]
-        copies = [
-            small(refs.cond_z.at[z], refs.cond_z.at[z], place.at(z=place.far(k)))
-            for k in (1, 2, 3)
-        ]
+        for copy in table:
+            copy.wait()
+        total = refs.table_yc[0, 0] + refs.table_yc[0, 1] + refs.table_yc[1, 0] + refs.table_yc[1, 1]
+        for head in range(2):
+            for frame in range(FRAMES):
+                first = (FRAMES - 1 - frame) * OFFSETS
+                row = head * (WIDE // WSIDE) + frame
+                refs.table_total[head : head + 1, first : first + OFFSETS] = total[
+                    row : row + 1, :OFFSETS
+                ]
         run(100)
         for copy in copies:
             copy.wait()
-        refs.cond_total[...] = refs.cond_z[0] + refs.cond_z[1] + refs.cond_z[2] + refs.cond_z[3]
+        for block in range(4):
+            total = refs.cond_all[0, 0, block // 2, block % 2]
+            for other in range(1, 8):
+                total = total + refs.cond_all[other // 2, other % 2, block // 2, block % 2]
+            for row in range(2 * clips):
+                clip, side = divmod(row, 2)
+                first = block * SHARE + side * LANES
+                value = refs.condition[clip : clip + 1, first : first + LANES]
+                gate = 1.0 / (1.0 + jnp.exp(-value))
+                refs.grad_condition[clip : clip + 1, first : first + LANES] = (
+                    total[row : row + 1] * gate * (1.0 + value * (1.0 - gate))
+                )
         work.sent()
 
 
-def enter(special, tokens, held, mod, own, mod_part, member, table):
+def enter(special, tokens, held, mod, own, smalls):
     rows = tokens.shape[0]
+    windows = rows // WIN
     inputs = {"tokens": (tokens, vmem())}
     outputs = {
         "normed": (shape(BF16, rows, D), vmem()),
@@ -1175,28 +1369,53 @@
         return out
     for name, block in zip(("qkv", "out", "up", "down"), own, strict=True):
         inputs[name] = (block, vmem())
-    inputs |= {
-        "mod_part": (mod_part, vmem()),
-        "member": (member, vmem()),
-        "table_own": (table, vmem()),
-    }
+    for name, array in zip(("condition", "ada", "bias", "rel_table"), smalls[1:], strict=True):
+        inputs[name] = (array, vmem())
+    inputs["frames"] = (smalls[0], smem())
     outputs |= {
         "held": (shape(BF16, UNITS, *SPLIT), anywhere()),
-        "mod": (shape(F32, member.shape[0], 8, D), vmem()),
-        "table": (shape(BF16, 4, 2, *table.shape), vmem()),
+        "mod": (shape(F32, windows, 8, D), vmem()),
+        "table": (shape(BF16, 4, 2, 2, SPREAD, LANES), vmem()),
+        "member": (shape(F32, windows, CLIP_ROWS, LANES), vmem()),
+        "live": (shape(jnp.int32, windows), smem()),
     }
-    rows_small = mod_part.shape[0]
     scratch |= {
         "own": pltpu.VMEM((UNITS, SHARE, LANES), BF16),
         "own_sem": pltpu.SemaphoreType.DMA((UNITS,)),
         "gather": Gather.semaphores(gather_stages(ENTER)),
-        "small": [pltpu.SemaphoreType.DMA((16,))] * 2,
-        "from_core": pltpu.VMEM((rows_small, LANES), F32),
-        "from_y": pltpu.VMEM((rows_small, LANES), F32),
-        "mod_sum": pltpu.VMEM((rows_small, LANES), F32),
-        "mods": pltpu.VMEM((4, 2, rows_small, LANES), F32),
+        "small": [pltpu.SemaphoreType.DMA((18,))] * 2,
+        "mod_part": pltpu.VMEM((MOD_ROWS, LANES), F32),
+        "mod_parts": pltpu.VMEM((2, 2, MOD_ROWS, LANES), F32),
+        "mods": pltpu.VMEM((4, 2, MOD_ROWS, LANES), F32),
+        "rows": pltpu.VMEM((24, TILE), F32),
+        "spread": pltpu.VMEM((2 * SPREAD, LANES), F32),
+        "table_own": pltpu.VMEM((2, SPREAD, LANES), BF16),
     }
     return call(enter_kernel, "enter", inputs, outputs, scratch, collective=0)
+
+
+def deliver_kernel(refs):
+    names = [name for name in vars(refs) if name.startswith("from_")]
+    loads, stores = [], []
+    for index, name in enumerate(names):
+        plain = name[len("from_") :]
+        held = getattr(refs, "held_" + plain)
+        loads.append(pltpu.make_async_copy(getattr(refs, name), held, refs.sems.at[0, index]))
+        stores.append(pltpu.make_async_copy(held, getattr(refs, plain), refs.sems.at[1, index]))
+        loads[-1].start()
+    for load, store in zip(loads, stores, strict=True):
+        load.wait()
+        store.start()
+    for store in stores:
+        store.wait()
+
+
+def deliver(**arrays):
+    inputs = {"from_" + name: (array, anywhere()) for name, array in arrays.items()}
+    outputs = {name: (shape(array.dtype, *array.shape), anywhere()) for name, array in arrays.items()}
+    scratch = {"held_" + name: pltpu.VMEM(array.shape, array.dtype) for name, array in arrays.items()}
+    scratch["sems"] = pltpu.SemaphoreType.DMA((2, len(arrays)))
+    return call(deliver_kernel, "deliver", inputs, outputs, scratch)
 
 
 def attend(special, packed, table, live_frames, held):
@@ -1235,7 +1454,7 @@
         aliases,
         collective,
         grid=(H // 2,),
-        limit=32,
+        limit=60,
     )
     if not special:
         out.held = held
@@ -1275,15 +1494,20 @@
     aliases, collective = (), None
     if special:
         outputs["held_out"] = (shape(BF16, UNITS, *SPLIT), anywhere())
-        outputs["total"] = (shape(F32, len(EARLY), SHARE, LANES), vmem())
+        outputs["side"] = (shape(BF16, *Reduce.side_shape(len(EARLY))), vmem())
         scratch["gather"] = Gather.semaphores(gather_stages(MIDDLE.values()))
-        scratch["reduce"] = Reduce.scratch(EARLY)
+        outputs["total"] = (shape(F32, len(DONE), SHARE, LANES), vmem())
+        scratch["core"] = pltpu.VMEM(Reduce.core_shape(len(EARLY)), BF16)
+        scratch["corner"] = pltpu.VMEM(Reduce.corner_shape(len(DONE)), BF16)
+        scratch["distant"] = pltpu.VMEM(Reduce.distant_shape(len(DONE)), BF16)
+        scratch["aside"] = pltpu.VMEM(Reduce.aside_shape(1), BF16)
+        scratch["reduce"] = Reduce.scratch(EARLY_POINTS)
         aliases, collective = (("held", "held_out"),), 2
     return call(middle_kernel, "middle", inputs, outputs, scratch, aliases, collective, limit=60)
 
 
 def back(
-    special, live_frames, tokens, mod, start, probs, mid, held, ada, member
+    special, live_frames, tokens, mod, start, probs, mid, held, ada, member, condition
 ):
     window_count = probs.shape[0]
     rows = window_count * WIN
@@ -1346,28 +1570,45 @@
     inputs |= {
         "late_sums": (mid.sums, whole(mid.sums)),
         "ada": (ada, whole(ada)),
+        "condition": (condition, whole(condition)),
         "member": (member, whole(member)),
+        "side_in": (mid.side, whole(mid.side)),
+        "done": (mid.total, whole(mid.total)),
         "part": (mid.part, anywhere()),
     }
     outputs |= {
-        "total": result(len(LATE), SHARE, LANES),
-        "clip_total": result(MOD_ROWS, LANES),
-        "table_total": result(2 * SPREAD, LANES),
-        "cond_total": result(2, 2, 8, SHARE),
+        "grad_qkv": result(SHARE, 3 * LANES),
+        "grad_out": result(SHARE, LANES),
+        "grad_up": result(SHARE, 4 * LANES),
+        "grad_down": result(4 * SHARE, LANES),
+        "grad_ada": result(SHARE, 6 * LANES),
+        "grad_bias": result(6, LANES),
+        "grad_condition": result(*condition.shape),
+        "table_total": result(2, REL),
     }
+    count, late = len(EARLY + LATE), len(LATE)
     scratch |= {
-        "spread": pltpu.VMEM((2, SPREAD, LANES), F32),
+        "spread": pltpu.VMEM((2, WIDE, LANES), F32),
+        "spreads": pltpu.VMEM((H * WIDE, LANES), F32),
         "made": pltpu.VMEM((3, *SPLIT), BF16),
         "sums": pltpu.VMEM((window_count, 8, D), F32),
-        "reduce": Reduce.scratch(LATE),
-        "table": pltpu.VMEM((4, 2, 2 * SPREAD, LANES), F32),
-        "table_small": Small.scratch(2 * SPREAD),
+        "core": pltpu.VMEM(Reduce.core_shape(late), BF16),
+        "side": pltpu.VMEM(Reduce.side_shape(late), BF16),
+        "corner": pltpu.VMEM(Reduce.corner_shape(count), BF16),
+        "distant": pltpu.VMEM(Reduce.distant_shape(count), BF16),
+        "aside": pltpu.VMEM(Reduce.aside_shape(1), BF16),
+        "reduce": Reduce.scratch(LATE_POINTS),
+        "table": pltpu.VMEM((4, 2, 2 * WIDE // WSIDE, TILE), F32),
+        "table_zx": pltpu.VMEM((4, 2, 2 * WIDE // WSIDE, TILE), F32),
+        "table_own": pltpu.VMEM((2 * WIDE // WSIDE, TILE), F32),
+        "table_yc": pltpu.VMEM((2, 2, 2 * WIDE // WSIDE, TILE), F32),
         "clip": pltpu.VMEM((4, 2, MOD_ROWS, LANES), F32),
-        "clip_small": Small.scratch(MOD_ROWS),
-        "cond": pltpu.VMEM((2, 2, 8, SHARE), F32),
-        "cond_x": pltpu.VMEM((2, 2, 8, SHARE), F32),
-        "cond_z": pltpu.VMEM((4, 2, 2, 8, SHARE), F32),
-        "cond_small": [pltpu.SemaphoreType.DMA((8,))] * 2,
+        "clip_zx": pltpu.VMEM((4, 2, MOD_ROWS, LANES), F32),
+        "clip_own": pltpu.VMEM((MOD_ROWS, LANES), F32),
+        "clip_yc": pltpu.VMEM((2, 2, MOD_ROWS, LANES), F32),
+        "cond_own": pltpu.VMEM((8, LANES), F32),
+        "cond_all": pltpu.VMEM((4, 2, 2, 2, 8, LANES), F32),
+        "small": [pltpu.SemaphoreType.DMA((51,))] * 2,
     }
     return call(
         back_kernel,
@@ -1398,31 +1639,27 @@
     window_count = tokens.shape[0]
     clip_count = condition.shape[0]
     rows_ada, cols_ada = ada_weight.shape
-    row_block = lax.axis_index("fsdp")
-    col_block = lax.axis_index("dp")
-    first_window = lax.axis_index(("dp", "fsdp")) * window_count
-    live_frames, member_int = window_layout(clip_frames, first_window, window_count)
-    member = member_int.astype(F32)
-    activity_low = jax.nn.silu(condition).astype(BF16)
-    act_rows = lax.dynamic_slice_in_dim(activity_low, row_block * rows_ada, rows_ada, 1)
-
-    mod_part = jnp.dot(act_rows, ada_weight, preferred_element_type=F32)
-    mod_part = mod_part + jnp.where(row_block == 0, ada_bias.astype(F32), 0.0)[None, :]
     token_rows = tokens.reshape(window_count * WIN, D)
     cotangent_rows = cotangent.reshape(window_count * WIN, D)
     own = (qkv_weight, out_weight, up_weight, down_weight)
     if special:
-        clips = jnp.pad(mod_part, ((0, 8 - clip_count), (0, 0)))
-        clips = clips.reshape(8, 6, LANES).transpose(1, 0, 2).reshape(MOD_ROWS, LANES)
-        member_wide = jnp.pad(member, ((0, 0), (0, 8 - clip_count)))[:, :, None]
-        member_wide = jnp.broadcast_to(member_wide, (window_count, 8, LANES))
-        start = enter(
-            True, token_rows, None, None, own, clips, member_wide, spread_table(rel_table)
-        )
+        smalls = (clip_frames, condition, ada_weight, ada_bias.reshape(1, cols_ada), rel_table)
+        start = enter(True, token_rows, None, None, own, smalls)
         table = start.table.reshape(H, SPREAD, LANES)
+        live_frames, member_wide = start.live, start.member
     else:
+        row_block = lax.axis_index("fsdp")
+        col_block = lax.axis_index("dp")
+        first_window = lax.axis_index(("dp", "fsdp")) * window_count
+        live_frames, member_int = window_layout(clip_frames, first_window, window_count)
+        member = member_int.astype(F32)
+        activity_low = jax.nn.silu(condition).astype(BF16)
+        rows_own = lax.dynamic_slice_in_dim(activity_low, row_block * rows_ada, rows_ada, 1)
+        mod_part = jnp.dot(rows_own, ada_weight, preferred_element_type=F32)
+        clip_mod = lax.all_gather(lax.psum(mod_part, "fsdp"), "dp", axis=1, tiled=True)
+        bias = lax.all_gather(ada_bias, "dp", axis=0, tiled=True)
+        clip_mod = clip_mod + bias.astype(F32)[None, :]
         member_wide = None
-        clip_mod = lax.all_gather(lax.psum(mod_part, "fsdp"), "dp", axis=1, tiled=True)
         window_mod = jnp.sum(member[:, :, None] * clip_mod[None], axis=1)
         window_mod = jnp.pad(window_mod.reshape(window_count, 6, D), ((0, 0), (0, 2), (0, 0)))
         whole = [
@@ -1432,7 +1669,7 @@
             for weight in own
         ]
         held = units_of(*whole).reshape(UNITS, *SPLIT)
-        start = enter(False, token_rows, held, window_mod, None, None, None, None)
+        start = enter(False, token_rows, held, window_mod, None, None)
         table = spread_table(lax.all_gather(rel_table, "dp", axis=0, tiled=True))
     mod = start.mod
     across = attend(special, start.packed, table, live_frames, start.held)
@@ -1451,48 +1688,63 @@
         held,
         ada_weight,
         member_wide,
+        condition,
     )
     if special:
-        shares = [None] * UNITS
-        for units, totals in ((EARLY, mid.total), (LATE, end.total)):
-            for index, unit in enumerate(units):
-                shares[unit] = totals[index]
-        grads = own_blocks(jnp.stack(shares))
-        clip_cols = end.clip_total.reshape(6, 8, LANES).transpose(1, 0, 2).reshape(8, cols_ada)
-        clip_cols = clip_cols[:clip_count].astype(BF16)
-        cond_total = end.cond_total.transpose(2, 0, 1, 3).reshape(8, D)[:clip_count]
-        table_grad = gather_table(end.table_total.reshape(2, SPREAD, LANES))
-    else:
-        part = jnp.concatenate([end.part, mid.part[OUT:]])
-        grads = [
-            lax.psum_scatter(
-                lax.psum_scatter(grad, "fsdp", scatter_dimension=0, tiled=True),
-                "dp",
-                scatter_dimension=1,
-                tiled=True,
-            ).astype(F32)
-            for grad in weights_of(part.reshape(UNITS, 8, D, LANES))
-        ]
-        grad_mod = (mid.sums + end.sums)[:, :6].reshape(window_count, 6 * D)
-        clip_part = lax.dot_general(
-            member,
-            grad_mod,
-            (((0,), (0,)), ((), ())),
-            precision=HIGHEST,
-            preferred_element_type=F32,
+        end = deliver(
+            output=mid.output,
+            grad_tokens=end.grad_tokens,
+            grad_condition=end.grad_condition,
+            grad_ada=end.grad_ada,
+            grad_bias=end.grad_bias,
+            grad_qkv=end.grad_qkv,
+            grad_out=end.grad_out,
+            grad_up=end.grad_up,
+            grad_down=end.grad_down,
+            table=end.table_total,
         )
-        clip_sum, table_sum = lax.psum((clip_part, gather_table(end.spread)), ("dp", "fsdp"))
-        clip_cols = lax.dynamic_slice_in_dim(
-            clip_sum.astype(BF16), col_block * cols_ada, cols_ada, 1
+        return (
+            end.output.reshape(tokens.shape),
+            end.grad_tokens.reshape(tokens.shape),
+            end.grad_condition,
+            end.grad_ada,
+            end.grad_bias.reshape(cols_ada),
+            end.grad_qkv,
+            end.grad_out,
+            end.grad_up,
+            end.grad_down,
+            end.table,
         )
-        heads_own = rel_table.shape[0]
-        table_grad = lax.dynamic_slice_in_dim(table_sum, col_block * heads_own, heads_own, 0)
-        cond_part = lax.dot_general(
-            clip_cols, ada_weight, (((1,), (1,)), ((), ())), preferred_element_type=F32
-        )
-        cond_total = lax.all_gather(lax.psum(cond_part, "dp"), "fsdp", axis=1, tiled=True)
+    part = jnp.concatenate([end.part, mid.part[OUT:]])
+    grads = [
+        lax.psum_scatter(
+            lax.psum_scatter(grad, "fsdp", scatter_dimension=0, tiled=True),
+            "dp",
+            scatter_dimension=1,
+            tiled=True,
+        ).astype(F32)
+        for grad in weights_of(part.reshape(UNITS, 8, D, LANES))
+    ]
+    grad_mod = (mid.sums + end.sums)[:, :6].reshape(window_count, 6 * D)
+    clip_part = lax.dot_general(
+        member,
+        grad_mod,
+        (((0,), (0,)), ((), ())),
+        precision=HIGHEST,
+        preferred_element_type=F32,
+    )
+    clip_sum, table_sum = lax.psum((clip_part, gather_table(end.spread)), ("dp", "fsdp"))
+    clip_cols = lax.dynamic_slice_in_dim(
+        clip_sum.astype(BF16), col_block * cols_ada, cols_ada, 1
+    )
+    heads_own = rel_table.shape[0]
+    table_grad = lax.dynamic_slice_in_dim(table_sum, col_block * heads_own, heads_own, 0)
+    cond_part = lax.dot_general(
+        clip_cols, ada_weight, (((1,), (1,)), ((), ())), preferred_element_type=F32
+    )
+    cond_total = lax.all_gather(lax.psum(cond_part, "dp"), "fsdp", axis=1, tiled=True)
     grad_ada_weight = lax.dot_general(
-        act_rows, clip_cols, (((0,), (0,)), ((), ())), preferred_element_type=F32
+        rows_own, clip_cols, (((0,), (0,)), ((), ())), preferred_element_type=F32
     )
     grad_ada_bias = jnp.sum(clip_cols.astype(F32), axis=0)
     _, silu_back = jax.vjp(jax.nn.silu, condition)

time: 353 us -> 304 us (0.86); the launches traced: 348 us -> 303 us
  local copies, waits for them, and re-layouts: 21.2 us -> 1.26 us
  Pallas kernels: 316 us -> 301 us
  other arithmetic: 7.04 us -> 0 us
    pallas_call x4 -> x5, Pallas kernels: 316 us -> 301 us  [call(): pl.pallas_call(body, in_specs=[spec for _, spec in inputs.values()], out_...]
    unnamed x26 -> x0, local copies, waits for them, and re-layouts: 12.8 us -> none
where the time goes in v4:
time: 304 us; the launch traced here: 303 us
  Pallas kernels  301 us (99%)
    pallas_call x5, Pallas kernels, call(): pl.pallas_call(body, in_specs=[spec for _, spec in inputs.values()], out_...  301 us

profile of v4, /device:TPU:0, one launch (start us, length us, event | category | flops | bytes accessed | tf_op | source)
XLA Modules:
  0.0 303.3 jit_solution(1900819812286755877)
XLA Ops:
  0.6 1.3 reshape.42.refs_7_
  1.9 69.4 %enter.1 = (bf16[640,1024]{1,0:T(8,128)(2,1)}, bf16[3,640,1024]{2,1,0:T(8,128)(2,1)}, bf16[12,4,2,2,2,256,128]{6,5,4,3,2,1,0:T(8,128)(2,1)}, f32[2,8,1024]{2,1,0...) custom-call(bf16[640,1024]{1,0:T(8,128)(2,1)} %bitcast.6, ...), custom_call_target="tpu_custom_call" | custom-call | tf_op jit(solution)/shard_map/enter/pallas_call | solution.py:611
  71.3 40.2 %attend.1 = (bf16[640,1024]{1,0:T(8,128)(2,1)}, bf16[2,16,320,320]{3,2,1,0:T(8,128)(2,1)}, bf16[12,4,2,2,2,256,128]{6,5,4,3,2,1,0:T(8,128)(2,1)}) custom-call(s32[2]{0:T(128)} %get-tuple-element.47.refs_0_, bf16[3,640,1024]{2,1,0:T(8,128)(2,1)} %get-tuple-element.48.refs_1_.refs_2_.refs_3_, ...), custom_call_target="tpu_custom_call", output_to_operand_aliasing={{2}: (5, {})} | custom-call | tf_op jit(solution)/shard_map/attend/pallas_call | solution.py:611
  111.5 88.3 %middle.1 = (bf16[640,1024]{1,0:T(8,128)(2,1)}, f32[640,1024]{1,0:T(8,128)}, bf16[640,1024]{1,0:T(8,128)(2,1)}, f32[2,8,1024]{2,1,0:T(8,128)}, bf16[12,4,2,2,2,2...) custom-call(s32[2]{0:T(128)} %get-tuple-element.47.refs_0_, ...), custom_call_target="tpu_custom_call", output_to_operand_aliasing={{5}: (5, {})} | custom-call | tf_op jit(solution)/shard_map/middle/pallas_call | solution.py:611
  199.8 98.6 %back.1 = (f32[640,1024]{1,0:T(8,128)}, f32[256,384]{1,0:T(8,128)}, f32[256,128]{1,0:T(8,128)}, f32[256,512]{1,0:T(8,128)}, f32[1024,128]{1,0:T(8,128)}, /*index...) custom-call(s32[2]{0:T(128)} %get-tuple-element.47.refs_0_, ...), custom_call_target="tpu_custom_call" | custom-call | tf_op jit(solution)/shard_map/back/pallas_call | solution.py:611
  298.4 4.8 %deliver.1 = (bf16[640,1024]{1,0:T(8,128)(2,1)}, f32[640,1024]{1,0:T(8,128)}, f32[3,1024]{1,0:T(4,128)}, f32[256,768]{1,0:T(8,128)}, f32[6,128]{1,0:T(8,128)}, /...) custom-call(bf16[640,1024]{1,0:T(8,128)(2,1)} %get-tuple-element.54., ...), custom_call_target="tpu_custom_call" | custom-call | tf_op jit(solution)/shard_map/deliver/pallas_call | solution.py:611
